TPU v7x, 256 devices: a whole 4x4x8 slice. The times are simulated.
256 devices in a mesh: row: 32 (over x, z), col: 8 (over y, core).
Axes of the slice: x: 4, y: 4, z: 8, core: 2. Of those that a mesh axis runs over, the one named last changes fastest.
Arguments:
- tile_vals: bfloat16 [32, 8, 256, 128, 128], P('row', 'col'), may hold values from -0.25 to 0.25
- tile_row: int32 [32, 8, 256], P('row', 'col'), may hold values from 0 to 31
- tile_col: int32 [32, 8, 256], P('row', 'col'), may hold values from 0 to 127
- tile_count: int32 [32, 8], P('row', 'col'), may hold values from 64 to 256
- out_grad: bfloat16 [131072, 128], P('row', 'col'), may hold values from -6 to 6
- relu_mask: int32 [131072, 128], P('row', 'col'), may hold values 0 or 1
- features: bfloat16 [131072, 128], P(('row', 'col')), may hold values from -6 to 6
- weight: bfloat16 [128, 128], replicated, may hold values from -0.5 to 0.5
- importance: float32 [128, 128], replicated, may hold values from 0 to 1
- weight_delta: float32 [128, 128], replicated, may hold values from -0.016572814 to 0.016572814
Outputs:
- input_grad: bfloat16 [131072, 128], P(('row', 'col'))
- importance_out: float32 [128, 128], replicated
All inputs are finite; a program needn't handle non-finite values. No bound on the sum of `relu_mask` on one device may be relied on, other than what follows from the above.
Results may differ from a plain program's by a relative error of at most 0.022.
Values may be sent and summed in bfloat16 or wider, within the bound.
No kernel may reach another device: no remote copies, remote signals or barrier semaphores. Data moves between devices by JAX's collectives and lax.ppermute only.
A program may use at most 128 MiB of HBM per device.

v0:
```python
import jax
import jax.numpy as jnp
from jax import lax
from jax.sharding import PartitionSpec as P


def local(
    tile_vals,
    tile_row,
    tile_col,
    tile_count,
    out_grad,
    relu_mask,
    features,
    weight,
    importance,
    weight_delta,
):
    tile_side = tile_vals.shape[-1]
    slots = tile_vals.shape[2]
    node_rows = features.shape[0]
    row_devices = lax.axis_size("row")
    masked = (out_grad.astype(jnp.float32) * relu_mask.astype(jnp.float32)).astype(jnp.bfloat16)
    gathered = lax.all_gather(masked, "col", axis=1, tiled=True)
    width = gathered.shape[1]
    row_tiles = gathered.reshape(-1, tile_side, width)
    picked = jnp.take(row_tiles, tile_row.reshape(slots), axis=0)
    product = jnp.einsum(
        "tij,tif->tjf",
        tile_vals.reshape(slots, tile_side, tile_side),
        picked,
        preferred_element_type=jnp.float32,
    )
    flat_product = product.reshape(slots, tile_side * width)
    usable = lax.iota(jnp.int32, slots) < tile_count.reshape(())
    column_ids = tile_col.reshape(slots)
    row_count = node_rows * row_devices
    tile_ids = lax.iota(jnp.int32, row_count // tile_side)
    selector = ((column_ids[None, :] == tile_ids[:, None]) & usable[None, :]).astype(jnp.float32)
    summed = jnp.dot(
        selector, flat_product, precision=lax.Precision.HIGHEST, preferred_element_type=jnp.float32
    )
    partial_value = summed.reshape(row_count, width)
    aggregate = lax.psum_scatter(
        partial_value.astype(jnp.bfloat16), "row", scatter_dimension=0, tiled=True
    )
    input_grad = lax.dot_general(
        aggregate, weight, (((1,), (1,)), ((), ())), preferred_element_type=jnp.float32
    ).astype(jnp.bfloat16)
    local_grad = lax.dot_general(
        features, aggregate, (((0,), (0,)), ((), ())), preferred_element_type=jnp.float32
    )
    weight_grad = lax.psum(local_grad, ("row", "col"))
    importance_out = importance - weight_grad * weight_delta
    return (input_grad, importance_out)


def solution(mesh):
    return jax.shard_map(
        local,
        mesh=mesh,
        in_specs=(
            P("row", "col", None, None, None),
            P("row", "col", None),
            P("row", "col", None),
            P("row", "col"),
            P("row", "col"),
            P("row", "col"),
            P(("row", "col"), None),
            P(),
            P(),
            P(),
        ),
        out_specs=(P(("row", "col"), None), P()),
        check_vma=False,
    )
```

profile of v0, /device:TPU:32, one launch (start us, length us, event | category | flops | bytes accessed | tf_op | source)
XLA Modules:
  0.0 575.0 jit_solution(161593572458637343)
XLA Ops:
  7.2 0.0 copy-start
  7.2 0.0 all-gather.2.cloned.1.call-start
  7.2 1.7 multiply_convert_fusion
  8.9 0.0 all-gather.2.cloned.1.call-update
  9.0 0.0 reduce-scatter.2.cloned.1.call-start
  9.7 0.7 compare_select_fusion
  10.4 0.7 compare_and_fusion
  11.0 28.0 %all-gather.2.cloned.1.call-done = bf16[4096,128]{0,1:T(8,128)(2,1)} async-done(((bf16[4096,16]{0,1:T(8,128)(2,1)}), bf16[4096,128]{0,1:T(8,128)(2,1)}) %all-gather.2.cloned.1.call-update) | async-done | bytes 1048592 | tf_op jit(solution)/shard_map/all_gather | solution.py:24
  39.0 1.6 copy.15
  40.6 8.6 %gather_fusion = bf16[256,128,128]{2,1,0:T(8,128)(2,1)} fusion(bf16[32,128,128]{2,1,0:T(8,128)(2,1)S(1)} %bitcast.21, s32[1024]{0:T(1024)S(1)} %pad_clamp_fusion), kind=kCustom, calls=%fused_computation | custom fusion | bytes 16778240 | tf_op jit(solution)/shard_map/jit(_take)/gather | solution.py:27
  49.3 14.7 %convolution_bitcast_fusion = f32[256,128,128]{1,2,0:T(8,128)} fusion(bf16[1,1,256,128,128]{4,3,2,1,0:T(8,128)(2,1)} %param.10, bf16[256,128,128]{2,1,0:T(8,128)(2,1)} %gather_fusion, pred[256]{0:T(512)(128)(4,1)S(1)} %compare_and_fusion), kind=kOutput, calls=%fused_computation.2 | convolution fusion | flops 1077936128 | bytes 33554688 | tf_op jit(solution)/shard_map/tij,tif->tjf/dot_general | solution.py:28
  63.9 0.0 copy-start.4
  63.9 17.8 %copy.17 = f32[256,128,128]{0,2,1:T(8,128)} copy(f32[256,128,128]{1,2,0:T(8,128)} %convolution_bitcast_fusion) | data formatting | bytes 33554432 | tf_op jit(solution)/shard_map/tij,tif->tjf/dot_general | solution.py:28
  81.7 0.0 copy-done.4
  81.7 14.6 %convolution_convert_fusion = bf16[128,16384]{1,0:T(8,128)(2,1)} fusion(f32[256,16384]{0,1:T(8,128)} %bitcast.22, s32[256]{0:T(256)S(1)} %bitcast.24, pred[256]{0:T(512)(128)(4,1)S(1)} %iota_compare_fusion.1), kind=kOutput, calls=%fused_computation.1 | convolution fusion | flops 6444613632 | bytes 20972800 | tf_op jit(solution)/shard_map/dot_general | solution.py:40
  96.3 0.0 copy-start.1
  96.3 0.0 copy-start.2
  96.3 0.0 copy-start.3
  96.3 7.5 %convert_element_type.23 = bf16[16384,128]{1,0:T(8,128)(2,1)} reshape(bf16[128,16384]{1,0:T(8,128)(2,1)} %convolution_convert_fusion) | data formatting | bytes 8388608 | tf_op jit(solution)/shard_map/convert_element_type | solution.py:45
  103.8 0.0 reduce-scatter.2.cloned.1.call-update
  103.8 0.0 all-reduce.2.cloned.1.call-start
  103.9 0.0 copy-done.1
  103.9 0.1 copy.18
  104.0 0.0 copy-done.2
  104.0 0.1 copy.19
  104.1 220.0 %reduce-scatter.2.cloned.1.call-done = bf16[512,128]{1,0:T(8,128)(2,1)} async-done(((bf16[16384,128]{1,0:T(8,128)(2,1)}), bf16[512,128]{1,0:T(8,128)(2,1)}) %reduce-scatter.2.cloned.1.call-update) | async-done | bytes 131088 | tf_op jit(solution)/shard_map/reduce_scatter | solution.py:44
  324.1 0.0 copy-done
  324.1 1.8 convolution_bitcast_fusion.1
  325.9 0.0 all-reduce.2.cloned.1.call-update
  325.9 0.0 copy-done.3
  325.9 1.7 convolution_convert_fusion.1
  327.7 239.2 %all-reduce.2.cloned.1.call-done = f32[128,128]{0,1:T(8,128)} async-done(((f32[128,128]{0,1:T(8,128)}), f32[128,128]{0,1:T(8,128)}) %all-reduce.2.cloned.1.call-update) | async-done | bytes 65552 | tf_op jit(solution)/shard_map/psum | solution.py:53
  566.9 0.9 multiply_subtract_fusion
  567.8 0.7 copy.20
  (2 shorter events, 0.0 us)
Async XLA Ops:
  7.2 317.0 %copy-start = (bf16[512,128]{1,0:T(8,128)(2,1)S(1)}, bf16[512,128]{1,0:T(8,128)(2,1)}, u32[]{:S(2)}) copy-start(bf16[512,128]{1,0:T(8,128)(2,1)} %param.16) | copy-start | bytes 393220
  7.2 31.8 %all-gather.2.cloned.1.call-start = ((), (), s32[]{:S(2)}) async-start(), calls=%async_computation.1 | async-start | bytes 1179648 | tf_op jit(solution)/shard_map/all_gather | solution.py:24
  9.0 315.2 %reduce-scatter.2.cloned.1.call-start = ((), (), s32[]{:S(2)}) async-start(), calls=%async_computation.2 | async-start | bytes 4325376 | tf_op jit(solution)/shard_map/reduce_scatter | solution.py:44
  63.9 17.8 %copy-start.4 = (s32[1,1,256]{2,1,0:T(1,128)S(1)}, s32[1,1,256]{2,1,0:T(1,128)}, u32[]{:S(2)}) copy-start(s32[1,1,256]{2,1,0:T(1,128)} %param.12) | copy-start | bytes 3076
  96.3 7.6 %copy-start.1 = (f32[128,128]{1,0:T(8,128)S(1)}, f32[128,128]{1,0:T(8,128)}, u32[]{:S(2)}) copy-start(f32[128,128]{1,0:T(8,128)} %param.19) | copy-start | bytes 196612
  96.3 7.7 %copy-start.2 = (f32[128,128]{1,0:T(8,128)S(1)}, f32[128,128]{1,0:T(8,128)}, u32[]{:S(2)}) copy-start(f32[128,128]{1,0:T(8,128)} %param.18) | copy-start | bytes 196612
  96.3 229.6 %copy-start.3 = (bf16[128,128]{1,0:T(8,128)(2,1)S(1)}, bf16[128,128]{1,0:T(8,128)(2,1)}, u32[]{:S(2)}) copy-start(bf16[128,128]{1,0:T(8,128)(2,1)} %param.17) | copy-start | bytes 98308
  103.8 463.1 %all-reduce.2.cloned.1.call-start = ((), (), s32[]{:S(2)}) async-start(), calls=%async_computation.3 | async-start | bytes 131072 | tf_op jit(solution)/shard_map/psum | solution.py:53
Sparse Core Ops, SparseCore 0:
  10.4 28.5 all-gather.1
  104.0 220.1 reduce-scatter.1
  331.1 235.7 all-reduce.1
where the time goes:
time: 578 us; the launch traced here: 575 us
  waiting for transfers between devices  487 us (84%)
  local copies, waits for them, and re-layouts  36.5 us (6%)
  matrix products  32.7 us (6%)
  between operations  14.5 us (3%)
    psum x1, waiting for transfers between devices, local(): weight_grad = lax.psum(local_grad, ('row', 'col'))  239 us
    reduce_scatter x1, waiting for transfers between devices, local(): lax.psum_scatter(partial_value.astype(jnp.bfloat16), 'row', scatter_dimen...  220 us
    all_gather x1, waiting for transfers between devices, local(): gathered = lax.all_gather(masked, 'col', axis=1, tiled=True)  28 us
    dot_general x1, local copies, waits for them, and re-layouts, local(): jnp.einsum('tij,tif->tjf', tile_vals.reshape(slots, tile_side, tile_side)...  17.8 us
    dot_general x1, matrix products, local(): jnp.einsum('tij,tif->tjf', tile_vals.reshape(slots, tile_side, tile_side)...  14.7 us
    dot_general x1, matrix products, local(): jnp.dot(selector, flat_product, precision=lax.Precision.HIGHEST, preferre...  14.6 us
  transfers between devices with their start and end apart: 3, of which 3 were waited for; matrix products, arithmetic and copies ran while one was open for 1% of the time, Pallas kernels for 0%

commit v1 on v0

v1 whole, which is shorter than its diff:
```python
import functools

import jax
import jax.numpy as jnp
from jax import lax
from jax.experimental import pallas as pl
from jax.experimental.pallas import tpu as pltpu
from jax.sharding import Mesh, PartitionSpec as P

XS, ZS, YS, CS = 4, 8, 4, 2
T = 128
GROUP = 32
UNROLL = 8
F32, BF16 = jnp.float32, jnp.bfloat16


def shift(value, axis, size, by):
    return lax.ppermute(value, axis, [(i, (i + by) % size) for i in range(size)])


def tile_kernel(rows, places, meta, tiles, mine, other, c0, c1, c2a, c2b, c3, wide, acc):
    step = pl.program_id(0)

    @pl.when(step == 0)
    def _():
        for part, dist in enumerate((0, 1, 3, 2)):
            y_of = (meta[1] - dist) & (YS - 1)
            for ref, core in ((mine, meta[2]), (other, 1 - meta[2])):
                at = pl.multiple_of((y_of * CS + core) * 16, 16)
                wide[pl.ds(at, 16), :] = ref[part * 16 : part * 16 + 16, :]

        def clear(i, _):
            acc[pl.ds(i * 4, 4)] = jnp.zeros((4, T, T), F32)
            return 0

        lax.fori_loop(0, 32, clear, 0)

    def several(g, _):
        base = step * GROUP + g * UNROLL
        products = []
        for u in range(UNROLL):
            at = pl.multiple_of(rows[base + u] * T, T)
            products.append(
                jnp.dot(wide[:, pl.ds(at, T)], tiles[g * UNROLL + u], preferred_element_type=F32)
            )
        for u in range(UNROLL):
            place = places[base + u]
            acc[place] = acc[place] + products[u]
        return 0

    used = jnp.clip(meta[0] - step * GROUP, 0, GROUP)
    lax.fori_loop(0, (used + UNROLL - 1) >> 3, several, 0)

    @pl.when(step == pl.num_programs(0) - 1)
    def _():
        for out, first, size in ((c2a, 64, 16), (c2b, 80, 16), (c1, 32, 32), (c3, 96, 32), (c0, 0, 32)):

            def put(i, _):
                out[pl.ds(i * 4, 4)] = acc[pl.ds(first + i * 4, 4)].astype(BF16)
                return 0

            lax.fori_loop(0, size // 4, put, 0)


def tile_products(rows, places, meta, tiles, mine, other):
    steps = tiles.shape[0] // GROUP
    sizes = (32, 32, 16, 16, 32)
    whole = lambda shape: pl.BlockSpec(shape, lambda i, *_: (0,) * len(shape))
    return pl.pallas_call(
        tile_kernel,
        grid_spec=pltpu.PrefetchScalarGridSpec(
            num_scalar_prefetch=3,
            grid=(steps,),
            in_specs=[
                pl.BlockSpec((GROUP, T, T), lambda i, *_: (i, 0, 0)),
                whole(mine.shape),
                whole(other.shape),
            ],
            out_specs=[whole((n, T, T)) for n in sizes],
            scratch_shapes=[pltpu.VMEM((T, mine.shape[1]), BF16), pltpu.VMEM((129, T, T), F32)],
        ),
        out_shape=[jax.ShapeDtypeStruct((n, T, T), BF16) for n in sizes],
        compiler_params=pltpu.CompilerParams(vmem_limit_bytes=40 * 2**20),
        cost_estimate=pl.CostEstimate(flops=2**30, bytes_accessed=13 * 2**20, transcendentals=0),
    )(rows, places, meta, tiles, mine, other)


def middle_kernel(meta, c0, up, down, feats, z4a, z4b, z3, z5, z2, z6, z1, z7, z0, grad):
    total = jnp.zeros((T, T), F32)
    outs = {0: z0, 1: z1, 2: z2, 3: z3, 5: z5, 6: z6, 7: z7}
    for dist in range(ZS):
        z_of = (meta[3] + dist) & (ZS - 1)
        for q in range(4):
            n = dist * 4 + q
            value = (c0[n].astype(F32) + up[n].astype(F32) + down[n].astype(F32)).astype(BF16)
            if dist == 4:
                (z4a if q < 2 else z4b)[q % 2] = value
            else:
                outs[dist][q] = value
            total += jnp.dot(value, feats[z_of * 4 + q], preferred_element_type=F32)
    grad[...] = total


def middle(meta, c0, up, down, feats):
    sizes = (2, 2, 4, 4, 4, 4, 4, 4, 4)
    spec = pl.BlockSpec(memory_space=pltpu.VMEM)
    return pl.pallas_call(
        middle_kernel,
        in_specs=[pl.BlockSpec(memory_space=pltpu.SMEM)] + [spec] * 4,
        out_specs=[spec] * 10,
        out_shape=[jax.ShapeDtypeStruct((n, T, T), BF16) for n in sizes]
        + [jax.ShapeDtypeStruct((T, T), F32)],
        compiler_params=pltpu.CompilerParams(vmem_limit_bytes=24 * 2**20),
        cost_estimate=pl.CostEstimate(flops=2**27, bytes_accessed=5 * 2**20, transcendentals=0),
    )(meta, c0, up, down, feats)


def add(*values):
    return sum(v.astype(F32) for v in values).astype(BF16)


def local(tile_vals, tile_row, tile_col, tile_count, out_grad, relu_mask, features, weight, importance, weight_delta):
    x, z, y, core = (lax.axis_index(a) for a in ("x", "z", "y", "core"))
    slots = tile_vals.shape[2]
    wide_feats = lax.all_gather(features, "z", axis=0, tiled=True).reshape(ZS * 4, T, T)

    masked = (out_grad.astype(F32) * relu_mask.astype(F32)).astype(BF16).T
    mine = jnp.concatenate([masked] + [shift(masked, "y", YS, d) for d in (1, 3, 2)], axis=0)
    other = lax.ppermute(mine, "core", [(0, 1), (1, 0)])

    count = tile_count.reshape(())
    cols = tile_col.reshape(slots)
    dest = cols >> 2
    dx = ((dest >> 3) - x) & (XS - 1)
    dz = ((dest & 7) - z) & (ZS - 1)
    places = jnp.where(lax.iota(jnp.int32, slots) < count, (dx * ZS + dz) * 4 + (cols & 3), 128)
    meta = jnp.stack([count, y, core, z]).astype(jnp.int32)
    c0, c1, c2a, c2b, c3 = tile_products(
        tile_row.reshape(slots), places, meta, tile_vals.reshape(slots, T, T), mine, other
    )

    up, down = shift(c2a, "x", XS, 1), shift(c2b, "x", XS, 3)
    s1 = jnp.concatenate([add(c1[:16], up), c1[16:]], axis=0)
    s3 = jnp.concatenate([c3[:16], add(c3[16:], down)], axis=0)
    z4a, z4b, z3, z5, z2, z6, z1, z7, z0, grad = middle(
        meta, c0, shift(s1, "x", XS, 1), shift(s3, "x", XS, 3), wide_feats
    )

    up, down = shift(z4a, "z", ZS, 1), shift(z4b, "z", ZS, 7)
    up = jnp.concatenate([add(z3[:2], up), z3[2:]], axis=0)
    down = jnp.concatenate([z5[:2], add(z5[2:], down)], axis=0)
    for u, d in ((z2, z6), (z1, z7)):
        up, down = add(u, shift(up, "z", ZS, 1)), add(d, shift(down, "z", ZS, 7))
    aggregate = add(z0, shift(up, "z", ZS, 1), shift(down, "z", ZS, 7))
    input_grad = jnp.einsum("qfj,df->qjd", aggregate, weight, preferred_element_type=F32)
    input_grad = input_grad.astype(BF16).reshape(features.shape[0], weight.shape[0])

    grad = grad + lax.ppermute(grad, "core", [(0, 1), (1, 0)])
    grad = grad + shift(grad, "y", YS, 1) + shift(grad, "y", YS, 3) + shift(grad, "y", YS, 2)
    grad = grad + shift(grad, "x", XS, 1) + shift(grad, "x", XS, 3) + shift(grad, "x", XS, 2)
    grad = grad + shift(grad, "z", ZS, 1) + shift(grad, "z", ZS, 7) + shift(grad, "z", ZS, 2)
    grad = grad + shift(grad, "z", ZS, 4)
    return input_grad, importance - grad.T * weight_delta


def solution(mesh):
    mesh = Mesh(mesh.devices.reshape(XS, ZS, YS, CS), ("x", "z", "y", "core"))
    row, col = ("x", "z"), ("y", "core")
    return jax.shard_map(
        local,
        mesh=mesh,
        in_specs=(
            P(row, col, None, None, None),
            P(row, col, None),
            P(row, col, None),
            P(row, col),
            P(row, col),
            P(row, col),
            P(row + col, None),
            P(),
            P(),
            P(),
        ),
        out_specs=(P(row + col, None), P()),
        check_vma=False,
    )
```

time: 578 us -> 145 us (0.25)
  waiting for transfers between devices: 487 us -> 49.1 us
  starting transfers between devices: 0.12 us -> 48.5 us
  matrix products: 32.7 us -> 0.88 us
  local copies, waits for them, and re-layouts: 36.5 us -> 13.5 us
  Pallas kernels: 0 us -> 8.35 us
  other arithmetic: 3.93 us -> 11 us
    psum x1 -> x0, waiting for transfers between devices: 239 us -> none  [local(): weight_grad = lax.psum(local_grad, ('row', 'col'))]
    reduce_scatter x1 -> x0, waiting for transfers between devices: 220 us -> none  [local(): lax.psum_scatter(partial_value.astype(jnp.bfloat16), 'row', scatter_dimen...]
    ppermute x0 -> x27, starting transfers between devices: none -> 48.4 us  [the longest x25 48.3 us: shift(): lax.ppermute(value, axis, [(i, (i + by) % size) for i in range(size)])]
    dot_general x4 -> x1, matrix products: 32.7 us -> 0.88 us  [local(): jnp.einsum('qfj,df->qjd', aggregate, weight, preferred_element_type=F32)]
    ppermute x0 -> x27, waiting for transfers between devices: none -> 24.3 us  [the longest x25 23.1 us: shift(): lax.ppermute(value, axis, [(i, (i + by) % size) for i in range(size)])]
    dot_general x1 -> x0, local copies, waits for them, and re-layouts: 17.8 us -> none  [local(): jnp.einsum('tij,tif->tjf', tile_vals.reshape(slots, tile_side, tile_side)...]
    unnamed x13 -> x23, local copies, waits for them, and re-layouts: 0.93 us -> 11.7 us
    gather x1 -> x0, local copies, waits for them, and re-layouts: 8.62 us -> none  [local(): picked = jnp.take(row_tiles, tile_row.reshape(slots), axis=0)]
  transfers between devices with their start and end apart: 3 -> 28, of which waited for: 3 -> 14; matrix products, arithmetic and copies ran while one was open for 1% -> 10% of each run, Pallas kernels for 0% -> 0%
where the time goes in v1:
time: 145 us; the launch traced here: 146 us
  waiting for transfers between devices  49.1 us (34%)
  starting transfers between devices  48.5 us (33%)
  between operations  14.9 us (10%)
  local copies, waits for them, and re-layouts  13.5 us (9%)
  other arithmetic  11 us (8%)
  Pallas kernels  8.35 us (6%)
    ppermute x25, starting transfers between devices, shift(): lax.ppermute(value, axis, [(i, (i + by) % size) for i in range(size)])  48.3 us
    all_gather x1, waiting for transfers between devices, local(): lax.all_gather(features, 'z', axis=0, tiled=True).reshape(ZS * 4, T, T)  24.8 us
    ppermute x25, waiting for transfers between devices, shift(): lax.ppermute(value, axis, [(i, (i + by) % size) for i in range(size)])  23.1 us
    unnamed x23, local copies, waits for them, and re-layouts  11.7 us
    convert_element_type x8, other arithmetic, add(): return sum((v.astype(F32) for v in values)).astype(BF16)  6.95 us
    pallas_call x1, Pallas kernels, tile_products(): pl.pallas_call(tile_kernel, grid_spec=pltpu.PrefetchScalarGridSpec(num_sc...  6.72 us
  transfers between devices with their start and end apart: 28, of which 14 were waited for; matrix products, arithmetic and copies ran while one was open for 10% of the time, Pallas kernels for 0%

profile of v1, /device:TPU:32, one launch (start us, length us, event | category | flops | bytes accessed | tf_op | source)
XLA Modules:
  0.0 146.2 jit_solution(11574631869583722163)
XLA Ops:
  7.2 1.0 fusion
  8.2 1.7 %collective-permute-start = (bf16[16,4096]{1,0:T(8,128)(2,1)S(1)}, bf16[16,4096]{1,0:T(8,128)(2,1)S(1)}, u32[]{:S(2)}, u32[]{:S(2)}) collective-permute-start(bf16[16,4096]{1,0:T(8,128)(2,1)S(1)} %fusion), channel_id=1, source_target_pairs={{0,2},{2,4},{4,6},{6,0},{1,3},{3,5},{5,7},{7,1},{8,10},{10,12},{12... | collective-permute-start | bytes 393224 | tf_op jit(solution)/shard_map/ppermute | solution.py:18
  9.9 1.7 %collective-permute-start.1 = (bf16[16,4096]{1,0:T(8,128)(2,1)S(1)}, bf16[16,4096]{1,0:T(8,128)(2,1)S(1)}, u32[]{:S(2)}, u32[]{:S(2)}) collective-permute-start(bf16[16,4096]{1,0:T(8,128)(2,1)S(1)} %fusion), channel_id=1, source_target_pairs={{0,6},{2,0},{4,2},{6,4},{1,7},{3,1},{5,3},{7,5},{8,14},{10,8},{12,... | collective-permute-start | bytes 393224 | tf_op jit(solution)/shard_map/ppermute | solution.py:18
  11.6 2.0 %collective-permute-start.2 = (bf16[16,4096]{1,0:T(8,128)(2,1)S(1)}, bf16[16,4096]{1,0:T(8,128)(2,1)S(1)}, u32[]{:S(2)}, u32[]{:S(2)}) collective-permute-start(bf16[16,4096]{1,0:T(8,128)(2,1)S(1)} %fusion), channel_id=1, source_target_pairs={{0,4},{2,6},{4,0},{6,2},{1,5},{3,7},{5,1},{7,3},{8,12},{10,14},{12... | collective-permute-start | bytes 393224 | tf_op jit(solution)/shard_map/ppermute | solution.py:18
  14.2 0.6 collective-permute-done
  14.8 2.2 %collective-permute-done.1 = bf16[16,4096]{1,0:T(8,128)(2,1)S(1)} collective-permute-done((bf16[16,4096]{1,0:T(8,128)(2,1)S(1)}, bf16[16,4096]{1,0:T(8,128)(2,1)S(1)}, u32[]{:S(2)}, u32[]{:S(2)}) %collective-permute-start.1) | collective-permute-done | bytes 131104 | tf_op jit(solution)/shard_map/ppermute | solution.py:18
  17.0 1.8 %collective-permute-done.2 = bf16[16,4096]{1,0:T(8,128)(2,1)S(1)} collective-permute-done((bf16[16,4096]{1,0:T(8,128)(2,1)S(1)}, bf16[16,4096]{1,0:T(8,128)(2,1)S(1)}, u32[]{:S(2)}, u32[]{:S(2)}) %collective-permute-start.2) | collective-permute-done | bytes 131104 | tf_op jit(solution)/shard_map/ppermute | solution.py:18
  18.9 0.1 collective-permute-start.3
  19.0 0.1 pad_add_fusion.meta
  19.0 0.7 multiply_add_fusion
  19.7 1.1 collective-permute-done.3.other
  20.9 3.4 %copy-done.1 = bf16[1,1,256,128,128]{4,3,2,1,0:T(8,128)(2,1)S(1)} copy-done((bf16[1,1,256,128,128]{4,3,2,1,0:T(8,128)(2,1)S(1)}, bf16[1,1,256,128,128]{4,3,2,1,0:T(8,128)(2,1)}, u32[]{:S(2)}) %copy-start.1) | copy-done | bytes 8388632
  24.2 0.7 copy-done.8
  24.9 6.7 %shard_map.113 = (bf16[32,128,128]{2,1,0:T(8,128)(2,1)S(1)}, bf16[32,128,128]{2,1,0:T(8,128)(2,1)S(1)}, bf16[16,128,128]{2,1,0:T(8,128)(2,1)}, bf16[16,128,128]{2,1,0:T(8,128)(2,1)}, bf16[32,128,128]{2,1,0:T(8,128)(2,1)S(1)}) custom-call(s32[256]{0:T(256)S(1)} %bitcast.23, s32[256]{0:T(256)S(1)} %compare_select_fusion.places, s32[4]{0:T(128)S(1)} %pad_add_fusion.meta, ...), custom_call_target="tpu_custom_call" | custom-call | flops 1073741824 | bytes 13631488 | tf_op jit(solution)/shard_map/pallas_call | solution.py:69
  31.6 3.9 %collective-permute-start.6 = (bf16[16,128,128]{2,1,0:T(8,128)(2,1)}, bf16[16,128,128]{2,1,0:T(8,128)(2,1)}, u32[]{:S(2)}, u32[]{:S(2)}) collective-permute-start(bf16[16,128,128]{2,1,0:T(8,128)(2,1)} %get-tuple-element.21), channel_id=1, source_target_pairs={{0,192},{64,0},{128,64},{192,128},{1,193},{65,1},{129,65},{193,129... | collective-permute-start | bytes 1572872 | tf_op jit(solution)/shard_map/ppermute | solution.py:18
  35.7 9.3 %collective-permute-done.6 = bf16[16,128,128]{2,1,0:T(8,128)(2,1)} collective-permute-done((bf16[16,128,128]{2,1,0:T(8,128)(2,1)}, bf16[16,128,128]{2,1,0:T(8,128)(2,1)}, u32[]{:S(2)}, u32[]{:S(2)}) %collective-permute-start.6) | collective-permute-done | bytes 524320 | tf_op jit(solution)/shard_map/ppermute | solution.py:18
  45.0 1.2 add_convert_fusion
  46.1 1.1 pad_maximum_fusion.1
  47.2 3.5 %collective-permute-start.7 = (bf16[32,128,128]{2,1,0:T(8,128)(2,1)}, bf16[32,128,128]{2,1,0:T(8,128)(2,1)S(1)}, u32[]{:S(2)}, u32[]{:S(2)}) collective-permute-start(bf16[32,128,128]{2,1,0:T(8,128)(2,1)} %pad_maximum_fusion.1), channel_id=1, source_target_pairs={{0,192},{64,0},{128,64},{192,128},{1,193},{65,1},{129,65},{193,129... | collective-permute-start | bytes 3145736 | tf_op jit(solution)/shard_map/ppermute | solution.py:18
  50.7 1.2 add_convert_fusion.1
  51.9 1.1 pad_maximum_fusion
  53.0 24.8 %all-gather.2.cloned.1.call-done = bf16[4096,128]{1,0:T(8,128)(2,1)} async-done(((bf16[512,128]{1,0:T(8,128)(2,1)}), bf16[4096,128]{1,0:T(8,128)(2,1)}) %all-gather.2.cloned.1.call-update) | async-done | bytes 1048592 | tf_op jit(solution)/shard_map/all_gather | solution.py:125
  77.8 0.1 collective-permute-done.5.up
  77.9 1.2 copy-done.2
  79.1 1.6 %shard_map.114 = (bf16[2,128,128]{2,1,0:T(8,128)(2,1)}, bf16[2,128,128]{2,1,0:T(8,128)(2,1)S(1)}, bf16[4,128,128]{2,1,0:T(8,128)(2,1)S(1)}, bf16[4,128,128]{2,1,...) custom-call(s32[4]{0:T(128)S(1)} %pad_add_fusion.meta, ...), custom_call_target="tpu_custom_call" | custom-call | flops 134217728 | bytes 5242880 | tf_op jit(solution)/shard_map/pallas_call | solution.py:107
  80.7 0.6 copy-done.3
  81.4 0.6 copy-done.4
  82.0 0.6 copy-done.5
  82.7 0.7 copy-done.6
  83.3 0.6 copy-done.7
  84.0 0.6 copy-done.9
  84.6 0.8 collective-permute-start.8
  85.4 0.9 copy.13
  86.3 0.9 copy.14
  87.2 0.8 slice.29
  88.1 4.6 %collective-permute-start.12 = (bf16[2,128,128]{2,1,0:T(8,128)(2,1)}, bf16[2,128,128]{2,1,0:T(8,128)(2,1)S(1)}, u32[]{:S(2)}, u32[]{:S(2)}) collective-permute-start(bf16[2,128,128]{2,1,0:T(8,128)(2,1)} %copy-done.9), channel_id=1, source_target_pairs={{0,56},{8,0},{16,8},{24,16},{32,24},{40,32},{48,40},{56,48},{1,57}... | collective-permute-start | bytes 196616 | tf_op jit(solution)/shard_map/ppermute | solution.py:18
  92.7 0.8 slice.30
  93.6 3.8 %collective-permute-start.17 = (f32[128,128]{1,0:T(8,128)S(1)}, f32[128,128]{1,0:T(8,128)S(1)}, u32[]{:S(2)}, u32[]{:S(2)}) collective-permute-start(f32[128,128]{1,0:T(8,128)S(1)} %add.81), channel_id=1, source_target_pairs={{0,2},{2,4},{4,6},{6,0},{1,3},{3,5},{5,7},{7,1},{8,10},{10,12},{12... | collective-permute-start | bytes 196616 | tf_op jit(solution)/shard_map/ppermute | solution.py:18
  97.3 2.2 %collective-permute-start.19 = (f32[128,128]{1,0:T(8,128)S(1)}, f32[128,128]{1,0:T(8,128)S(1)}, u32[]{:S(2)}, u32[]{:S(2)}) collective-permute-start(f32[128,128]{1,0:T(8,128)S(1)} %add.81), channel_id=1, source_target_pairs={{0,4},{2,6},{4,0},{6,2},{1,5},{3,7},{5,1},{7,3},{8,12},{10,14},{12... | collective-permute-start | bytes 196616 | tf_op jit(solution)/shard_map/ppermute | solution.py:18
  99.5 0.9 add_convert_fusion.9
  100.4 1.1 collective-permute-start.9
  101.5 0.9 add_convert_fusion.8
  102.4 0.7 collective-permute-done.19
  103.1 0.1 collective-permute-start.20
  103.2 3.2 %collective-permute-start.21 = (f32[128,128]{1,0:T(8,128)S(1)}, f32[128,128]{1,0:T(8,128)S(1)}, u32[]{:S(2)}, u32[]{:S(2)}) collective-permute-start(f32[128,128]{1,0:T(8,128)S(1)} %add_add_fusion.2), channel_id=1, source_target_pairs={{0,192},{64,0},{128,64},{192,128},{1,193},{65,1},{129,65},{193,129... | collective-permute-start | bytes 196616 | tf_op jit(solution)/shard_map/ppermute | solution.py:18
  106.5 2.9 %collective-permute-start.13 = (bf16[4,128,128]{2,1,0:T(8,128)(2,1)S(1)}, bf16[4,128,128]{2,1,0:T(8,128)(2,1)S(1)}, u32[]{:S(2)}, u32[]{:S(2)}) collective-permute-start(bf16[4,128,128]{2,1,0:T(8,128)(2,1)S(1)} %pad_maximum_fusion.4), channel_id=1, source_target_pairs={{0,56},{8,0},{16,8},{24,16},{32,24},{40,32},{48,40},{56,48},{1,57}... | collective-permute-start | bytes 393224 | tf_op jit(solution)/shard_map/ppermute | solution.py:18
  109.4 2.8 %collective-permute-done.22 = f32[128,128]{1,0:T(8,128)S(1)} collective-permute-done((f32[128,128]{1,0:T(8,128)S(1)}, f32[128,128]{1,0:T(8,128)S(1)}, u32[]{:S(2)}, u32[]{:S(2)}) %collective-permute-start.22) | collective-permute-done | bytes 65568 | tf_op jit(solution)/shard_map/ppermute | solution.py:18
  112.2 1.8 %collective-permute-start.23 = (f32[128,128]{1,0:T(8,128)S(1)}, f32[128,128]{1,0:T(8,128)S(1)}, u32[]{:S(2)}, u32[]{:S(2)}) collective-permute-start(f32[128,128]{1,0:T(8,128)S(1)} %add_add_fusion.1), channel_id=1, source_target_pairs={{0,8},{8,16},{16,24},{24,32},{32,40},{40,48},{48,56},{56,0},{1,9},... | collective-permute-start | bytes 196616 | tf_op jit(solution)/shard_map/ppermute | solution.py:18
  114.0 1.2 collective-permute-start.24
  115.2 5.2 %collective-permute-start.25 = (f32[128,128]{1,0:T(8,128)S(1)}, f32[128,128]{1,0:T(8,128)S(1)}, u32[]{:S(2)}, u32[]{:S(2)}) collective-permute-start(f32[128,128]{1,0:T(8,128)S(1)} %add_add_fusion.1), channel_id=1, source_target_pairs={{0,16},{8,24},{16,32},{24,40},{32,48},{40,56},{48,0},{56,8},{1,17}... | collective-permute-start | bytes 196616 | tf_op jit(solution)/shard_map/ppermute | solution.py:18
  120.4 0.9 add_convert_fusion.6
  121.4 3.3 %collective-permute-start.10 = (bf16[4,128,128]{2,1,0:T(8,128)(2,1)S(1)}, bf16[4,128,128]{2,1,0:T(8,128)(2,1)S(1)}, u32[]{:S(2)}, u32[]{:S(2)}) collective-permute-start(bf16[4,128,128]{2,1,0:T(8,128)(2,1)S(1)} %add_convert_fusion.6), channel_id=1, source_target_pairs={{0,8},{8,16},{16,24},{24,32},{32,40},{40,48},{48,56},{56,0},{1,9},... | collective-permute-start | bytes 393224 | tf_op jit(solution)/shard_map/ppermute | solution.py:18
  124.7 0.9 add_convert_fusion.4
  125.6 0.1 collective-permute-start.14
  125.8 2.8 %collective-permute-start.26 = (f32[128,128]{1,0:T(8,128)S(1)}, f32[128,128]{1,0:T(8,128)S(1)}, u32[]{:S(2)}, u32[]{:S(2)}) collective-permute-start(f32[128,128]{1,0:T(8,128)S(1)} %add_add_fusion), channel_id=1, source_target_pairs={{0,32},{8,40},{16,48},{24,56},{32,0},{40,8},{48,16},{56,24},{1,33}... | collective-permute-start | bytes 196616 | tf_op jit(solution)/shard_map/ppermute | solution.py:18
  128.6 1.3 collective-permute-done.10
  129.9 0.9 add_convert_fusion.5
  130.8 2.6 %collective-permute-start.11 = (bf16[4,128,128]{2,1,0:T(8,128)(2,1)S(1)}, bf16[4,128,128]{2,1,0:T(8,128)(2,1)S(1)}, u32[]{:S(2)}, u32[]{:S(2)}) collective-permute-start(bf16[4,128,128]{2,1,0:T(8,128)(2,1)S(1)} %add_convert_fusion.5), channel_id=1, source_target_pairs={{0,8},{8,16},{16,24},{24,32},{32,40},{40,48},{48,56},{56,0},{1,9},... | collective-permute-start | bytes 393224 | tf_op jit(solution)/shard_map/ppermute | solution.py:18
  133.4 0.1 collective-permute-start.15
  133.5 0.5 collective-permute-done.26
  134.1 0.7 copy.15
  134.8 1.2 collective-permute-done.11
  136.0 2.5 %collective-permute-done.15 = bf16[4,128,128]{2,1,0:T(8,128)(2,1)S(1)} collective-permute-done((bf16[4,128,128]{2,1,0:T(8,128)(2,1)S(1)}, bf16[4,128,128]{2,1,0:T(8,128)(2,1)S(1)}, u32[]{:S(2)}, u32[]{:S(2)}) %collective-permute-start.15) | collective-permute-done | bytes 131104 | tf_op jit(solution)/shard_map/ppermute | solution.py:18
  138.5 0.9 convolution_convert_fusion
  (45 shorter events, 0.4 us)
Async XLA Ops:
  7.2 131.3 %copy-start = (bf16[128,128]{1,0:T(8,128)(2,1)S(1)}, bf16[128,128]{1,0:T(8,128)(2,1)}, u32[]{:S(2)}) copy-start(bf16[128,128]{1,0:T(8,128)(2,1)} %param.17) | copy-start | bytes 98308
  7.2 70.6 %all-gather.2.cloned.1.call-start = ((), (), s32[]{:S(2)}) async-start(), calls=%async_computation | async-start | bytes 1179648 | tf_op jit(solution)/shard_map/all_gather | solution.py:125
  8.2 6.6 %collective-permute-start = (bf16[16,4096]{1,0:T(8,128)(2,1)S(1)}, bf16[16,4096]{1,0:T(8,128)(2,1)S(1)}, u32[]{:S(2)}, u32[]{:S(2)}) collective-permute-start(bf16[16,4096]{1,0:T(8,128)(2,1)S(1)} %fusion), channel_id=1, source_target_pairs={{0,2},{2,4},{4,6},{6,0},{1,3},{3,5},{5,7},{7,1},{8,10},{10,12},{12... | collective-permute-start | bytes 393224 | tf_op jit(solution)/shard_map/ppermute | solution.py:18
  9.9 7.1 %collective-permute-start.1 = (bf16[16,4096]{1,0:T(8,128)(2,1)S(1)}, bf16[16,4096]{1,0:T(8,128)(2,1)S(1)}, u32[]{:S(2)}, u32[]{:S(2)}) collective-permute-start(bf16[16,4096]{1,0:T(8,128)(2,1)S(1)} %fusion), channel_id=1, source_target_pairs={{0,6},{2,0},{4,2},{6,4},{1,7},{3,1},{5,3},{7,5},{8,14},{10,8},{12,... | collective-permute-start | bytes 393224 | tf_op jit(solution)/shard_map/ppermute | solution.py:18
  11.6 7.3 %collective-permute-start.2 = (bf16[16,4096]{1,0:T(8,128)(2,1)S(1)}, bf16[16,4096]{1,0:T(8,128)(2,1)S(1)}, u32[]{:S(2)}, u32[]{:S(2)}) collective-permute-start(bf16[16,4096]{1,0:T(8,128)(2,1)S(1)} %fusion), channel_id=1, source_target_pairs={{0,4},{2,6},{4,0},{6,2},{1,5},{3,7},{5,1},{7,3},{8,12},{10,14},{12... | collective-permute-start | bytes 393224 | tf_op jit(solution)/shard_map/ppermute | solution.py:18
  18.9 2.0 %collective-permute-start.3 = (bf16[64,4096]{1,0:T(8,128)(2,1)S(1)}, bf16[64,4096]{1,0:T(8,128)(2,1)S(1)}, u32[]{:S(2)}, u32[]{:S(2)}) collective-permute-start(bf16[64,4096]{1,0:T(8,128)(2,1)S(1)} %pad_maximum_fusion.2.mine), channel_id=1, source_target_pairs={{0,1},{1,0},{2,3},{3,2},{4,5},{5,4},{6,7},{7,6},{8,9},{9,8},{10,11... | collective-permute-start | bytes 1572872 | tf_op jit(solution)/shard_map/ppermute | solution.py:129
  20.9 3.4 %copy-start.1 = (bf16[1,1,256,128,128]{4,3,2,1,0:T(8,128)(2,1)S(1)}, bf16[1,1,256,128,128]{4,3,2,1,0:T(8,128)(2,1)}, u32[]{:S(2)}) copy-start(bf16[1,1,256,128,128]{4,3,2,1,0:T(8,128)(2,1)} %param.10) | copy-start | bytes 25165828
  24.2 0.7 copy-start.8
  31.6 13.3 %collective-permute-start.6 = (bf16[16,128,128]{2,1,0:T(8,128)(2,1)}, bf16[16,128,128]{2,1,0:T(8,128)(2,1)}, u32[]{:S(2)}, u32[]{:S(2)}) collective-permute-start(bf16[16,128,128]{2,1,0:T(8,128)(2,1)} %get-tuple-element.21), channel_id=1, source_target_pairs={{0,192},{64,0},{128,64},{192,128},{1,193},{65,1},{129,65},{193,129... | collective-permute-start | bytes 1572872 | tf_op jit(solution)/shard_map/ppermute | solution.py:18
  35.6 15.2 %collective-permute-start.4 = (bf16[16,128,128]{2,1,0:T(8,128)(2,1)}, bf16[16,128,128]{2,1,0:T(8,128)(2,1)}, u32[]{:S(2)}, u32[]{:S(2)}) collective-permute-start(bf16[16,128,128]{2,1,0:T(8,128)(2,1)} %get-tuple-element.19), channel_id=1, source_target_pairs={{0,64},{64,128},{128,192},{192,0},{1,65},{65,129},{129,193},{193,1... | collective-permute-start | bytes 1572872 | tf_op jit(solution)/shard_map/ppermute | solution.py:18
  47.2 30.6 %collective-permute-start.7 = (bf16[32,128,128]{2,1,0:T(8,128)(2,1)}, bf16[32,128,128]{2,1,0:T(8,128)(2,1)S(1)}, u32[]{:S(2)}, u32[]{:S(2)}) collective-permute-start(bf16[32,128,128]{2,1,0:T(8,128)(2,1)} %pad_maximum_fusion.1), channel_id=1, source_target_pairs={{0,192},{64,0},{128,64},{192,128},{1,193},{65,1},{129,65},{193,129... | collective-permute-start | bytes 3145736 | tf_op jit(solution)/shard_map/ppermute | solution.py:18
  53.0 24.9 %collective-permute-start.5 = (bf16[32,128,128]{2,1,0:T(8,128)(2,1)}, bf16[32,128,128]{2,1,0:T(8,128)(2,1)S(1)}, u32[]{:S(2)}, u32[]{:S(2)}) collective-permute-start(bf16[32,128,128]{2,1,0:T(8,128)(2,1)} %pad_maximum_fusion), channel_id=1, source_target_pairs={{0,64},{64,128},{128,192},{192,0},{1,65},{65,129},{129,193},{193,1... | collective-permute-start | bytes 3145736 | tf_op jit(solution)/shard_map/ppermute | solution.py:18
  77.9 1.2 copy-start.2
  80.7 0.6 copy-start.3
  81.4 0.7 copy-start.4
  82.0 0.7 copy-start.5
  82.7 0.7 copy-start.6
  83.3 0.6 copy-start.7
  84.0 0.6 copy-start.9
  84.6 9.0 %collective-permute-start.16 = (f32[128,128]{1,0:T(8,128)S(1)}, f32[128,128]{1,0:T(8,128)S(1)}, u32[]{:S(2)}, u32[]{:S(2)}) collective-permute-start(f32[128,128]{1,0:T(8,128)S(1)} %get-tuple-element.31), channel_id=1, source_target_pairs={{0,1},{1,0},{2,3},{3,2},{4,5},{5,4},{6,7},{7,6},{8,9},{9,8},{10,11... | collective-permute-start | bytes 196616 | tf_op jit(solution)/shard_map/ppermute | solution.py:158
  84.6 14.9 %collective-permute-start.8 = (bf16[2,128,128]{2,1,0:T(8,128)(2,1)}, bf16[2,128,128]{2,1,0:T(8,128)(2,1)S(1)}, u32[]{:S(2)}, u32[]{:S(2)}) collective-permute-start(bf16[2,128,128]{2,1,0:T(8,128)(2,1)} %get-tuple-element.26), channel_id=1, source_target_pairs={{0,8},{8,16},{16,24},{24,32},{32,40},{40,48},{48,56},{56,0},{1,9},... | collective-permute-start | bytes 196616 | tf_op jit(solution)/shard_map/ppermute | solution.py:18
  88.1 13.4 %collective-permute-start.12 = (bf16[2,128,128]{2,1,0:T(8,128)(2,1)}, bf16[2,128,128]{2,1,0:T(8,128)(2,1)S(1)}, u32[]{:S(2)}, u32[]{:S(2)}) collective-permute-start(bf16[2,128,128]{2,1,0:T(8,128)(2,1)} %copy-done.9), channel_id=1, source_target_pairs={{0,56},{8,0},{16,8},{24,16},{32,24},{40,32},{48,40},{56,48},{1,57}... | collective-permute-start | bytes 196616 | tf_op jit(solution)/shard_map/ppermute | solution.py:18
  93.6 8.8 %collective-permute-start.17 = (f32[128,128]{1,0:T(8,128)S(1)}, f32[128,128]{1,0:T(8,128)S(1)}, u32[]{:S(2)}, u32[]{:S(2)}) collective-permute-start(f32[128,128]{1,0:T(8,128)S(1)} %add.81), channel_id=1, source_target_pairs={{0,2},{2,4},{4,6},{6,0},{1,3},{3,5},{5,7},{7,1},{8,10},{10,12},{12... | collective-permute-start | bytes 196616 | tf_op jit(solution)/shard_map/ppermute | solution.py:18
  97.3 5.0 %collective-permute-start.18 = (f32[128,128]{1,0:T(8,128)S(1)}, f32[128,128]{1,0:T(8,128)S(1)}, u32[]{:S(2)}, u32[]{:S(2)}) collective-permute-start(f32[128,128]{1,0:T(8,128)S(1)} %add.81), channel_id=1, source_target_pairs={{0,6},{2,0},{4,2},{6,4},{1,7},{3,1},{5,3},{7,5},{8,14},{10,8},{12,... | collective-permute-start | bytes 196616 | tf_op jit(solution)/shard_map/ppermute | solution.py:18
  97.3 5.8 %collective-permute-start.19 = (f32[128,128]{1,0:T(8,128)S(1)}, f32[128,128]{1,0:T(8,128)S(1)}, u32[]{:S(2)}, u32[]{:S(2)}) collective-permute-start(f32[128,128]{1,0:T(8,128)S(1)} %add.81), channel_id=1, source_target_pairs={{0,4},{2,6},{4,0},{6,2},{1,5},{3,7},{5,1},{7,3},{8,12},{10,14},{12... | collective-permute-start | bytes 196616 | tf_op jit(solution)/shard_map/ppermute | solution.py:18
  100.4 20.0 %collective-permute-start.9 = (bf16[4,128,128]{2,1,0:T(8,128)(2,1)S(1)}, bf16[4,128,128]{2,1,0:T(8,128)(2,1)S(1)}, u32[]{:S(2)}, u32[]{:S(2)}) collective-permute-start(bf16[4,128,128]{2,1,0:T(8,128)(2,1)S(1)} %pad_maximum_fusion.3), channel_id=1, source_target_pairs={{0,8},{8,16},{16,24},{24,32},{32,40},{40,48},{48,56},{56,0},{1,9},... | collective-permute-start | bytes 393224 | tf_op jit(solution)/shard_map/ppermute | solution.py:18
  103.1 6.3 %collective-permute-start.20 = (f32[128,128]{1,0:T(8,128)S(1)}, f32[128,128]{1,0:T(8,128)S(1)}, u32[]{:S(2)}, u32[]{:S(2)}) collective-permute-start(f32[128,128]{1,0:T(8,128)S(1)} %add_add_fusion.2), channel_id=1, source_target_pairs={{0,64},{64,128},{128,192},{192,0},{1,65},{65,129},{129,193},{193,1... | collective-permute-start | bytes 196616 | tf_op jit(solution)/shard_map/ppermute | solution.py:18
  103.2 6.2 %collective-permute-start.21 = (f32[128,128]{1,0:T(8,128)S(1)}, f32[128,128]{1,0:T(8,128)S(1)}, u32[]{:S(2)}, u32[]{:S(2)}) collective-permute-start(f32[128,128]{1,0:T(8,128)S(1)} %add_add_fusion.2), channel_id=1, source_target_pairs={{0,192},{64,0},{128,64},{192,128},{1,193},{65,1},{129,65},{193,129... | collective-permute-start | bytes 196616 | tf_op jit(solution)/shard_map/ppermute | solution.py:18
  106.5 5.8 %collective-permute-start.22 = (f32[128,128]{1,0:T(8,128)S(1)}, f32[128,128]{1,0:T(8,128)S(1)}, u32[]{:S(2)}, u32[]{:S(2)}) collective-permute-start(f32[128,128]{1,0:T(8,128)S(1)} %add_add_fusion.2), channel_id=1, source_target_pairs={{0,128},{64,192},{128,0},{192,64},{1,129},{65,193},{129,1},{193,65... | collective-permute-start | bytes 196616 | tf_op jit(solution)/shard_map/ppermute | solution.py:18
  106.5 18.2 %collective-permute-start.13 = (bf16[4,128,128]{2,1,0:T(8,128)(2,1)S(1)}, bf16[4,128,128]{2,1,0:T(8,128)(2,1)S(1)}, u32[]{:S(2)}, u32[]{:S(2)}) collective-permute-start(bf16[4,128,128]{2,1,0:T(8,128)(2,1)S(1)} %pad_maximum_fusion.4), channel_id=1, source_target_pairs={{0,56},{8,0},{16,8},{24,16},{32,24},{40,32},{48,40},{56,48},{1,57}... | collective-permute-start | bytes 393224 | tf_op jit(solution)/shard_map/ppermute | solution.py:18
  112.2 13.5 %collective-permute-start.23 = (f32[128,128]{1,0:T(8,128)S(1)}, f32[128,128]{1,0:T(8,128)S(1)}, u32[]{:S(2)}, u32[]{:S(2)}) collective-permute-start(f32[128,128]{1,0:T(8,128)S(1)} %add_add_fusion.1), channel_id=1, source_target_pairs={{0,8},{8,16},{16,24},{24,32},{32,40},{40,48},{48,56},{56,0},{1,9},... | collective-permute-start | bytes 196616 | tf_op jit(solution)/shard_map/ppermute | solution.py:18
  114.0 11.7 %collective-permute-start.24 = (f32[128,128]{1,0:T(8,128)S(1)}, f32[128,128]{1,0:T(8,128)S(1)}, u32[]{:S(2)}, u32[]{:S(2)}) collective-permute-start(f32[128,128]{1,0:T(8,128)S(1)} %add_add_fusion.1), channel_id=1, source_target_pairs={{0,56},{8,0},{16,8},{24,16},{32,24},{40,32},{48,40},{56,48},{1,57}... | collective-permute-start | bytes 196616 | tf_op jit(solution)/shard_map/ppermute | solution.py:18
  115.2 10.5 %collective-permute-start.25 = (f32[128,128]{1,0:T(8,128)S(1)}, f32[128,128]{1,0:T(8,128)S(1)}, u32[]{:S(2)}, u32[]{:S(2)}) collective-permute-start(f32[128,128]{1,0:T(8,128)S(1)} %add_add_fusion.1), channel_id=1, source_target_pairs={{0,16},{8,24},{16,32},{24,40},{32,48},{40,56},{48,0},{56,8},{1,17}... | collective-permute-start | bytes 196616 | tf_op jit(solution)/shard_map/ppermute | solution.py:18
  121.4 8.5 %collective-permute-start.10 = (bf16[4,128,128]{2,1,0:T(8,128)(2,1)S(1)}, bf16[4,128,128]{2,1,0:T(8,128)(2,1)S(1)}, u32[]{:S(2)}, u32[]{:S(2)}) collective-permute-start(bf16[4,128,128]{2,1,0:T(8,128)(2,1)S(1)} %add_convert_fusion.6), channel_id=1, source_target_pairs={{0,8},{8,16},{16,24},{24,32},{32,40},{40,48},{48,56},{56,0},{1,9},... | collective-permute-start | bytes 393224 | tf_op jit(solution)/shard_map/ppermute | solution.py:18
  125.6 7.7 %collective-permute-start.14 = (bf16[4,128,128]{2,1,0:T(8,128)(2,1)S(1)}, bf16[4,128,128]{2,1,0:T(8,128)(2,1)S(1)}, u32[]{:S(2)}, u32[]{:S(2)}) collective-permute-start(bf16[4,128,128]{2,1,0:T(8,128)(2,1)S(1)} %add_convert_fusion.4), channel_id=1, source_target_pairs={{0,56},{8,0},{16,8},{24,16},{32,24},{40,32},{48,40},{56,48},{1,57}... | collective-permute-start | bytes 393224 | tf_op jit(solution)/shard_map/ppermute | solution.py:18
  125.8 8.3 %collective-permute-start.26 = (f32[128,128]{1,0:T(8,128)S(1)}, f32[128,128]{1,0:T(8,128)S(1)}, u32[]{:S(2)}, u32[]{:S(2)}) collective-permute-start(f32[128,128]{1,0:T(8,128)S(1)} %add_add_fusion), channel_id=1, source_target_pairs={{0,32},{8,40},{16,48},{24,56},{32,0},{40,8},{48,16},{56,24},{1,33}... | collective-permute-start | bytes 196616 | tf_op jit(solution)/shard_map/ppermute | solution.py:18
  130.8 5.2 %collective-permute-start.11 = (bf16[4,128,128]{2,1,0:T(8,128)(2,1)S(1)}, bf16[4,128,128]{2,1,0:T(8,128)(2,1)S(1)}, u32[]{:S(2)}, u32[]{:S(2)}) collective-permute-start(bf16[4,128,128]{2,1,0:T(8,128)(2,1)S(1)} %add_convert_fusion.5), channel_id=1, source_target_pairs={{0,8},{8,16},{16,24},{24,32},{32,40},{40,48},{48,56},{56,0},{1,9},... | collective-permute-start | bytes 393224 | tf_op jit(solution)/shard_map/ppermute | solution.py:18
  133.4 5.0 %collective-permute-start.15 = (bf16[4,128,128]{2,1,0:T(8,128)(2,1)S(1)}, bf16[4,128,128]{2,1,0:T(8,128)(2,1)S(1)}, u32[]{:S(2)}, u32[]{:S(2)}) collective-permute-start(bf16[4,128,128]{2,1,0:T(8,128)(2,1)S(1)} %add_convert_fusion.3), channel_id=1, source_target_pairs={{0,56},{8,0},{16,8},{24,16},{32,24},{40,32},{48,40},{56,48},{1,57}... | collective-permute-start | bytes 393224 | tf_op jit(solution)/shard_map/ppermute | solution.py:18
Sparse Core Ops, SparseCore 0:
  35.7 42.0 all-gather.1

commit v2 on v1

v2 whole, which is shorter than its diff:
```python
import jax
import jax.numpy as jnp
from jax import lax
from jax.experimental import pallas as pl
from jax.experimental.pallas import tpu as pltpu
from jax.sharding import Mesh, PartitionSpec as P

XS, ZS, YS, CS = 4, 8, 4, 2
T = 128
UNROLL = 8
F32, BF16 = jnp.float32, jnp.bfloat16


def shift(value, axis, size, by):
    return lax.ppermute(value, axis, [(i, (i + by) % size) for i in range(size)])


def fetch_kernel(source, target, sem):
    copy = pltpu.make_async_copy(source, target, sem)
    copy.start()
    copy.wait()


def fetch(array):
    return pl.pallas_call(
        fetch_kernel,
        in_specs=[pl.BlockSpec(memory_space=pl.ANY)],
        out_specs=pl.BlockSpec(memory_space=pltpu.VMEM),
        out_shape=jax.ShapeDtypeStruct(array.shape, array.dtype),
        scratch_shapes=[pltpu.SemaphoreType.DMA],
        compiler_params=pltpu.CompilerParams(vmem_limit_bytes=12 * 2**20),
        cost_estimate=pl.CostEstimate(flops=0, bytes_accessed=16 * 2**20, transcendentals=0),
    )(array)


PLACED = ((64, 16), (80, 16), (48, 16), (96, 16), (32, 16), (112, 16), (0, 32))


def tile_kernel(rows, places, meta, tiles, mine, other, *rest):
    outs, (wide, acc) = rest[:7], rest[7:]
    for part, dist in enumerate((0, 1, 3, 2)):
        y_of = (meta[1] - dist) & (YS - 1)
        for ref, core in ((mine, meta[2]), (other, 1 - meta[2])):
            at = pl.multiple_of((y_of * CS + core) * 16, 16)
            wide[pl.ds(at, 16), :] = ref[part * 16 : part * 16 + 16, :]

    def clear(i, _):
        acc[pl.ds(i * 4, 4)] = jnp.zeros((4, T, T), F32)
        return 0

    lax.fori_loop(0, 32, clear, 0)

    def several(g, _):
        base = g * UNROLL
        products = []
        for u in range(UNROLL):
            at = pl.multiple_of(rows[base + u] * T, T)
            products.append(jnp.dot(wide[:, pl.ds(at, T)], tiles[base + u], preferred_element_type=F32))
        for u in range(UNROLL):
            place = places[base + u]
            acc[place] = acc[place] + products[u]
        return 0

    used = jnp.clip(meta[0], 0, tiles.shape[0])
    lax.fori_loop(0, (used + UNROLL - 1) >> 3, several, 0)

    for out, (first, size) in zip(outs, PLACED):

        def put(i, _):
            out[pl.ds(i * 4, 4)] = acc[pl.ds(first + i * 4, 4)].astype(BF16)
            return 0

        lax.fori_loop(0, size // 4, put, 0)


def tile_products(rows, places, meta, tiles, mine, other):
    smem, vmem = pl.BlockSpec(memory_space=pltpu.SMEM), pl.BlockSpec(memory_space=pltpu.VMEM)
    return pl.pallas_call(
        tile_kernel,
        in_specs=[smem] * 3 + [vmem] * 3,
        out_specs=[vmem] * 7,
        scratch_shapes=[pltpu.VMEM((T, mine.shape[1]), BF16), pltpu.VMEM((129, T, T), F32)],
        out_shape=[jax.ShapeDtypeStruct((n, T, T), BF16) for _, n in PLACED],
        compiler_params=pltpu.CompilerParams(vmem_limit_bytes=32 * 2**20),
        cost_estimate=pl.CostEstimate(flops=2**30, bytes_accessed=13 * 2**20, transcendentals=0),
    )(rows, places, meta, tiles, mine, other)


def middle_kernel(c0, upa, upb, downa, downb, feats, out, grad):
    grad[...] = jnp.zeros((T, T), F32)
    for first, up, down in ((0, upa, downa), (16, upb, downb)):

        def several(i, _):
            total = grad[...]
            for u in range(4):
                n, k = i * 4 + u, first + i * 4 + u
                value = (c0[k].astype(F32) + up[n].astype(F32) + down[n].astype(F32)).astype(BF16)
                out[k] = value
                total += jnp.dot(value, feats[k], preferred_element_type=F32)
            grad[...] = total
            return 0

        lax.fori_loop(0, 4, several, 0)


def middle(*operands):
    spec = pl.BlockSpec(memory_space=pltpu.VMEM)
    return pl.pallas_call(
        middle_kernel,
        in_specs=[spec] * 6,
        out_specs=[spec] * 2,
        out_shape=[jax.ShapeDtypeStruct((32, T, T), BF16), jax.ShapeDtypeStruct((T, T), F32)],
        compiler_params=pltpu.CompilerParams(vmem_limit_bytes=12 * 2**20),
        cost_estimate=pl.CostEstimate(flops=2**27, bytes_accessed=5 * 2**20, transcendentals=0),
    )(*operands)


def add(*values):
    return sum(v.astype(F32) for v in values).astype(BF16)


def local(tile_vals, tile_row, tile_col, tile_count, out_grad, relu_mask, features, weight, importance, weight_delta):
    x, y, core = (lax.axis_index(a) for a in ("x", "y", "core"))
    slots = tile_vals.shape[2]
    wide_feats = lax.all_gather(features, "z", axis=0, tiled=True).reshape(ZS * 4, T, T)

    masked = (out_grad.astype(F32) * relu_mask.astype(F32)).astype(BF16).T
    mine = jnp.concatenate([masked] + [shift(masked, "y", YS, d) for d in (1, 3, 2)], axis=0)
    other = lax.ppermute(mine, "core", [(0, 1), (1, 0)])

    count = tile_count.reshape(())
    cols = tile_col.reshape(slots)
    dest = cols >> 2
    dx = ((dest >> 3) - x) & (XS - 1)
    places = jnp.where(lax.iota(jnp.int32, slots) < count, dx * 32 + (cols & 31), 128)
    meta = jnp.stack([count, y, core]).astype(jnp.int32)
    tiles = fetch(tile_vals.reshape(slots, T, T))
    c2a, c2b, c1b, c3a, c1a, c3b, c0 = tile_products(tile_row.reshape(slots), places, meta, tiles, mine, other)

    up, down = shift(c2a, "x", XS, 1), shift(c2b, "x", XS, 3)
    upb, downa = shift(c1b, "x", XS, 1), shift(c3a, "x", XS, 3)
    upa, downb = shift(add(c1a, up), "x", XS, 1), shift(add(c3b, down), "x", XS, 3)
    reduced, grad = middle(c0, upa, upb, downa, downb, wide_feats)

    aggregate = lax.psum_scatter(reduced, "z", scatter_dimension=0, tiled=True)
    input_grad = jnp.einsum("qfj,df->qjd", aggregate, weight, preferred_element_type=F32)
    input_grad = input_grad.astype(BF16).reshape(features.shape[0], weight.shape[0])

    grad = grad + lax.ppermute(grad, "core", [(0, 1), (1, 0)])
    grad = grad + shift(grad, "y", YS, 1) + shift(grad, "y", YS, 3) + shift(grad, "y", YS, 2)
    grad = grad + shift(grad, "x", XS, 1) + shift(grad, "x", XS, 3) + shift(grad, "x", XS, 2)
    grad = grad + shift(grad, "z", ZS, 1) + shift(grad, "z", ZS, 7) + shift(grad, "z", ZS, 2)
    grad = grad + shift(grad, "z", ZS, 4)
    return input_grad, importance - grad.T * weight_delta


def solution(mesh):
    mesh = Mesh(mesh.devices.reshape(XS, ZS, YS, CS), ("x", "z", "y", "core"))
    row, col = ("x", "z"), ("y", "core")
    return jax.shard_map(
        local,
        mesh=mesh,
        in_specs=(
            P(row, col, None, None, None),
            P(row, col, None),
            P(row, col, None),
            P(row, col),
            P(row, col),
            P(row, col),
            P(row + col, None),
            P(),
            P(),
            P(),
        ),
        out_specs=(P(row + col, None), P()),
        check_vma=False,
    )
```

time: 145 us -> 125 us (0.86); the launches traced: 146 us -> 124 us
  starting transfers between devices: 48.5 us -> 31.7 us
  other arithmetic: 11 us -> 2.18 us
  waiting for transfers between devices: 49.1 us -> 57.2 us
  local copies, waits for them, and re-layouts: 13.5 us -> 5.55 us
  Pallas kernels: 8.35 us -> 10.8 us
    ppermute x25 -> x19, waiting for transfers between devices: 23.1 us -> 56 us  [shift(): lax.ppermute(value, axis, [(i, (i + by) % size) for i in range(size)])]
    all_gather x1, waiting for transfers between devices: 24.8 us -> 0.01 us  [local(): lax.all_gather(features, 'z', axis=0, tiled=True).reshape(ZS * 4, T, T)]
    ppermute x25 -> x19, starting transfers between devices: 48.3 us -> 31.4 us  [shift(): lax.ppermute(value, axis, [(i, (i + by) % size) for i in range(size)])]
    convert_element_type x8 -> x2, other arithmetic: 6.95 us -> 0.28 us  [add(): return sum((v.astype(F32) for v in values)).astype(BF16)]
    unnamed x23 -> x15, local copies, waits for them, and re-layouts: 11.7 us -> 5.55 us
    pallas_call x2 -> x3, Pallas kernels: 8.35 us -> 10.8 us  [the longest x1 7.86 us: tile_products(): pl.pallas_call(tile_kernel, in_specs=[smem] * 3 + [vmem] * 3, out_specs=[...]
    concatenate x4 -> x0, other arithmetic: 2.17 us -> none  [the longest x1 1.08 us: local(): s1 = jnp.concatenate([add(c1[:16], up), c1[16:]], axis=0)]
    slice x4 -> x0, local copies, waits for them, and re-layouts: 1.77 us -> none  [the longest x1 0.85 us: local(): up = jnp.concatenate([add(z3[:2], up), z3[2:]], axis=0)]
  transfers between devices with their start and end apart: 28 -> 23, of which waited for: 14 -> 16; matrix products, arithmetic and copies ran while one was open for 10% -> 2% of each run, Pallas kernels for 0% -> 7%
where the time goes in v2:
time: 125 us; the launch traced here: 124 us
  waiting for transfers between devices  57.2 us (46%)
  starting transfers between devices  31.7 us (25%)
  between operations  14.8 us (12%)
  Pallas kernels  10.8 us (9%)
  local copies, waits for them, and re-layouts  5.55 us (4%)
  other arithmetic  2.18 us (2%)
  matrix products  1.77 us (1%)
    ppermute x19, waiting for transfers between devices, shift(): lax.ppermute(value, axis, [(i, (i + by) % size) for i in range(size)])  56 us
    ppermute x19, starting transfers between devices, shift(): lax.ppermute(value, axis, [(i, (i + by) % size) for i in range(size)])  31.4 us
    pallas_call x1, Pallas kernels, tile_products(): pl.pallas_call(tile_kernel, in_specs=[smem] * 3 + [vmem] * 3, out_specs=[...  7.86 us
    unnamed x15, local copies, waits for them, and re-layouts  5.55 us
  transfers between devices with their start and end apart: 23, of which 16 were waited for; matrix products, arithmetic and copies ran while one was open for 2% of the time, Pallas kernels for 7%

profile of v2, /device:TPU:32, one launch (start us, length us, event | category | flops | bytes accessed | tf_op | source)
XLA Modules:
  0.0 124.0 jit_solution(4571374993063037211)
XLA Ops:
  7.2 0.0 copy-start
  7.2 0.0 all-gather.2.cloned.1.call-start
  7.2 1.0 fusion
  8.2 1.7 %collective-permute-start = (bf16[16,4096]{1,0:T(8,128)(2,1)S(1)}, bf16[16,4096]{1,0:T(8,128)(2,1)S(1)}, u32[]{:S(2)}, u32[]{:S(2)}) collective-permute-start(bf16[16,4096]{1,0:T(8,128)(2,1)S(1)} %fusion), channel_id=1, source_target_pairs={{0,2},{2,4},{4,6},{6,0},{1,3},{3,5},{5,7},{7,1},{8,10},{10,12},{12... | collective-permute-start | bytes 393224 | tf_op jit(solution)/shard_map/ppermute | solution.py:15
  9.9 1.7 %collective-permute-start.1 = (bf16[16,4096]{1,0:T(8,128)(2,1)S(1)}, bf16[16,4096]{1,0:T(8,128)(2,1)S(1)}, u32[]{:S(2)}, u32[]{:S(2)}) collective-permute-start(bf16[16,4096]{1,0:T(8,128)(2,1)S(1)} %fusion), channel_id=1, source_target_pairs={{0,6},{2,0},{4,2},{6,4},{1,7},{3,1},{5,3},{7,5},{8,14},{10,8},{12,... | collective-permute-start | bytes 393224 | tf_op jit(solution)/shard_map/ppermute | solution.py:15
  11.6 2.0 %collective-permute-start.2 = (bf16[16,4096]{1,0:T(8,128)(2,1)S(1)}, bf16[16,4096]{1,0:T(8,128)(2,1)S(1)}, u32[]{:S(2)}, u32[]{:S(2)}) collective-permute-start(bf16[16,4096]{1,0:T(8,128)(2,1)S(1)} %fusion), channel_id=1, source_target_pairs={{0,4},{2,6},{4,0},{6,2},{1,5},{3,7},{5,1},{7,3},{8,12},{10,14},{12... | collective-permute-start | bytes 393224 | tf_op jit(solution)/shard_map/ppermute | solution.py:15
  13.5 0.0 all-gather.2.cloned.1.call-update
  13.6 0.0 reduce-scatter.2.cloned.1.call-start
  14.3 0.6 collective-permute-done
  14.8 2.2 %collective-permute-done.1 = bf16[16,4096]{1,0:T(8,128)(2,1)S(1)} collective-permute-done((bf16[16,4096]{1,0:T(8,128)(2,1)S(1)}, bf16[16,4096]{1,0:T(8,128)(2,1)S(1)}, u32[]{:S(2)}, u32[]{:S(2)}) %collective-permute-start.1) | collective-permute-done | bytes 131104 | tf_op jit(solution)/shard_map/ppermute | solution.py:15
  17.0 1.8 %collective-permute-done.2 = bf16[16,4096]{1,0:T(8,128)(2,1)S(1)} collective-permute-done((bf16[16,4096]{1,0:T(8,128)(2,1)S(1)}, bf16[16,4096]{1,0:T(8,128)(2,1)S(1)}, u32[]{:S(2)}, u32[]{:S(2)}) %collective-permute-start.2) | collective-permute-done | bytes 131104 | tf_op jit(solution)/shard_map/ppermute | solution.py:15
  18.9 0.1 collective-permute-start.3
  19.0 0.7 multiply_add_fusion
  19.7 3.4 %copy-done.1 = bf16[1,1,256,128,128]{4,3,2,1,0:T(8,128)(2,1)S(1)} copy-done((bf16[1,1,256,128,128]{4,3,2,1,0:T(8,128)(2,1)S(1)}, bf16[1,1,256,128,128]{4,3,2,1,0:T(8,128)(2,1)}, u32[]{:S(2)}) %copy-start.1) | copy-done | bytes 8388632
  23.0 0.6 shard_map.113.tiles
  23.6 0.1 pad_add_fusion.meta
  23.7 0.0 collective-permute-done.3.other
  23.7 0.0 copy-done.3
  23.7 7.9 %shard_map.114 = (bf16[16,128,128]{2,1,0:T(8,128)(2,1)S(1)}, bf16[16,128,128]{2,1,0:T(8,128)(2,1)S(1)}, bf16[16,128,128]{2,1,0:T(8,128)(2,1)S(1)}, bf16[16,128,1...) custom-call(s32[256]{0:T(256)S(1)} %bitcast.23, ...), custom_call_target="tpu_custom_call" | custom-call | flops 1073741824 | bytes 13631488 | tf_op jit(solution)/shard_map/pallas_call | solution.py:78
  31.6 1.6 %collective-permute-start.8 = (bf16[16,128,128]{2,1,0:T(8,128)(2,1)S(1)}, bf16[16,128,128]{2,1,0:T(8,128)(2,1)S(1)}, u32[]{:S(2)}, u32[]{:S(2)}) collective-permute-start(bf16[16,128,128]{2,1,0:T(8,128)(2,1)S(1)} %get-tuple-element.17), channel_id=1, source_target_pairs={{0,192},{64,0},{128,64},{192,128},{1,193},{65,1},{129,65},{193,129... | collective-permute-start | bytes 1572872 | tf_op jit(solution)/shard_map/ppermute | solution.py:15
  33.2 0.5 collective-permute-start.4
  33.7 1.0 collective-permute-start.6
  34.7 2.2 %collective-permute-start.7 = (bf16[16,128,128]{2,1,0:T(8,128)(2,1)S(1)}, bf16[16,128,128]{2,1,0:T(8,128)(2,1)S(1)}, u32[]{:S(2)}, u32[]{:S(2)}) collective-permute-start(bf16[16,128,128]{2,1,0:T(8,128)(2,1)S(1)} %get-tuple-element.15), channel_id=1, source_target_pairs={{0,192},{64,0},{128,64},{192,128},{1,193},{65,1},{129,65},{193,129... | collective-permute-start | bytes 1572872 | tf_op jit(solution)/shard_map/ppermute | solution.py:15
  36.9 9.5 %collective-permute-done.8 = bf16[16,128,128]{2,1,0:T(8,128)(2,1)S(1)} collective-permute-done((bf16[16,128,128]{2,1,0:T(8,128)(2,1)S(1)}, bf16[16,128,128]{2,1,0:T(8,128)(2,1)S(1)}, u32[]{:S(2)}, u32[]{:S(2)}) %collective-permute-start.8) | collective-permute-done | bytes 524320 | tf_op jit(solution)/shard_map/ppermute | solution.py:15
  46.5 0.1 add_convert_fusion
  46.6 2.9 %collective-permute-start.9 = (bf16[16,128,128]{2,1,0:T(8,128)(2,1)S(1)}, bf16[16,128,128]{2,1,0:T(8,128)(2,1)S(1)}, u32[]{:S(2)}, u32[]{:S(2)}) collective-permute-start(bf16[16,128,128]{2,1,0:T(8,128)(2,1)S(1)} %add_convert_fusion), channel_id=1, source_target_pairs={{0,192},{64,0},{128,64},{192,128},{1,193},{65,1},{129,65},{193,129... | collective-permute-start | bytes 1572872 | tf_op jit(solution)/shard_map/ppermute | solution.py:15
  49.5 0.0 collective-permute-done.4
  49.5 0.1 add_convert_fusion.1
  49.7 0.1 collective-permute-start.5
  49.8 10.7 %collective-permute-done.6.upb = bf16[16,128,128]{2,1,0:T(8,128)(2,1)S(1)} collective-permute-done((bf16[16,128,128]{2,1,0:T(8,128)(2,1)S(1)}, bf16[16,128,128]{2,1,0:T(8,128)(2,1)S(1)}, u32[]{:S(2)}, u32[]{:S(2)}) %collective-permute-start.6) | collective-permute-done | bytes 524320 | tf_op jit(solution)/shard_map/ppermute | solution.py:15
  60.4 0.0 collective-permute-done.7.downa
  60.4 7.6 %collective-permute-done.9.downb = bf16[16,128,128]{2,1,0:T(8,128)(2,1)S(1)} collective-permute-done((bf16[16,128,128]{2,1,0:T(8,128)(2,1)S(1)}, bf16[16,128,128]{2,1,0:T(8,128)(2,1)S(1)}, u32[]{:S(2)}, u32[]{:S(2)}) %collective-permute-start.9) | collective-permute-done | bytes 524320 | tf_op jit(solution)/shard_map/ppermute | solution.py:15
  68.0 3.0 %collective-permute-done.5.upa = bf16[16,128,128]{2,1,0:T(8,128)(2,1)S(1)} collective-permute-done((bf16[16,128,128]{2,1,0:T(8,128)(2,1)S(1)}, bf16[16,128,128]{2,1,0:T(8,128)(2,1)S(1)}, u32[]{:S(2)}, u32[]{:S(2)}) %collective-permute-start.5) | collective-permute-done | bytes 524320 | tf_op jit(solution)/shard_map/ppermute | solution.py:15
  71.0 1.2 copy-done.2
  72.2 2.3 %shard_map.115 = (bf16[32,128,128]{2,1,0:T(8,128)(2,1)}, f32[128,128]{1,0:T(8,128)S(1)}) custom-call(bf16[32,128,128]{2,1,0:T(8,128)(2,1)S(1)} %get-tuple-element.11.c0, bf16[16,128,128]{2,1,0:T(8,128)(2,1)S(1)} %collective-permute-done.5.upa, bf16[16,128,128]{2,1,0:T(8,128)(2,1)S(1)} %collective-permute-done.6.upb, ...), custom_call_target="tpu_custom_call" | custom-call | flops 134217728 | bytes 5242880 | tf_op jit(solution)/shard_map/pallas_call | solution.py:108
  74.5 0.0 reduce-scatter.2.cloned.1.call-update
  74.6 0.1 collective-permute-start.10
  74.7 1.2 %collective-permute-done.10 = f32[128,128]{1,0:T(8,128)S(1)} collective-permute-done((f32[128,128]{1,0:T(8,128)S(1)}, f32[128,128]{1,0:T(8,128)S(1)}, u32[]{:S(2)}, u32[]{:S(2)}) %collective-permute-start.10) | collective-permute-done | bytes 65568 | tf_op jit(solution)/shard_map/ppermute | solution.py:149
  75.9 2.9 %collective-permute-start.11 = (f32[128,128]{1,0:T(8,128)S(1)}, f32[128,128]{1,0:T(8,128)S(1)}, u32[]{:S(2)}, u32[]{:S(2)}) collective-permute-start(f32[128,128]{1,0:T(8,128)S(1)} %add.47), channel_id=1, source_target_pairs={{0,2},{2,4},{4,6},{6,0},{1,3},{3,5},{5,7},{7,1},{8,10},{10,12},{12... | collective-permute-start | bytes 196616 | tf_op jit(solution)/shard_map/ppermute | solution.py:15
  78.8 0.4 collective-permute-start.12
  79.2 1.7 %collective-permute-start.13 = (f32[128,128]{1,0:T(8,128)S(1)}, f32[128,128]{1,0:T(8,128)S(1)}, u32[]{:S(2)}, u32[]{:S(2)}) collective-permute-start(f32[128,128]{1,0:T(8,128)S(1)} %add.47), channel_id=1, source_target_pairs={{0,4},{2,6},{4,0},{6,2},{1,5},{3,7},{5,1},{7,3},{8,12},{10,14},{12... | collective-permute-start | bytes 196616 | tf_op jit(solution)/shard_map/ppermute | solution.py:15
  81.0 0.5 collective-permute-done.11
  81.5 1.9 %collective-permute-done.12 = f32[128,128]{1,0:T(8,128)S(1)} collective-permute-done((f32[128,128]{1,0:T(8,128)S(1)}, f32[128,128]{1,0:T(8,128)S(1)}, u32[]{:S(2)}, u32[]{:S(2)}) %collective-permute-start.12) | collective-permute-done | bytes 65568 | tf_op jit(solution)/shard_map/ppermute | solution.py:15
  83.4 1.6 %collective-permute-done.13 = f32[128,128]{1,0:T(8,128)S(1)} collective-permute-done((f32[128,128]{1,0:T(8,128)S(1)}, f32[128,128]{1,0:T(8,128)S(1)}, u32[]{:S(2)}, u32[]{:S(2)}) %collective-permute-start.13) | collective-permute-done | bytes 65568 | tf_op jit(solution)/shard_map/ppermute | solution.py:15
  85.0 0.1 collective-permute-start.14
  85.1 3.2 %collective-permute-start.15 = (f32[128,128]{1,0:T(8,128)S(1)}, f32[128,128]{1,0:T(8,128)S(1)}, u32[]{:S(2)}, u32[]{:S(2)}) collective-permute-start(f32[128,128]{1,0:T(8,128)S(1)} %add_add_fusion.2), channel_id=1, source_target_pairs={{0,192},{64,0},{128,64},{192,128},{1,193},{65,1},{129,65},{193,129... | collective-permute-start | bytes 196616 | tf_op jit(solution)/shard_map/ppermute | solution.py:15
  88.3 0.0 collective-permute-start.16
  88.3 2.9 %collective-permute-done.14 = f32[128,128]{1,0:T(8,128)S(1)} collective-permute-done((f32[128,128]{1,0:T(8,128)S(1)}, f32[128,128]{1,0:T(8,128)S(1)}, u32[]{:S(2)}, u32[]{:S(2)}) %collective-permute-start.14) | collective-permute-done | bytes 65568 | tf_op jit(solution)/shard_map/ppermute | solution.py:15
  91.3 0.0 collective-permute-done.15
  91.3 2.8 %collective-permute-done.16 = f32[128,128]{1,0:T(8,128)S(1)} collective-permute-done((f32[128,128]{1,0:T(8,128)S(1)}, f32[128,128]{1,0:T(8,128)S(1)}, u32[]{:S(2)}, u32[]{:S(2)}) %collective-permute-start.16) | collective-permute-done | bytes 65568 | tf_op jit(solution)/shard_map/ppermute | solution.py:15
  94.1 1.3 %collective-permute-start.17 = (f32[128,128]{1,0:T(8,128)S(1)}, f32[128,128]{1,0:T(8,128)S(1)}, u32[]{:S(2)}, u32[]{:S(2)}) collective-permute-start(f32[128,128]{1,0:T(8,128)S(1)} %add_add_fusion.1), channel_id=1, source_target_pairs={{0,8},{8,16},{16,24},{24,32},{32,40},{40,48},{48,56},{56,0},{1,9},... | collective-permute-start | bytes 196616 | tf_op jit(solution)/shard_map/ppermute | solution.py:15
  95.4 1.1 collective-permute-start.18
  96.5 3.4 %collective-permute-start.19 = (f32[128,128]{1,0:T(8,128)S(1)}, f32[128,128]{1,0:T(8,128)S(1)}, u32[]{:S(2)}, u32[]{:S(2)}) collective-permute-start(f32[128,128]{1,0:T(8,128)S(1)} %add_add_fusion.1), channel_id=1, source_target_pairs={{0,16},{8,24},{16,32},{24,40},{32,48},{40,56},{48,0},{56,8},{1,17}... | collective-permute-start | bytes 196616 | tf_op jit(solution)/shard_map/ppermute | solution.py:15
  99.9 0.0 collective-permute-done.17
  99.9 0.7 collective-permute-done.18
  100.6 4.8 %collective-permute-done.19 = f32[128,128]{1,0:T(8,128)S(1)} collective-permute-done((f32[128,128]{1,0:T(8,128)S(1)}, f32[128,128]{1,0:T(8,128)S(1)}, u32[]{:S(2)}, u32[]{:S(2)}) %collective-permute-start.19) | collective-permute-done | bytes 65568 | tf_op jit(solution)/shard_map/ppermute | solution.py:15
  105.5 3.7 %collective-permute-start.20 = (f32[128,128]{1,0:T(8,128)S(1)}, f32[128,128]{1,0:T(8,128)S(1)}, u32[]{:S(2)}, u32[]{:S(2)}) collective-permute-start(f32[128,128]{1,0:T(8,128)S(1)} %add_add_fusion), channel_id=1, source_target_pairs={{0,32},{8,40},{16,48},{24,56},{32,0},{40,8},{48,16},{56,24},{1,33}... | collective-permute-start | bytes 196616 | tf_op jit(solution)/shard_map/ppermute | solution.py:15
  109.1 0.0 copy-done.4
  109.1 0.1 copy.13
  109.2 0.1 copy.14
  109.3 5.3 %collective-permute-done.20 = f32[128,128]{1,0:T(8,128)S(1)} collective-permute-done((f32[128,128]{1,0:T(8,128)S(1)}, f32[128,128]{1,0:T(8,128)S(1)}, u32[]{:S(2)}, u32[]{:S(2)}) %collective-permute-start.20) | collective-permute-done | bytes 65568 | tf_op jit(solution)/shard_map/ppermute | solution.py:15
  114.7 0.7 copy.15
  115.4 0.0 copy-done
  115.4 1.8 %convolution_convert_fusion = bf16[4,128,128]{2,1,0:T(8,128)(2,1)} fusion(bf16[4,128,128]{2,1,0:T(8,128)(2,1)} %reduce-scatter.2.cloned.1.call-done, bf16[128,128]{1,0:T(8,128)(2,1)S(1)} %copy-done), kind=kOutput, calls=%fused_computation | convolution fusion | flops 16842752 | bytes 294912 | tf_op jit(solution)/shard_map/qfj,df->qjd/dot_general | solution.py:146
  (15 shorter events, 0.1 us)
Async XLA Ops:
  7.2 108.3 %copy-start = (bf16[128,128]{1,0:T(8,128)(2,1)S(1)}, bf16[128,128]{1,0:T(8,128)(2,1)}, u32[]{:S(2)}) copy-start(bf16[128,128]{1,0:T(8,128)(2,1)} %param.17) | copy-start | bytes 98308
  7.2 63.8 %all-gather.2.cloned.1.call-start = ((), (), s32[]{:S(2)}) async-start(), calls=%async_computation.1 | async-start | bytes 1179648 | tf_op jit(solution)/shard_map/all_gather | solution.py:125
  8.2 6.6 %collective-permute-start = (bf16[16,4096]{1,0:T(8,128)(2,1)S(1)}, bf16[16,4096]{1,0:T(8,128)(2,1)S(1)}, u32[]{:S(2)}, u32[]{:S(2)}) collective-permute-start(bf16[16,4096]{1,0:T(8,128)(2,1)S(1)} %fusion), channel_id=1, source_target_pairs={{0,2},{2,4},{4,6},{6,0},{1,3},{3,5},{5,7},{7,1},{8,10},{10,12},{12... | collective-permute-start | bytes 393224 | tf_op jit(solution)/shard_map/ppermute | solution.py:15
  9.9 7.1 %collective-permute-start.1 = (bf16[16,4096]{1,0:T(8,128)(2,1)S(1)}, bf16[16,4096]{1,0:T(8,128)(2,1)S(1)}, u32[]{:S(2)}, u32[]{:S(2)}) collective-permute-start(bf16[16,4096]{1,0:T(8,128)(2,1)S(1)} %fusion), channel_id=1, source_target_pairs={{0,6},{2,0},{4,2},{6,4},{1,7},{3,1},{5,3},{7,5},{8,14},{10,8},{12,... | collective-permute-start | bytes 393224 | tf_op jit(solution)/shard_map/ppermute | solution.py:15
  11.6 7.3 %collective-permute-start.2 = (bf16[16,4096]{1,0:T(8,128)(2,1)S(1)}, bf16[16,4096]{1,0:T(8,128)(2,1)S(1)}, u32[]{:S(2)}, u32[]{:S(2)}) collective-permute-start(bf16[16,4096]{1,0:T(8,128)(2,1)S(1)} %fusion), channel_id=1, source_target_pairs={{0,4},{2,6},{4,0},{6,2},{1,5},{3,7},{5,1},{7,3},{8,12},{10,14},{12... | collective-permute-start | bytes 393224 | tf_op jit(solution)/shard_map/ppermute | solution.py:15
  13.6 101.9 %reduce-scatter.2.cloned.1.call-start = ((), (), s32[]{:S(2)}) async-start(), calls=%async_computation.2 | async-start | bytes 1179648 | tf_op jit(solution)/shard_map/reduce_scatter | solution.py:145
  18.9 4.8 %collective-permute-start.3 = (bf16[64,4096]{1,0:T(8,128)(2,1)S(1)}, bf16[64,4096]{1,0:T(8,128)(2,1)S(1)}, u32[]{:S(2)}, u32[]{:S(2)}) collective-permute-start(bf16[64,4096]{1,0:T(8,128)(2,1)S(1)} %pad_maximum_fusion.mine), channel_id=1, source_target_pairs={{0,1},{1,0},{2,3},{3,2},{4,5},{5,4},{6,7},{7,6},{8,9},{9,8},{10,11... | collective-permute-start | bytes 1572872 | tf_op jit(solution)/shard_map/ppermute | solution.py:129
  19.7 3.4 %copy-start.1 = (bf16[1,1,256,128,128]{4,3,2,1,0:T(8,128)(2,1)S(1)}, bf16[1,1,256,128,128]{4,3,2,1,0:T(8,128)(2,1)}, u32[]{:S(2)}) copy-start(bf16[1,1,256,128,128]{4,3,2,1,0:T(8,128)(2,1)} %param.10) | copy-start | bytes 25165828
  23.0 0.7 copy-start.3
  23.7 85.4 %copy-start.4 = (f32[128,128]{1,0:T(8,128)S(1)}, f32[128,128]{1,0:T(8,128)}, u32[]{:S(2)}) copy-start(f32[128,128]{1,0:T(8,128)} %param.19) | copy-start | bytes 196612
  23.7 85.5 %copy-start.5 = (f32[128,128]{1,0:T(8,128)S(1)}, f32[128,128]{1,0:T(8,128)}, u32[]{:S(2)}) copy-start(f32[128,128]{1,0:T(8,128)} %param.18) | copy-start | bytes 196612
  31.6 14.9 %collective-permute-start.8 = (bf16[16,128,128]{2,1,0:T(8,128)(2,1)S(1)}, bf16[16,128,128]{2,1,0:T(8,128)(2,1)S(1)}, u32[]{:S(2)}, u32[]{:S(2)}) collective-permute-start(bf16[16,128,128]{2,1,0:T(8,128)(2,1)S(1)} %get-tuple-element.17), channel_id=1, source_target_pairs={{0,192},{64,0},{128,64},{192,128},{1,193},{65,1},{129,65},{193,129... | collective-permute-start | bytes 1572872 | tf_op jit(solution)/shard_map/ppermute | solution.py:15
  33.2 16.3 %collective-permute-start.4 = (bf16[16,128,128]{2,1,0:T(8,128)(2,1)S(1)}, bf16[16,128,128]{2,1,0:T(8,128)(2,1)S(1)}, u32[]{:S(2)}, u32[]{:S(2)}) collective-permute-start(bf16[16,128,128]{2,1,0:T(8,128)(2,1)S(1)} %get-tuple-element.13), channel_id=1, source_target_pairs={{0,64},{64,128},{128,192},{192,0},{1,65},{65,129},{129,193},{193,1... | collective-permute-start | bytes 1572872 | tf_op jit(solution)/shard_map/ppermute | solution.py:15
  33.7 26.7 %collective-permute-start.6 = (bf16[16,128,128]{2,1,0:T(8,128)(2,1)S(1)}, bf16[16,128,128]{2,1,0:T(8,128)(2,1)S(1)}, u32[]{:S(2)}, u32[]{:S(2)}) collective-permute-start(bf16[16,128,128]{2,1,0:T(8,128)(2,1)S(1)} %get-tuple-element.14), channel_id=1, source_target_pairs={{0,64},{64,128},{128,192},{192,0},{1,65},{65,129},{129,193},{193,1... | collective-permute-start | bytes 1572872 | tf_op jit(solution)/shard_map/ppermute | solution.py:15
  34.7 25.7 %collective-permute-start.7 = (bf16[16,128,128]{2,1,0:T(8,128)(2,1)S(1)}, bf16[16,128,128]{2,1,0:T(8,128)(2,1)S(1)}, u32[]{:S(2)}, u32[]{:S(2)}) collective-permute-start(bf16[16,128,128]{2,1,0:T(8,128)(2,1)S(1)} %get-tuple-element.15), channel_id=1, source_target_pairs={{0,192},{64,0},{128,64},{192,128},{1,193},{65,1},{129,65},{193,129... | collective-permute-start | bytes 1572872 | tf_op jit(solution)/shard_map/ppermute | solution.py:15
  46.6 21.4 %collective-permute-start.9 = (bf16[16,128,128]{2,1,0:T(8,128)(2,1)S(1)}, bf16[16,128,128]{2,1,0:T(8,128)(2,1)S(1)}, u32[]{:S(2)}, u32[]{:S(2)}) collective-permute-start(bf16[16,128,128]{2,1,0:T(8,128)(2,1)S(1)} %add_convert_fusion), channel_id=1, source_target_pairs={{0,192},{64,0},{128,64},{192,128},{1,193},{65,1},{129,65},{193,129... | collective-permute-start | bytes 1572872 | tf_op jit(solution)/shard_map/ppermute | solution.py:15
  49.7 21.3 %collective-permute-start.5 = (bf16[16,128,128]{2,1,0:T(8,128)(2,1)S(1)}, bf16[16,128,128]{2,1,0:T(8,128)(2,1)S(1)}, u32[]{:S(2)}, u32[]{:S(2)}) collective-permute-start(bf16[16,128,128]{2,1,0:T(8,128)(2,1)S(1)} %add_convert_fusion.1), channel_id=1, source_target_pairs={{0,64},{64,128},{128,192},{192,0},{1,65},{65,129},{129,193},{193,1... | collective-permute-start | bytes 1572872 | tf_op jit(solution)/shard_map/ppermute | solution.py:15
  71.0 1.2 copy-start.2
  74.6 1.3 %collective-permute-start.10 = (f32[128,128]{1,0:T(8,128)S(1)}, f32[128,128]{1,0:T(8,128)S(1)}, u32[]{:S(2)}, u32[]{:S(2)}) collective-permute-start(f32[128,128]{1,0:T(8,128)S(1)} %get-tuple-element.19), channel_id=1, source_target_pairs={{0,1},{1,0},{2,3},{3,2},{4,5},{5,4},{6,7},{7,6},{8,9},{9,8},{10,11... | collective-permute-start | bytes 196616 | tf_op jit(solution)/shard_map/ppermute | solution.py:149
  75.9 5.6 %collective-permute-start.11 = (f32[128,128]{1,0:T(8,128)S(1)}, f32[128,128]{1,0:T(8,128)S(1)}, u32[]{:S(2)}, u32[]{:S(2)}) collective-permute-start(f32[128,128]{1,0:T(8,128)S(1)} %add.47), channel_id=1, source_target_pairs={{0,2},{2,4},{4,6},{6,0},{1,3},{3,5},{5,7},{7,1},{8,10},{10,12},{12... | collective-permute-start | bytes 196616 | tf_op jit(solution)/shard_map/ppermute | solution.py:15
  78.8 4.6 %collective-permute-start.12 = (f32[128,128]{1,0:T(8,128)S(1)}, f32[128,128]{1,0:T(8,128)S(1)}, u32[]{:S(2)}, u32[]{:S(2)}) collective-permute-start(f32[128,128]{1,0:T(8,128)S(1)} %add.47), channel_id=1, source_target_pairs={{0,6},{2,0},{4,2},{6,4},{1,7},{3,1},{5,3},{7,5},{8,14},{10,8},{12,... | collective-permute-start | bytes 196616 | tf_op jit(solution)/shard_map/ppermute | solution.py:15
  79.2 5.8 %collective-permute-start.13 = (f32[128,128]{1,0:T(8,128)S(1)}, f32[128,128]{1,0:T(8,128)S(1)}, u32[]{:S(2)}, u32[]{:S(2)}) collective-permute-start(f32[128,128]{1,0:T(8,128)S(1)} %add.47), channel_id=1, source_target_pairs={{0,4},{2,6},{4,0},{6,2},{1,5},{3,7},{5,1},{7,3},{8,12},{10,14},{12... | collective-permute-start | bytes 196616 | tf_op jit(solution)/shard_map/ppermute | solution.py:15
  85.0 6.3 %collective-permute-start.14 = (f32[128,128]{1,0:T(8,128)S(1)}, f32[128,128]{1,0:T(8,128)S(1)}, u32[]{:S(2)}, u32[]{:S(2)}) collective-permute-start(f32[128,128]{1,0:T(8,128)S(1)} %add_add_fusion.2), channel_id=1, source_target_pairs={{0,64},{64,128},{128,192},{192,0},{1,65},{65,129},{129,193},{193,1... | collective-permute-start | bytes 196616 | tf_op jit(solution)/shard_map/ppermute | solution.py:15
  85.1 6.2 %collective-permute-start.15 = (f32[128,128]{1,0:T(8,128)S(1)}, f32[128,128]{1,0:T(8,128)S(1)}, u32[]{:S(2)}, u32[]{:S(2)}) collective-permute-start(f32[128,128]{1,0:T(8,128)S(1)} %add_add_fusion.2), channel_id=1, source_target_pairs={{0,192},{64,0},{128,64},{192,128},{1,193},{65,1},{129,65},{193,129... | collective-permute-start | bytes 196616 | tf_op jit(solution)/shard_map/ppermute | solution.py:15
  88.3 5.8 %collective-permute-start.16 = (f32[128,128]{1,0:T(8,128)S(1)}, f32[128,128]{1,0:T(8,128)S(1)}, u32[]{:S(2)}, u32[]{:S(2)}) collective-permute-start(f32[128,128]{1,0:T(8,128)S(1)} %add_add_fusion.2), channel_id=1, source_target_pairs={{0,128},{64,192},{128,0},{192,64},{1,129},{65,193},{129,1},{193,65... | collective-permute-start | bytes 196616 | tf_op jit(solution)/shard_map/ppermute | solution.py:15
  94.1 5.8 %collective-permute-start.17 = (f32[128,128]{1,0:T(8,128)S(1)}, f32[128,128]{1,0:T(8,128)S(1)}, u32[]{:S(2)}, u32[]{:S(2)}) collective-permute-start(f32[128,128]{1,0:T(8,128)S(1)} %add_add_fusion.1), channel_id=1, source_target_pairs={{0,8},{8,16},{16,24},{24,32},{32,40},{40,48},{48,56},{56,0},{1,9},... | collective-permute-start | bytes 196616 | tf_op jit(solution)/shard_map/ppermute | solution.py:15
  95.4 5.2 %collective-permute-start.18 = (f32[128,128]{1,0:T(8,128)S(1)}, f32[128,128]{1,0:T(8,128)S(1)}, u32[]{:S(2)}, u32[]{:S(2)}) collective-permute-start(f32[128,128]{1,0:T(8,128)S(1)} %add_add_fusion.1), channel_id=1, source_target_pairs={{0,56},{8,0},{16,8},{24,16},{32,24},{40,32},{48,40},{56,48},{1,57}... | collective-permute-start | bytes 196616 | tf_op jit(solution)/shard_map/ppermute | solution.py:15
  96.5 8.9 %collective-permute-start.19 = (f32[128,128]{1,0:T(8,128)S(1)}, f32[128,128]{1,0:T(8,128)S(1)}, u32[]{:S(2)}, u32[]{:S(2)}) collective-permute-start(f32[128,128]{1,0:T(8,128)S(1)} %add_add_fusion.1), channel_id=1, source_target_pairs={{0,16},{8,24},{16,32},{24,40},{32,48},{40,56},{48,0},{56,8},{1,17}... | collective-permute-start | bytes 196616 | tf_op jit(solution)/shard_map/ppermute | solution.py:15
  105.5 9.2 %collective-permute-start.20 = (f32[128,128]{1,0:T(8,128)S(1)}, f32[128,128]{1,0:T(8,128)S(1)}, u32[]{:S(2)}, u32[]{:S(2)}) collective-permute-start(f32[128,128]{1,0:T(8,128)S(1)} %add_add_fusion), channel_id=1, source_target_pairs={{0,32},{8,40},{16,48},{24,56},{32,0},{40,8},{48,16},{56,24},{1,33}... | collective-permute-start | bytes 196616 | tf_op jit(solution)/shard_map/ppermute | solution.py:15
Sparse Core Ops, SparseCore 0:
  13.7 38.9 all-gather.1
  74.7 38.8 reduce-scatter.1

commit v3 on v2

v3 whole, which is shorter than its diff:
```python
import jax
import jax.numpy as jnp
from jax import lax
from jax.experimental import pallas as pl
from jax.experimental.pallas import tpu as pltpu
from jax.sharding import Mesh, PartitionSpec as P

XS, ZS, YS, CS = 4, 8, 4, 2
T = 128
GROUP = 32
F32, BF16 = jnp.float32, jnp.bfloat16


def shift(value, axis, size, by):
    return lax.ppermute(value, axis, [(i, (i + by) % size) for i in range(size)])


def swap(value):
    return lax.ppermute(value, "core", [(0, 1), (1, 0)])


def spread(value, axis, size, dists, core):
    total = jnp.where(core == 0, value, jnp.zeros_like(value))
    for by in dists:
        pairs = [
            (i * CS + c, (i + d) % size * CS + c) for c, d in enumerate(by) if d is not None for i in range(size)
        ]
        total = total + lax.ppermute(value, (axis, "core"), pairs)
    return total


def fetch_kernel(source, target, sem):
    copy = pltpu.make_async_copy(source, target, sem)
    copy.start()
    copy.wait()


def fetch(array):
    return pl.pallas_call(
        fetch_kernel,
        in_specs=[pl.BlockSpec(memory_space=pl.ANY)],
        out_specs=pl.BlockSpec(memory_space=pltpu.VMEM),
        out_shape=jax.ShapeDtypeStruct(array.shape, array.dtype),
        scratch_shapes=[pltpu.SemaphoreType.DMA],
        compiler_params=pltpu.CompilerParams(vmem_limit_bytes=12 * 2**20),
        cost_estimate=pl.CostEstimate(flops=0, bytes_accessed=2 * array.size, transcendentals=0),
    )(array)


DISTS = (2, 1, 3)
PLACED = ((64, 16), (80, 16), (48, 16), (96, 16), (32, 16), (112, 16), (0, 32))


def tile_kernel(codes, meta, source, mine, other, *rest):
    outs, (tiles, wide, acc, sems) = rest[:7], rest[7:]
    steps = source.shape[0] // GROUP

    def chunk(g):
        at = pl.ds(pl.multiple_of(g * GROUP, GROUP), GROUP)
        return pltpu.make_async_copy(source.at[at], tiles.at[at], sems.at[g])

    for g in range(steps):
        chunk(g).start()
    for part, dist in enumerate((0,) + DISTS):
        y_of = (meta[1] - dist) & (YS - 1)
        for ref, core in ((mine, meta[2]), (other, 1 - meta[2])):
            at = pl.multiple_of((y_of * CS + core) * 16, 16)
            wide[pl.ds(at, 16), :] = ref[part * 16 : part * 16 + 16, :]

    def clear(i, _):
        acc[pl.ds(i * 4, 4)] = jnp.zeros((4, T, T), F32)
        return 0

    lax.fori_loop(0, 32, clear, 0)

    def several(g, _):
        chunk(g).wait()

        @pl.when(g * GROUP < meta[0])
        def _():
            base = g * GROUP
            products = []
            for u in range(GROUP):
                at = pl.multiple_of((codes[base + u] >> 8) * T, T)
                products.append(
                    jnp.dot(wide[:, pl.ds(at, T)], tiles[base + u], preferred_element_type=F32)
                )
            for u in range(GROUP):
                place = codes[base + u] & 255
                acc[place] = acc[place] + products[u]

        return 0

    lax.fori_loop(0, steps, several, 0)

    for out, (first, size) in zip(outs, PLACED):

        def put(i, _):
            out[pl.ds(i * 4, 4)] = acc[pl.ds(first + i * 4, 4)].astype(BF16)
            return 0

        lax.fori_loop(0, size // 4, put, 0)


def tile_products(codes, meta, tiles, mine, other):
    smem, vmem = pl.BlockSpec(memory_space=pltpu.SMEM), pl.BlockSpec(memory_space=pltpu.VMEM)
    return pl.pallas_call(
        tile_kernel,
        in_specs=[smem] * 2 + [pl.BlockSpec(memory_space=pl.ANY)] + [vmem] * 2,
        out_specs=[vmem] * 7,
        scratch_shapes=[
            pltpu.VMEM(tiles.shape, BF16),
            pltpu.VMEM((T, mine.shape[1]), BF16),
            pltpu.VMEM((129, T, T), F32),
            pltpu.SemaphoreType.DMA((tiles.shape[0] // GROUP,)),
        ],
        out_shape=[jax.ShapeDtypeStruct((n, T, T), BF16) for _, n in PLACED],
        compiler_params=pltpu.CompilerParams(vmem_limit_bytes=50 * 2**20),
        cost_estimate=pl.CostEstimate(flops=2**30, bytes_accessed=13 * 2**20, transcendentals=0),
    )(codes, meta, tiles, mine, other)


def middle_kernel(c0, upa, upb, downa, downb, feats, out, grad, sums):
    sums[...] = jnp.zeros((T, T), F32)
    for first, up, down in ((0, upa, downa), (16, upb, downb)):

        def several(i, _):
            total = sums[...]
            for u in range(4):
                n, k = i * 4 + u, first + i * 4 + u
                value = (c0[k].astype(F32) + up[n].astype(F32) + down[n].astype(F32)).astype(BF16)
                out[k] = value
                total += jnp.dot(value, feats[k], preferred_element_type=F32)
            sums[...] = total
            return 0

        lax.fori_loop(0, 4, several, 0)
    grad[...] = sums[...].T


def middle(*operands):
    spec = pl.BlockSpec(memory_space=pltpu.VMEM)
    return pl.pallas_call(
        middle_kernel,
        in_specs=[spec] * 6,
        out_specs=[spec] * 2,
        out_shape=[jax.ShapeDtypeStruct((32, T, T), BF16), jax.ShapeDtypeStruct((T, T), F32)],
        scratch_shapes=[pltpu.VMEM((T, T), F32)],
        compiler_params=pltpu.CompilerParams(vmem_limit_bytes=12 * 2**20),
        cost_estimate=pl.CostEstimate(flops=2**27, bytes_accessed=5 * 2**20, transcendentals=0),
    )(*operands)


def last_kernel(aggregate, weight, grad, more, importance, delta, input_grad, importance_out):
    for q in range(4):
        product = jnp.dot(weight[...], aggregate[q], preferred_element_type=F32)
        input_grad[q * T : q * T + T, :] = product.T.astype(BF16)
    importance_out[...] = importance[...] - (grad[...] + more[...]) * delta[...]


def last(*operands):
    spec = pl.BlockSpec(memory_space=pltpu.VMEM)
    return pl.pallas_call(
        last_kernel,
        in_specs=[spec] * 6,
        out_specs=[spec] * 2,
        out_shape=[jax.ShapeDtypeStruct((4 * T, T), BF16), jax.ShapeDtypeStruct((T, T), F32)],
        compiler_params=pltpu.CompilerParams(vmem_limit_bytes=4 * 2**20),
        cost_estimate=pl.CostEstimate(flops=2**24, bytes_accessed=2**19, transcendentals=0),
    )(*operands)


def add(*values):
    return sum(v.astype(F32) for v in values).astype(BF16)


def local(tile_vals, tile_row, tile_col, tile_count, out_grad, relu_mask, features, weight, importance, weight_delta):
    x, y, core = (lax.axis_index(a) for a in ("x", "y", "core"))
    slots = tile_vals.shape[2]
    wide_feats = lax.all_gather(features, "z", axis=0, tiled=True).reshape(ZS * 4, T, T)

    masked = (out_grad.astype(F32) * relu_mask.astype(F32)).astype(BF16).T
    mine = jnp.concatenate([masked] + [shift(masked, "y", YS, d) for d in DISTS], axis=0)
    other = swap(mine)

    count = tile_count.reshape(())
    cols = tile_col.reshape(slots)
    dest = cols >> 2
    dx = ((dest >> 3) - x) & (XS - 1)
    places = jnp.where(lax.iota(jnp.int32, slots) < count, dx * 32 + (cols & 31), 128)
    codes = tile_row.reshape(slots) * 256 + places
    meta = jnp.stack([count, y, core]).astype(jnp.int32)
    tiles = tile_vals.reshape(slots, T, T)
    c2a, c2b, c1b, c3a, c1a, c3b, c0 = tile_products(codes, meta, tiles, mine, other)

    up, down = shift(c2a, "x", XS, 1), shift(c2b, "x", XS, 3)
    upb, downa = shift(c1b, "x", XS, 1), shift(c3a, "x", XS, 3)
    upa, downb = shift(add(c1a, up), "x", XS, 1), shift(add(c3b, down), "x", XS, 3)
    reduced, grad = middle(c0, upa, upb, downa, downb, fetch(wide_feats))

    aggregate = lax.psum_scatter(reduced, "z", scatter_dimension=0, tiled=True)

    grad = grad + swap(grad)
    grad = grad + shift(grad, "y", YS, 2) + shift(grad, "y", YS, 1) + shift(grad, "y", YS, 3)
    grad = grad + shift(grad, "x", XS, 2) + shift(grad, "x", XS, 1) + shift(grad, "x", XS, 3)
    grad = spread(grad, "z", ZS, ((4, None), (3, 5), (2, 6), (1, 7)), core)
    return last(aggregate, weight, grad, swap(grad), importance, weight_delta)


def solution(mesh):
    mesh = Mesh(mesh.devices.reshape(XS, ZS, YS, CS), ("x", "z", "y", "core"))
    row, col = ("x", "z"), ("y", "core")
    return jax.shard_map(
        local,
        mesh=mesh,
        in_specs=(
            P(row, col, None, None, None),
            P(row, col, None),
            P(row, col, None),
            P(row, col),
            P(row, col),
            P(row, col),
            P(row + col, None),
            P(),
            P(),
            P(),
        ),
        out_specs=(P(row + col, None), P()),
        check_vma=False,
    )
```

time: 125 us -> 124 us (level)
  starting transfers between devices: 31.7 us -> 37.7 us
  waiting for transfers between devices: 57.2 us -> 53.3 us
  other arithmetic: 2.18 us -> 4.44 us
  matrix products: 1.77 us -> 0 us
  Pallas kernels: 10.8 us -> 9.4 us
  local copies, waits for them, and re-layouts: 5.55 us -> 4.16 us
    ppermute x19 -> x15, waiting for transfers between devices: 56 us -> 32.7 us  [shift(): lax.ppermute(value, axis, [(i, (i + by) % size) for i in range(size)])]
    ppermute x2 -> x7, starting transfers between devices: 0.19 us -> 11.3 us  [the longest x4 11 us: spread(): total = total + lax.ppermute(value, (axis, 'core'), pairs)]
    ppermute x2 -> x7, waiting for transfers between devices: 1.24 us -> 11.8 us  [the longest x4 8.22 us: spread(): total = total + lax.ppermute(value, (axis, 'core'), pairs)]
    reduce_scatter x1, waiting for transfers between devices: 0.01 us -> 5.77 us  [local(): aggregate = lax.psum_scatter(reduced, 'z', scatter_dimension=0, tiled=True)]
    ppermute x19 -> x15, starting transfers between devices: 31.4 us -> 26.3 us  [shift(): lax.ppermute(value, axis, [(i, (i + by) % size) for i in range(size)])]
    all_gather x1, waiting for transfers between devices: 0.01 us -> 2.9 us  [local(): lax.all_gather(features, 'z', axis=0, tiled=True).reshape(ZS * 4, T, T)]
    dot_general x1 -> x0, matrix products: 1.77 us -> none  [local(): jnp.einsum('qfj,df->qjd', aggregate, weight, preferred_element_type=F32)]
    convert_element_type x2, other arithmetic: 0.28 us -> 1.87 us  [add(): return sum((v.astype(F32) for v in values)).astype(BF16)]
  transfers between devices with their start and end apart: 23 -> 24, of which waited for: 16 -> 18; matrix products, arithmetic and copies ran while one was open for 2% -> 3% of each run, Pallas kernels for 7% -> 5%
where the time goes in v3:
time: 124 us
  waiting for transfers between devices  53.3 us (43%)
  starting transfers between devices  37.7 us (30%)
  between operations  14.8 us (12%)
  Pallas kernels  9.4 us (8%)
  other arithmetic  4.44 us (4%)
  local copies, waits for them, and re-layouts  4.16 us (3%)
    ppermute x15, waiting for transfers between devices, shift(): lax.ppermute(value, axis, [(i, (i + by) % size) for i in range(size)])  32.7 us
    ppermute x15, starting transfers between devices, shift(): lax.ppermute(value, axis, [(i, (i + by) % size) for i in range(size)])  26.3 us
    ppermute x4, starting transfers between devices, spread(): total = total + lax.ppermute(value, (axis, 'core'), pairs)  11 us
    ppermute x4, waiting for transfers between devices, spread(): total = total + lax.ppermute(value, (axis, 'core'), pairs)  8.22 us
    pallas_call x1, Pallas kernels, tile_products(): pl.pallas_call(tile_kernel, in_specs=[smem] * 2 + [pl.BlockSpec(memory_sp...  6.05 us
    reduce_scatter x1, waiting for transfers between devices, local(): aggregate = lax.psum_scatter(reduced, 'z', scatter_dimension=0, tiled=True)  5.77 us
    unnamed x14, local copies, waits for them, and re-layouts  4.16 us
    ppermute x3, waiting for transfers between devices, swap(): return lax.ppermute(value, 'core', [(0, 1), (1, 0)])  3.61 us
  transfers between devices with their start and end apart: 24, of which 18 were waited for; matrix products, arithmetic and copies ran while one was open for 3% of the time, Pallas kernels for 5%

profile of v3, /device:TPU:32, one launch (start us, length us, event | category | flops | bytes accessed | tf_op | source)
XLA Modules:
  0.0 123.8 jit_solution(1897803931769105728)
XLA Ops:
  7.2 0.0 all-gather.2.cloned.1.call-start
  7.2 1.0 fusion
  8.2 3.3 %collective-permute-start = (bf16[16,4096]{1,0:T(8,128)(2,1)S(1)}, bf16[16,4096]{1,0:T(8,128)(2,1)S(1)}, u32[]{:S(2)}, u32[]{:S(2)}) collective-permute-start(bf16[16,4096]{1,0:T(8,128)(2,1)S(1)} %fusion), channel_id=1, source_target_pairs={{0,4},{2,6},{4,0},{6,2},{1,5},{3,7},{5,1},{7,3},{8,12},{10,14},{12... | collective-permute-start | bytes 393224 | tf_op jit(solution)/shard_map/ppermute | solution.py:15
  11.5 0.7 collective-permute-start.1
  12.2 2.6 %collective-permute-start.2 = (bf16[16,4096]{1,0:T(8,128)(2,1)S(1)}, bf16[16,4096]{1,0:T(8,128)(2,1)S(1)}, u32[]{:S(2)}, u32[]{:S(2)}) collective-permute-start(bf16[16,4096]{1,0:T(8,128)(2,1)S(1)} %fusion), channel_id=1, source_target_pairs={{0,6},{2,0},{4,2},{6,4},{1,7},{3,1},{5,3},{7,5},{8,14},{10,8},{12,... | collective-permute-start | bytes 393224 | tf_op jit(solution)/shard_map/ppermute | solution.py:15
  14.7 0.0 all-gather.2.cloned.1.call-update
  14.8 0.0 reduce-scatter.2.cloned.1.call-start
  15.5 0.7 broadcast_multiply_fusion
  16.2 0.0 collective-permute-done
  16.2 2.1 %collective-permute-done.1 = bf16[16,4096]{1,0:T(8,128)(2,1)S(1)} collective-permute-done((bf16[16,4096]{1,0:T(8,128)(2,1)S(1)}, bf16[16,4096]{1,0:T(8,128)(2,1)S(1)}, u32[]{:S(2)}, u32[]{:S(2)}) %collective-permute-start.1) | collective-permute-done | bytes 131104 | tf_op jit(solution)/shard_map/ppermute | solution.py:15
  18.2 0.0 collective-permute-done.2
  18.3 0.1 collective-permute-start.3
  18.4 0.7 multiply_add_fusion
  19.1 0.1 pad_add_fusion.meta
  19.2 1.1 collective-permute-done.3.other
  20.3 0.8 copy-done.6
  21.1 6.0 %shard_map.113 = (bf16[16,128,128]{2,1,0:T(8,128)(2,1)S(1)}, bf16[16,128,128]{2,1,0:T(8,128)(2,1)S(1)}, bf16[16,128,128]{2,1,0:T(8,128)(2,1)S(1)}, bf16[16,128,1...) custom-call(s32[256]{0:T(256)S(1)} %fusion.1.codes, ...), custom_call_target="tpu_custom_call" | custom-call | flops 1073741824 | bytes 13631488 | tf_op jit(solution)/shard_map/pallas_call | solution.py:107
  27.1 4.9 %collective-permute-start.8 = (bf16[16,128,128]{2,1,0:T(8,128)(2,1)S(1)}, bf16[16,128,128]{2,1,0:T(8,128)(2,1)S(1)}, u32[]{:S(2)}, u32[]{:S(2)}) collective-permute-start(bf16[16,128,128]{2,1,0:T(8,128)(2,1)S(1)} %get-tuple-element.17), channel_id=1, source_target_pairs={{0,192},{64,0},{128,64},{192,128},{1,193},{65,1},{129,65},{193,129... | collective-permute-start | bytes 1572872 | tf_op jit(solution)/shard_map/ppermute | solution.py:15
  32.1 0.0 collective-permute-start.4
  32.1 0.2 collective-permute-start.6
  32.3 3.0 %collective-permute-start.7 = (bf16[16,128,128]{2,1,0:T(8,128)(2,1)S(1)}, bf16[16,128,128]{2,1,0:T(8,128)(2,1)S(1)}, u32[]{:S(2)}, u32[]{:S(2)}) collective-permute-start(bf16[16,128,128]{2,1,0:T(8,128)(2,1)S(1)} %get-tuple-element.15), channel_id=1, source_target_pairs={{0,192},{64,0},{128,64},{192,128},{1,193},{65,1},{129,65},{193,129... | collective-permute-start | bytes 1572872 | tf_op jit(solution)/shard_map/ppermute | solution.py:15
  35.3 9.1 %collective-permute-done.8 = bf16[16,128,128]{2,1,0:T(8,128)(2,1)S(1)} collective-permute-done((bf16[16,128,128]{2,1,0:T(8,128)(2,1)S(1)}, bf16[16,128,128]{2,1,0:T(8,128)(2,1)S(1)}, u32[]{:S(2)}, u32[]{:S(2)}) %collective-permute-start.8) | collective-permute-done | bytes 524320 | tf_op jit(solution)/shard_map/ppermute | solution.py:15
  44.4 0.9 add_convert_fusion
  45.4 3.7 %collective-permute-start.9 = (bf16[16,128,128]{2,1,0:T(8,128)(2,1)}, bf16[16,128,128]{2,1,0:T(8,128)(2,1)S(1)}, u32[]{:S(2)}, u32[]{:S(2)}) collective-permute-start(bf16[16,128,128]{2,1,0:T(8,128)(2,1)} %add_convert_fusion), channel_id=1, source_target_pairs={{0,192},{64,0},{128,64},{192,128},{1,193},{65,1},{129,65},{193,129... | collective-permute-start | bytes 1572872 | tf_op jit(solution)/shard_map/ppermute | solution.py:15
  49.1 0.0 collective-permute-done.4
  49.1 0.9 add_convert_fusion.1
  50.0 0.0 collective-permute-start.5
  50.0 2.9 %all-gather.2.cloned.1.call-done = bf16[4096,128]{1,0:T(8,128)(2,1)} async-done(((bf16[512,128]{1,0:T(8,128)(2,1)}), bf16[4096,128]{1,0:T(8,128)(2,1)}) %all-gather.2.cloned.1.call-update) | async-done | bytes 1048592 | tf_op jit(solution)/shard_map/all_gather | solution.py:180
  52.9 1.2 copy-done
  54.1 0.1 shard_map.114.feats
  54.2 5.2 %collective-permute-done.6.upb = bf16[16,128,128]{2,1,0:T(8,128)(2,1)S(1)} collective-permute-done((bf16[16,128,128]{2,1,0:T(8,128)(2,1)S(1)}, bf16[16,128,128]{2,1,0:T(8,128)(2,1)S(1)}, u32[]{:S(2)}, u32[]{:S(2)}) %collective-permute-start.6) | collective-permute-done | bytes 524320 | tf_op jit(solution)/shard_map/ppermute | solution.py:15
  59.4 0.0 collective-permute-done.7.downa
  59.4 6.2 %collective-permute-done.9.downb = bf16[16,128,128]{2,1,0:T(8,128)(2,1)S(1)} collective-permute-done((bf16[16,128,128]{2,1,0:T(8,128)(2,1)}, bf16[16,128,128]{2,1,0:T(8,128)(2,1)S(1)}, u32[]{:S(2)}, u32[]{:S(2)}) %collective-permute-start.9) | collective-permute-done | bytes 524320 | tf_op jit(solution)/shard_map/ppermute | solution.py:15
  65.6 3.3 %collective-permute-done.5.upa = bf16[16,128,128]{2,1,0:T(8,128)(2,1)S(1)} collective-permute-done((bf16[16,128,128]{2,1,0:T(8,128)(2,1)}, bf16[16,128,128]{2,1,0:T(8,128)(2,1)S(1)}, u32[]{:S(2)}, u32[]{:S(2)}) %collective-permute-start.5) | collective-permute-done | bytes 524320 | tf_op jit(solution)/shard_map/ppermute | solution.py:15
  68.9 1.2 copy-done.1
  70.1 2.4 %shard_map.115 = (bf16[32,128,128]{2,1,0:T(8,128)(2,1)}, f32[128,128]{1,0:T(8,128)S(1)}) custom-call(bf16[32,128,128]{2,1,0:T(8,128)(2,1)S(1)} %copy-done.1, bf16[16,128,128]{2,1,0:T(8,128)(2,1)S(1)} %collective-permute-done.5.upa, bf16[16,128,128]{2,1,0:T(8,128)(2,1)S(1)} %collective-permute-done.6.upb, ...), custom_call_target="tpu_custom_call" | custom-call | flops 134217728 | bytes 5242880 | tf_op jit(solution)/shard_map/pallas_call | solution.py:143
  72.5 0.0 reduce-scatter.2.cloned.1.call-update
  72.5 0.1 collective-permute-start.10
  72.6 1.2 %collective-permute-done.10 = f32[128,128]{1,0:T(8,128)S(1)} collective-permute-done((f32[128,128]{1,0:T(8,128)S(1)}, f32[128,128]{1,0:T(8,128)S(1)}, u32[]{:S(2)}, u32[]{:S(2)}) %collective-permute-start.10) | collective-permute-done | bytes 65568 | tf_op jit(solution)/shard_map/ppermute | solution.py:19
  73.9 1.1 collective-permute-start.11
  75.0 2.9 %collective-permute-start.12 = (f32[128,128]{1,0:T(8,128)S(1)}, f32[128,128]{1,0:T(8,128)S(1)}, u32[]{:S(2)}, u32[]{:S(2)}) collective-permute-start(f32[128,128]{1,0:T(8,128)S(1)} %add.51), channel_id=1, source_target_pairs={{0,2},{2,4},{4,6},{6,0},{1,3},{3,5},{5,7},{7,1},{8,10},{10,12},{12... | collective-permute-start | bytes 196616 | tf_op jit(solution)/shard_map/ppermute | solution.py:15
  77.9 0.3 collective-permute-start.13
  78.2 1.9 %collective-permute-done.11 = f32[128,128]{1,0:T(8,128)S(1)} collective-permute-done((f32[128,128]{1,0:T(8,128)S(1)}, f32[128,128]{1,0:T(8,128)S(1)}, u32[]{:S(2)}, u32[]{:S(2)}) %collective-permute-start.11) | collective-permute-done | bytes 65568 | tf_op jit(solution)/shard_map/ppermute | solution.py:15
  80.1 0.9 collective-permute-done.12
  81.0 1.1 collective-permute-done.13
  82.2 0.1 collective-permute-start.14
  82.3 1.1 collective-permute-start.15
  83.4 2.4 %collective-permute-start.16 = (f32[128,128]{1,0:T(8,128)S(1)}, f32[128,128]{1,0:T(8,128)S(1)}, u32[]{:S(2)}, u32[]{:S(2)}) collective-permute-start(f32[128,128]{1,0:T(8,128)S(1)} %add_add_fusion.2), channel_id=1, source_target_pairs={{0,192},{64,0},{128,64},{192,128},{1,193},{65,1},{129,65},{193,129... | collective-permute-start | bytes 196616 | tf_op jit(solution)/shard_map/ppermute | solution.py:15
  85.8 2.4 %collective-permute-done.14 = f32[128,128]{1,0:T(8,128)S(1)} collective-permute-done((f32[128,128]{1,0:T(8,128)S(1)}, f32[128,128]{1,0:T(8,128)S(1)}, u32[]{:S(2)}, u32[]{:S(2)}) %collective-permute-start.14) | collective-permute-done | bytes 65568 | tf_op jit(solution)/shard_map/ppermute | solution.py:15
  88.1 0.6 collective-permute-done.15
  88.7 0.0 collective-permute-done.16
  88.7 8.2 %collective-permute-start.17 = (f32[128,128]{1,0:T(8,128)S(1)}, f32[128,128]{1,0:T(8,128)S(1)}, u32[]{:S(2)}, u32[]{:S(2)}) collective-permute-start(f32[128,128]{1,0:T(8,128)S(1)} %add_add_fusion.1), channel_id=1, source_target_pairs={{0,32},{8,40},{16,48},{24,56},{32,0},{40,8},{48,16},{56,24},{2,34}... | collective-permute-start | bytes 196616 | tf_op jit(solution)/shard_map/ppermute | solution.py:28
  96.9 0.1 collective-permute-start.18
  97.0 1.1 collective-permute-start.19
  98.1 1.7 %collective-permute-start.20 = (f32[128,128]{1,0:T(8,128)S(1)}, f32[128,128]{1,0:T(8,128)S(1)}, u32[]{:S(2)}, u32[]{:S(2)}) collective-permute-start(f32[128,128]{1,0:T(8,128)S(1)} %add_add_fusion.1), channel_id=1, source_target_pairs={{0,8},{8,16},{16,24},{24,32},{32,40},{40,48},{48,56},{56,0},{1,57}... | collective-permute-start | bytes 196616 | tf_op jit(solution)/shard_map/ppermute | solution.py:28
  99.8 2.2 %collective-permute-done.17 = f32[128,128]{1,0:T(8,128)S(1)} collective-permute-done((f32[128,128]{1,0:T(8,128)S(1)}, f32[128,128]{1,0:T(8,128)S(1)}, u32[]{:S(2)}, u32[]{:S(2)}) %collective-permute-start.17) | collective-permute-done | bytes 65568 | tf_op jit(solution)/shard_map/ppermute | solution.py:28
  102.0 3.9 %collective-permute-done.18 = f32[128,128]{1,0:T(8,128)S(1)} collective-permute-done((f32[128,128]{1,0:T(8,128)S(1)}, f32[128,128]{1,0:T(8,128)S(1)}, u32[]{:S(2)}, u32[]{:S(2)}) %collective-permute-start.18) | collective-permute-done | bytes 65568 | tf_op jit(solution)/shard_map/ppermute | solution.py:28
  105.9 2.1 %collective-permute-done.19 = f32[128,128]{1,0:T(8,128)S(1)} collective-permute-done((f32[128,128]{1,0:T(8,128)S(1)}, f32[128,128]{1,0:T(8,128)S(1)}, u32[]{:S(2)}, u32[]{:S(2)}) %collective-permute-start.19) | collective-permute-done | bytes 65568 | tf_op jit(solution)/shard_map/ppermute | solution.py:28
  108.0 0.0 collective-permute-done.20
  108.0 0.1 collective-permute-start.21
  108.1 1.2 %collective-permute-done.21.more = f32[128,128]{1,0:T(8,128)S(1)} collective-permute-done((f32[128,128]{1,0:T(8,128)S(1)}, f32[128,128]{1,0:T(8,128)S(1)}, u32[]{:S(2)}, u32[]{:S(2)}) %collective-permute-start.21) | collective-permute-done | bytes 65568 | tf_op jit(solution)/shard_map/ppermute | solution.py:19
  109.4 5.8 %reduce-scatter.2.cloned.1.call-done.aggregate = bf16[4,128,128]{2,1,0:T(8,128)(2,1)} async-done(((bf16[32,128,128]{2,1,0:T(8,128)(2,1)}), bf16[4,128,128]{2,1,0:T(8,128)(2,1)}) %reduce-scatter.2.cloned.1.call-update) | async-done | bytes 131088 | tf_op jit(solution)/shard_map/reduce_scatter | solution.py:201
  115.1 0.9 copy-done.2
  116.0 0.9 shard_map.116
  (16 shorter events, 0.1 us)
Async XLA Ops:
  7.2 45.7 %all-gather.2.cloned.1.call-start = ((), (), s32[]{:S(2)}) async-start(), calls=%async_computation.1 | async-start | bytes 1179648 | tf_op jit(solution)/shard_map/all_gather | solution.py:180
  8.2 7.9 %collective-permute-start = (bf16[16,4096]{1,0:T(8,128)(2,1)S(1)}, bf16[16,4096]{1,0:T(8,128)(2,1)S(1)}, u32[]{:S(2)}, u32[]{:S(2)}) collective-permute-start(bf16[16,4096]{1,0:T(8,128)(2,1)S(1)} %fusion), channel_id=1, source_target_pairs={{0,4},{2,6},{4,0},{6,2},{1,5},{3,7},{5,1},{7,3},{8,12},{10,14},{12... | collective-permute-start | bytes 393224 | tf_op jit(solution)/shard_map/ppermute | solution.py:15
  11.5 6.7 %collective-permute-start.1 = (bf16[16,4096]{1,0:T(8,128)(2,1)S(1)}, bf16[16,4096]{1,0:T(8,128)(2,1)S(1)}, u32[]{:S(2)}, u32[]{:S(2)}) collective-permute-start(bf16[16,4096]{1,0:T(8,128)(2,1)S(1)} %fusion), channel_id=1, source_target_pairs={{0,2},{2,4},{4,6},{6,0},{1,3},{3,5},{5,7},{7,1},{8,10},{10,12},{12... | collective-permute-start | bytes 393224 | tf_op jit(solution)/shard_map/ppermute | solution.py:15
  12.2 6.1 %collective-permute-start.2 = (bf16[16,4096]{1,0:T(8,128)(2,1)S(1)}, bf16[16,4096]{1,0:T(8,128)(2,1)S(1)}, u32[]{:S(2)}, u32[]{:S(2)}) collective-permute-start(bf16[16,4096]{1,0:T(8,128)(2,1)S(1)} %fusion), channel_id=1, source_target_pairs={{0,6},{2,0},{4,2},{6,4},{1,7},{3,1},{5,3},{7,5},{8,14},{10,8},{12,... | collective-permute-start | bytes 393224 | tf_op jit(solution)/shard_map/ppermute | solution.py:15
  14.8 100.4 %reduce-scatter.2.cloned.1.call-start = ((), (), s32[]{:S(2)}) async-start(), calls=%async_computation.2 | async-start | bytes 1179648 | tf_op jit(solution)/shard_map/reduce_scatter | solution.py:201
  18.3 2.0 %collective-permute-start.3 = (bf16[64,4096]{1,0:T(8,128)(2,1)S(1)}, bf16[64,4096]{1,0:T(8,128)(2,1)S(1)}, u32[]{:S(2)}, u32[]{:S(2)}) collective-permute-start(bf16[64,4096]{1,0:T(8,128)(2,1)S(1)} %pad_maximum_fusion.mine), channel_id=1, source_target_pairs={{0,1},{1,0},{2,3},{3,2},{4,5},{5,4},{6,7},{7,6},{8,9},{9,8},{10,11... | collective-permute-start | bytes 1572872 | tf_op jit(solution)/shard_map/ppermute | solution.py:19
  20.3 0.8 copy-start.6
  21.1 94.0 %copy-start.3 = (f32[128,128]{1,0:T(8,128)S(1)}, f32[128,128]{1,0:T(8,128)}, u32[]{:S(2)}) copy-start(f32[128,128]{1,0:T(8,128)} %importance.1) | copy-start | bytes 196612
  21.1 94.0 %copy-start.4 = (f32[128,128]{1,0:T(8,128)S(1)}, f32[128,128]{1,0:T(8,128)}, u32[]{:S(2)}) copy-start(f32[128,128]{1,0:T(8,128)} %delta.1) | copy-start | bytes 196612
  21.1 94.1 %copy-start.5 = (bf16[128,128]{1,0:T(8,128)(2,1)S(1)}, bf16[128,128]{1,0:T(8,128)(2,1)}, u32[]{:S(2)}) copy-start(bf16[128,128]{1,0:T(8,128)(2,1)} %weight.1) | copy-start | bytes 98308
  27.1 17.3 %collective-permute-start.8 = (bf16[16,128,128]{2,1,0:T(8,128)(2,1)S(1)}, bf16[16,128,128]{2,1,0:T(8,128)(2,1)S(1)}, u32[]{:S(2)}, u32[]{:S(2)}) collective-permute-start(bf16[16,128,128]{2,1,0:T(8,128)(2,1)S(1)} %get-tuple-element.17), channel_id=1, source_target_pairs={{0,192},{64,0},{128,64},{192,128},{1,193},{65,1},{129,65},{193,129... | collective-permute-start | bytes 1572872 | tf_op jit(solution)/shard_map/ppermute | solution.py:15
  32.1 17.0 %collective-permute-start.4 = (bf16[16,128,128]{2,1,0:T(8,128)(2,1)S(1)}, bf16[16,128,128]{2,1,0:T(8,128)(2,1)S(1)}, u32[]{:S(2)}, u32[]{:S(2)}) collective-permute-start(bf16[16,128,128]{2,1,0:T(8,128)(2,1)S(1)} %get-tuple-element.13), channel_id=1, source_target_pairs={{0,64},{64,128},{128,192},{192,0},{1,65},{65,129},{129,193},{193,1... | collective-permute-start | bytes 1572872 | tf_op jit(solution)/shard_map/ppermute | solution.py:15
  32.1 27.3 %collective-permute-start.6 = (bf16[16,128,128]{2,1,0:T(8,128)(2,1)S(1)}, bf16[16,128,128]{2,1,0:T(8,128)(2,1)S(1)}, u32[]{:S(2)}, u32[]{:S(2)}) collective-permute-start(bf16[16,128,128]{2,1,0:T(8,128)(2,1)S(1)} %get-tuple-element.14), channel_id=1, source_target_pairs={{0,64},{64,128},{128,192},{192,0},{1,65},{65,129},{129,193},{193,1... | collective-permute-start | bytes 1572872 | tf_op jit(solution)/shard_map/ppermute | solution.py:15
  32.3 27.1 %collective-permute-start.7 = (bf16[16,128,128]{2,1,0:T(8,128)(2,1)S(1)}, bf16[16,128,128]{2,1,0:T(8,128)(2,1)S(1)}, u32[]{:S(2)}, u32[]{:S(2)}) collective-permute-start(bf16[16,128,128]{2,1,0:T(8,128)(2,1)S(1)} %get-tuple-element.15), channel_id=1, source_target_pairs={{0,192},{64,0},{128,64},{192,128},{1,193},{65,1},{129,65},{193,129... | collective-permute-start | bytes 1572872 | tf_op jit(solution)/shard_map/ppermute | solution.py:15
  45.4 20.2 %collective-permute-start.9 = (bf16[16,128,128]{2,1,0:T(8,128)(2,1)}, bf16[16,128,128]{2,1,0:T(8,128)(2,1)S(1)}, u32[]{:S(2)}, u32[]{:S(2)}) collective-permute-start(bf16[16,128,128]{2,1,0:T(8,128)(2,1)} %add_convert_fusion), channel_id=1, source_target_pairs={{0,192},{64,0},{128,64},{192,128},{1,193},{65,1},{129,65},{193,129... | collective-permute-start | bytes 1572872 | tf_op jit(solution)/shard_map/ppermute | solution.py:15
  50.0 18.9 %collective-permute-start.5 = (bf16[16,128,128]{2,1,0:T(8,128)(2,1)}, bf16[16,128,128]{2,1,0:T(8,128)(2,1)S(1)}, u32[]{:S(2)}, u32[]{:S(2)}) collective-permute-start(bf16[16,128,128]{2,1,0:T(8,128)(2,1)} %add_convert_fusion.1), channel_id=1, source_target_pairs={{0,64},{64,128},{128,192},{192,0},{1,65},{65,129},{129,193},{193,1... | collective-permute-start | bytes 1572872 | tf_op jit(solution)/shard_map/ppermute | solution.py:15
  52.9 1.2 copy-start
  68.9 1.2 copy-start.1
  72.5 1.3 %collective-permute-start.10 = (f32[128,128]{1,0:T(8,128)S(1)}, f32[128,128]{1,0:T(8,128)S(1)}, u32[]{:S(2)}, u32[]{:S(2)}) collective-permute-start(f32[128,128]{1,0:T(8,128)S(1)} %get-tuple-element.19), channel_id=1, source_target_pairs={{0,1},{1,0},{2,3},{3,2},{4,5},{5,4},{6,7},{7,6},{8,9},{9,8},{10,11... | collective-permute-start | bytes 196616 | tf_op jit(solution)/shard_map/ppermute | solution.py:19
  73.9 6.3 %collective-permute-start.11 = (f32[128,128]{1,0:T(8,128)S(1)}, f32[128,128]{1,0:T(8,128)S(1)}, u32[]{:S(2)}, u32[]{:S(2)}) collective-permute-start(f32[128,128]{1,0:T(8,128)S(1)} %add.51), channel_id=1, source_target_pairs={{0,4},{2,6},{4,0},{6,2},{1,5},{3,7},{5,1},{7,3},{8,12},{10,14},{12... | collective-permute-start | bytes 196616 | tf_op jit(solution)/shard_map/ppermute | solution.py:15
  75.0 6.0 %collective-permute-start.12 = (f32[128,128]{1,0:T(8,128)S(1)}, f32[128,128]{1,0:T(8,128)S(1)}, u32[]{:S(2)}, u32[]{:S(2)}) collective-permute-start(f32[128,128]{1,0:T(8,128)S(1)} %add.51), channel_id=1, source_target_pairs={{0,2},{2,4},{4,6},{6,0},{1,3},{3,5},{5,7},{7,1},{8,10},{10,12},{12... | collective-permute-start | bytes 196616 | tf_op jit(solution)/shard_map/ppermute | solution.py:15
  77.9 4.3 %collective-permute-start.13 = (f32[128,128]{1,0:T(8,128)S(1)}, f32[128,128]{1,0:T(8,128)S(1)}, u32[]{:S(2)}, u32[]{:S(2)}) collective-permute-start(f32[128,128]{1,0:T(8,128)S(1)} %add.51), channel_id=1, source_target_pairs={{0,6},{2,0},{4,2},{6,4},{1,7},{3,1},{5,3},{7,5},{8,14},{10,8},{12,... | collective-permute-start | bytes 196616 | tf_op jit(solution)/shard_map/ppermute | solution.py:15
  82.2 6.0 %collective-permute-start.14 = (f32[128,128]{1,0:T(8,128)S(1)}, f32[128,128]{1,0:T(8,128)S(1)}, u32[]{:S(2)}, u32[]{:S(2)}) collective-permute-start(f32[128,128]{1,0:T(8,128)S(1)} %add_add_fusion.2), channel_id=1, source_target_pairs={{0,128},{64,192},{128,0},{192,64},{1,129},{65,193},{129,1},{193,65... | collective-permute-start | bytes 196616 | tf_op jit(solution)/shard_map/ppermute | solution.py:15
  82.3 6.4 %collective-permute-start.15 = (f32[128,128]{1,0:T(8,128)S(1)}, f32[128,128]{1,0:T(8,128)S(1)}, u32[]{:S(2)}, u32[]{:S(2)}) collective-permute-start(f32[128,128]{1,0:T(8,128)S(1)} %add_add_fusion.2), channel_id=1, source_target_pairs={{0,64},{64,128},{128,192},{192,0},{1,65},{65,129},{129,193},{193,1... | collective-permute-start | bytes 196616 | tf_op jit(solution)/shard_map/ppermute | solution.py:15
  83.4 5.3 %collective-permute-start.16 = (f32[128,128]{1,0:T(8,128)S(1)}, f32[128,128]{1,0:T(8,128)S(1)}, u32[]{:S(2)}, u32[]{:S(2)}) collective-permute-start(f32[128,128]{1,0:T(8,128)S(1)} %add_add_fusion.2), channel_id=1, source_target_pairs={{0,192},{64,0},{128,64},{192,128},{1,193},{65,1},{129,65},{193,129... | collective-permute-start | bytes 196616 | tf_op jit(solution)/shard_map/ppermute | solution.py:15
  88.7 13.3 %collective-permute-start.17 = (f32[128,128]{1,0:T(8,128)S(1)}, f32[128,128]{1,0:T(8,128)S(1)}, u32[]{:S(2)}, u32[]{:S(2)}) collective-permute-start(f32[128,128]{1,0:T(8,128)S(1)} %add_add_fusion.1), channel_id=1, source_target_pairs={{0,32},{8,40},{16,48},{24,56},{32,0},{40,8},{48,16},{56,24},{2,34}... | collective-permute-start | bytes 196616 | tf_op jit(solution)/shard_map/ppermute | solution.py:28
  96.9 9.0 %collective-permute-start.18 = (f32[128,128]{1,0:T(8,128)S(1)}, f32[128,128]{1,0:T(8,128)S(1)}, u32[]{:S(2)}, u32[]{:S(2)}) collective-permute-start(f32[128,128]{1,0:T(8,128)S(1)} %add_add_fusion.1), channel_id=1, source_target_pairs={{0,24},{8,32},{16,40},{24,48},{32,56},{40,0},{48,8},{56,16},{1,41}... | collective-permute-start | bytes 196616 | tf_op jit(solution)/shard_map/ppermute | solution.py:28
  97.0 11.0 %collective-permute-start.19 = (f32[128,128]{1,0:T(8,128)S(1)}, f32[128,128]{1,0:T(8,128)S(1)}, u32[]{:S(2)}, u32[]{:S(2)}) collective-permute-start(f32[128,128]{1,0:T(8,128)S(1)} %add_add_fusion.1), channel_id=1, source_target_pairs={{0,16},{8,24},{16,32},{24,40},{32,48},{40,56},{48,0},{56,8},{1,49}... | collective-permute-start | bytes 196616 | tf_op jit(solution)/shard_map/ppermute | solution.py:28
  98.1 9.9 %collective-permute-start.20 = (f32[128,128]{1,0:T(8,128)S(1)}, f32[128,128]{1,0:T(8,128)S(1)}, u32[]{:S(2)}, u32[]{:S(2)}) collective-permute-start(f32[128,128]{1,0:T(8,128)S(1)} %add_add_fusion.1), channel_id=1, source_target_pairs={{0,8},{8,16},{16,24},{24,32},{32,40},{40,48},{48,56},{56,0},{1,57}... | collective-permute-start | bytes 196616 | tf_op jit(solution)/shard_map/ppermute | solution.py:28
  108.0 1.3 %collective-permute-start.21 = (f32[128,128]{1,0:T(8,128)S(1)}, f32[128,128]{1,0:T(8,128)S(1)}, u32[]{:S(2)}, u32[]{:S(2)}) collective-permute-start(f32[128,128]{1,0:T(8,128)S(1)} %add_add_fusion.grad), channel_id=1, source_target_pairs={{0,1},{1,0},{2,3},{3,2},{4,5},{5,4},{6,7},{7,6},{8,9},{9,8},{10,11... | collective-permute-start | bytes 196616 | tf_op jit(solution)/shard_map/ppermute | solution.py:19
  115.1 0.9 copy-start.2
Sparse Core Ops, SparseCore 0:
  14.9 37.9 all-gather.1
  72.6 42.4 reduce-scatter.1

commit v4 on v3

--- a/solution.py
+++ b/solution.py
@@ -1,3 +1,5 @@
+import functools
+
 import jax
 import jax.numpy as jnp
 from jax import lax
@@ -48,52 +50,112 @@
 
 
 DISTS = (2, 1, 3)
-PLACED = ((64, 16), (80, 16), (48, 16), (96, 16), (32, 16), (112, 16), (0, 32))
-
-
-def tile_kernel(codes, meta, source, mine, other, *rest):
-    outs, (tiles, wide, acc, sems) = rest[:7], rest[7:]
-    steps = source.shape[0] // GROUP
-
-    def chunk(g):
-        at = pl.ds(pl.multiple_of(g * GROUP, GROUP), GROUP)
-        return pltpu.make_async_copy(source.at[at], tiles.at[at], sems.at[g])
-
-    for g in range(steps):
-        chunk(g).start()
+CHUNK2 = ((64, 16), (80, 16))
+OTHERS = ((48, 16), (96, 16), (32, 16), (112, 16), (0, 32))
+UNUSED = 128
+
+
+def sort_kernel(rows, cols, count, x, lists):
+    slots = rows.shape[0]
+    second = slots + GROUP
+
+    def some(i, found):
+        a, b = found
+        for u in range(4):
+            t = i * 4 + u
+            col = cols[t]
+            dx = ((col >> 5) - x[0]) & (XS - 1)
+            entry = t * 8192 + rows[t] * 256 + dx * 32 + (col & 31)
+            lists[a] = entry
+            lists[b] = entry
+            used = jnp.where(t < count[0], 1, 0)
+            is_first = jnp.where(dx == 2, used, 0)
+            a = a + is_first
+            b = b + (used - is_first)
+        return a, b
+
+    a, b = lax.fori_loop(0, slots // 4, some, (jnp.int32(0), jnp.int32(second)))
+
+    def fill(i, _):
+        lists[a + i] = UNUSED
+        lists[b + i] = UNUSED
+        return 0
+
+    lax.fori_loop(0, GROUP, fill, 0)
+    lists[2 * second] = a
+    lists[2 * second + 1] = b - second
+
+
+def sort_tiles(*operands):
+    smem = pl.BlockSpec(memory_space=pltpu.SMEM)
+    return pl.pallas_call(
+        sort_kernel,
+        in_specs=[smem] * 4,
+        out_specs=smem,
+        out_shape=jax.ShapeDtypeStruct((2 * (operands[0].shape[0] + GROUP) + 2,), jnp.int32),
+        cost_estimate=pl.CostEstimate(flops=0, bytes_accessed=2**12, transcendentals=0),
+    )(*operands)
+
+
+def join_kernel(token, *refs):
+    for i, ref in enumerate(refs[:-1]):
+        refs[-1][i * 16 : i * 16 + 16, :] = ref[...]
+
+
+def join(token, *parts):
+    spec = pl.BlockSpec(memory_space=pltpu.VMEM)
+    return pl.pallas_call(
+        join_kernel,
+        in_specs=[pl.BlockSpec(memory_space=pltpu.SMEM)] + [spec] * len(parts),
+        out_specs=spec,
+        out_shape=jax.ShapeDtypeStruct((16 * len(parts), parts[0].shape[1]), BF16),
+        compiler_params=pltpu.CompilerParams(vmem_limit_bytes=4 * 2**20),
+        cost_estimate=pl.CostEstimate(flops=0, bytes_accessed=2**18, transcendentals=0),
+    )(token, *parts)
+
+
+def tile_kernel(which, placed, codes, meta, source, mine, other, *rest):
+    outs, (tiles, wide, acc, sems) = rest[: len(placed)], rest[len(placed) :]
+    slots = source.shape[0]
+    start = which * (slots + GROUP)
+    groups = (codes[2 * (slots + GROUP) + which] + GROUP - 1) >> 5
+
+    def bring(g, _):
+        for u in range(GROUP):
+            n = g * GROUP + u
+            pltpu.make_async_copy(source.at[codes[start + n] >> 13], tiles.at[n], sems.at[g]).start()
+        return 0
+
+    lax.fori_loop(0, groups, bring, 0)
     for part, dist in enumerate((0,) + DISTS):
-        y_of = (meta[1] - dist) & (YS - 1)
-        for ref, core in ((mine, meta[2]), (other, 1 - meta[2])):
+        y_of = (meta[0] - dist) & (YS - 1)
+        for ref, core in ((mine, meta[1]), (other, 1 - meta[1])):
             at = pl.multiple_of((y_of * CS + core) * 16, 16)
             wide[pl.ds(at, 16), :] = ref[part * 16 : part * 16 + 16, :]
-
-    def clear(i, _):
-        acc[pl.ds(i * 4, 4)] = jnp.zeros((4, T, T), F32)
+    for first, size in placed:
+
+        def clear(i, _):
+            acc[pl.ds(first + i * 4, 4)] = jnp.zeros((4, T, T), F32)
+            return 0
+
+        lax.fori_loop(0, size // 4, clear, 0)
+
+    def several(g, _):
+        base = pl.multiple_of(g * GROUP, GROUP)
+        here = tiles.at[pl.ds(base, GROUP)]
+        pltpu.make_async_copy(source.at[pl.ds(0, GROUP)], here, sems.at[g]).wait()
+        products = []
+        for u in range(GROUP):
+            at = pl.multiple_of(((codes[start + base + u] >> 8) & 31) * T, T)
+            products.append(jnp.dot(wide[:, pl.ds(at, T)], tiles[base + u], preferred_element_type=F32))
+        for u in range(GROUP):
+            place = codes[start + base + u] & 255
+            acc[place] = acc[place] + products[u]
         return 0
 
-    lax.fori_loop(0, 32, clear, 0)
-
-    def several(g, _):
-        chunk(g).wait()
-
-        @pl.when(g * GROUP < meta[0])
-        def _():
-            base = g * GROUP
-            products = []
-            for u in range(GROUP):
-                at = pl.multiple_of((codes[base + u] >> 8) * T, T)
-                products.append(
-                    jnp.dot(wide[:, pl.ds(at, T)], tiles[base + u], preferred_element_type=F32)
-                )
-            for u in range(GROUP):
-                place = codes[base + u] & 255
-                acc[place] = acc[place] + products[u]
-
-        return 0
-
-    lax.fori_loop(0, steps, several, 0)
-
-    for out, (first, size) in zip(outs, PLACED):
+    lax.fori_loop(0, groups, several, 0)
+
+    for out, (first, size) in zip(outs, placed):
 
         def put(i, _):
             out[pl.ds(i * 4, 4)] = acc[pl.ds(first + i * 4, 4)].astype(BF16)
@@ -102,40 +164,33 @@
         lax.fori_loop(0, size // 4, put, 0)
 
 
-def tile_products(codes, meta, tiles, mine, other):
+def tile_products(which, placed, codes, meta, tiles, mine, other):
     smem, vmem = pl.BlockSpec(memory_space=pltpu.SMEM), pl.BlockSpec(memory_space=pltpu.VMEM)
     return pl.pallas_call(
-        tile_kernel,
+        functools.partial(tile_kernel, which, placed),
         in_specs=[smem] * 2 + [pl.BlockSpec(memory_space=pl.ANY)] + [vmem] * 2,
-        out_specs=[vmem] * 7,
+        out_specs=[vmem] * len(placed),
         scratch_shapes=[
             pltpu.VMEM(tiles.shape, BF16),
             pltpu.VMEM((T, mine.shape[1]), BF16),
             pltpu.VMEM((129, T, T), F32),
             pltpu.SemaphoreType.DMA((tiles.shape[0] // GROUP,)),
         ],
-        out_shape=[jax.ShapeDtypeStruct((n, T, T), BF16) for _, n in PLACED],
-        compiler_params=pltpu.CompilerParams(vmem_limit_bytes=50 * 2**20),
-        cost_estimate=pl.CostEstimate(flops=2**30, bytes_accessed=13 * 2**20, transcendentals=0),
+        out_shape=[jax.ShapeDtypeStruct((n, T, T), BF16) for _, n in placed],
+        compiler_params=pltpu.CompilerParams(vmem_limit_bytes=46 * 2**20),
+        cost_estimate=pl.CostEstimate(flops=0, bytes_accessed=2**24, transcendentals=0),
     )(codes, meta, tiles, mine, other)
 
 
-def middle_kernel(c0, upa, upb, downa, downb, feats, out, grad, sums):
-    sums[...] = jnp.zeros((T, T), F32)
-    for first, up, down in ((0, upa, downa), (16, upb, downb)):
-
-        def several(i, _):
-            total = sums[...]
-            for u in range(4):
-                n, k = i * 4 + u, first + i * 4 + u
-                value = (c0[k].astype(F32) + up[n].astype(F32) + down[n].astype(F32)).astype(BF16)
-                out[k] = value
-                total += jnp.dot(value, feats[k], preferred_element_type=F32)
-            sums[...] = total
-            return 0
-
-        lax.fori_loop(0, 4, several, 0)
-    grad[...] = sums[...].T
+def middle_kernel(c0, upa, upb, downa, downb, feats, out, grad):
+    total = jnp.zeros((T, T), F32)
+    for k in range(32):
+        up, down = (upa, downa) if k < 16 else (upb, downb)
+        n = k % 16
+        value = (c0[k].astype(F32) + up[n].astype(F32) + down[n].astype(F32)).astype(BF16)
+        out[k] = value
+        total += jnp.dot(value, feats[k], preferred_element_type=F32)
+    grad[...] = total.T
 
 
 def middle(*operands):
@@ -145,7 +200,6 @@
         in_specs=[spec] * 6,
         out_specs=[spec] * 2,
         out_shape=[jax.ShapeDtypeStruct((32, T, T), BF16), jax.ShapeDtypeStruct((T, T), F32)],
-        scratch_shapes=[pltpu.VMEM((T, T), F32)],
         compiler_params=pltpu.CompilerParams(vmem_limit_bytes=12 * 2**20),
         cost_estimate=pl.CostEstimate(flops=2**27, bytes_accessed=5 * 2**20, transcendentals=0),
     )(*operands)
@@ -180,23 +234,18 @@
     wide_feats = lax.all_gather(features, "z", axis=0, tiled=True).reshape(ZS * 4, T, T)
 
     masked = (out_grad.astype(F32) * relu_mask.astype(F32)).astype(BF16).T
-    mine = jnp.concatenate([masked] + [shift(masked, "y", YS, d) for d in DISTS], axis=0)
-    other = swap(mine)
-
-    count = tile_count.reshape(())
-    cols = tile_col.reshape(slots)
-    dest = cols >> 2
-    dx = ((dest >> 3) - x) & (XS - 1)
-    places = jnp.where(lax.iota(jnp.int32, slots) < count, dx * 32 + (cols & 31), 128)
-    codes = tile_row.reshape(slots) * 256 + places
-    meta = jnp.stack([count, y, core]).astype(jnp.int32)
-    tiles = tile_vals.reshape(slots, T, T)
-    c2a, c2b, c1b, c3a, c1a, c3b, c0 = tile_products(codes, meta, tiles, mine, other)
+    codes = sort_tiles(tile_row.reshape(slots), tile_col.reshape(slots), tile_count.reshape(1), x.reshape(1))
+    meta = jnp.stack([y, core]).astype(jnp.int32)
+
+    mine = join(codes, masked, *(shift(masked, "y", YS, d) for d in DISTS))
+    operands = (codes, meta, tile_vals.reshape(slots, T, T), mine, swap(mine))
+    c2a, c2b = tile_products(0, CHUNK2, *operands)
+    c1b, c3a, c1a, c3b, c0 = tile_products(1, OTHERS, *operands)
 
     up, down = shift(c2a, "x", XS, 1), shift(c2b, "x", XS, 3)
     upb, downa = shift(c1b, "x", XS, 1), shift(c3a, "x", XS, 3)
     upa, downb = shift(add(c1a, up), "x", XS, 1), shift(add(c3b, down), "x", XS, 3)
-    reduced, grad = middle(c0, upa, upb, downa, downb, fetch(wide_feats))
+    reduced, grad = middle(fetch(c0), upa, upb, downa, downb, fetch(wide_feats))
 
     aggregate = lax.psum_scatter(reduced, "z", scatter_dimension=0, tiled=True)
 

time: 124 us -> 119 us (0.960)
  waiting for transfers between devices: 53.3 us -> 44.2 us
  Pallas kernels: 9.4 us -> 15.9 us
  other arithmetic: 4.44 us -> 3.03 us
    ppermute x15, waiting for transfers between devices: 32.7 us -> 13.3 us  [shift(): lax.ppermute(value, axis, [(i, (i + by) % size) for i in range(size)])]
    all_gather x1, waiting for transfers between devices: 2.9 us -> 13.7 us  [local(): lax.all_gather(features, 'z', axis=0, tiled=True).reshape(ZS * 4, T, T)]
    pallas_call x1 -> x4, Pallas kernels: 6.05 us -> 13.4 us  [the longest x2 9.34 us: tile_products(): pl.pallas_call(functools.partial(tile_kernel, which, placed), in_specs=[s...]
    ppermute x15, starting transfers between devices: 26.3 us -> 24.3 us  [shift(): lax.ppermute(value, axis, [(i, (i + by) % size) for i in range(size)])]
    reduce_scatter x1, waiting for transfers between devices: 5.77 us -> 4.35 us  [local(): aggregate = lax.psum_scatter(reduced, 'z', scatter_dimension=0, tiled=True)]
    unnamed x14 -> x16, local copies, waits for them, and re-layouts: 4.16 us -> 3.52 us
  transfers between devices with their start and end apart: 24 -> 24, of which waited for: 18 -> 16; matrix products, arithmetic and copies ran while one was open for 3% -> 2% of each run, Pallas kernels for 5% -> 11%
where the time goes in v4:
time: 119 us; the launch traced here: 118 us
  waiting for transfers between devices  44.2 us (37%)
  starting transfers between devices  36.6 us (31%)
  Pallas kernels  15.9 us (13%)
  between operations  14.9 us (13%)
  local copies, waits for them, and re-layouts  3.52 us (3%)
  other arithmetic  3.03 us (3%)
    ppermute x15, starting transfers between devices, shift(): lax.ppermute(value, axis, [(i, (i + by) % size) for i in range(size)])  24.3 us
    all_gather x1, waiting for transfers between devices, local(): lax.all_gather(features, 'z', axis=0, tiled=True).reshape(ZS * 4, T, T)  13.7 us
    ppermute x15, waiting for transfers between devices, shift(): lax.ppermute(value, axis, [(i, (i + by) % size) for i in range(size)])  13.3 us
    ppermute x4, starting transfers between devices, spread(): total = total + lax.ppermute(value, (axis, 'core'), pairs)  12 us
    pallas_call x2, Pallas kernels, tile_products(): pl.pallas_call(functools.partial(tile_kernel, which, placed), in_specs=[s...  9.34 us
    ppermute x4, waiting for transfers between devices, spread(): total = total + lax.ppermute(value, (axis, 'core'), pairs)  8.6 us
    reduce_scatter x1, waiting for transfers between devices, local(): aggregate = lax.psum_scatter(reduced, 'z', scatter_dimension=0, tiled=True)  4.35 us
    ppermute x3, waiting for transfers between devices, swap(): return lax.ppermute(value, 'core', [(0, 1), (1, 0)])  4.23 us
  transfers between devices with their start and end apart: 24, of which 16 were waited for; matrix products, arithmetic and copies ran while one was open for 2% of the time, Pallas kernels for 11%

profile of v4, /device:TPU:32, one launch (start us, length us, event | category | flops | bytes accessed | tf_op | source)
XLA Modules:
  0.0 118.2 jit_solution(18147607823236135423)
XLA Ops:
  7.2 0.0 all-gather.2.cloned.1.call-start
  7.2 1.0 fusion.refs_0_
  8.2 3.3 %collective-permute-start = (bf16[16,4096]{1,0:T(8,128)(2,1)S(1)}, bf16[16,4096]{1,0:T(8,128)(2,1)S(1)}, u32[]{:S(2)}, u32[]{:S(2)}) collective-permute-start(bf16[16,4096]{1,0:T(8,128)(2,1)S(1)} %fusion.refs_0_), channel_id=1, source_target_pairs={{0,4},{2,6},{4,0},{6,2},{1,5},{3,7},{5,1},{7,3},{8,12},{10,14},{12... | collective-permute-start | bytes 393224 | tf_op jit(solution)/shard_map/ppermute | solution.py:17
  11.5 0.7 collective-permute-start.1
  12.2 2.6 %collective-permute-start.2 = (bf16[16,4096]{1,0:T(8,128)(2,1)S(1)}, bf16[16,4096]{1,0:T(8,128)(2,1)S(1)}, u32[]{:S(2)}, u32[]{:S(2)}) collective-permute-start(bf16[16,4096]{1,0:T(8,128)(2,1)S(1)} %fusion.refs_0_), channel_id=1, source_target_pairs={{0,6},{2,0},{4,2},{6,4},{1,7},{3,1},{5,3},{7,5},{8,14},{10,8},{12,... | collective-permute-start | bytes 393224 | tf_op jit(solution)/shard_map/ppermute | solution.py:17
  15.4 3.5 %shard_map.113.token.codes = s32[578]{0:T(1024)} custom-call(s32[256]{0:T(256)} %bitcast.14, s32[256]{0:T(256)} %bitcast.15, s32[1]{0:T(128)} %bitcast.10.count, s32[1]{0:T(128)} %bitcast.3.x), custom_call_target="tpu_custom_call" | custom-call | bytes 4096 | tf_op jit(solution)/shard_map/pallas_call | solution.py:91
  18.9 0.0 collective-permute-done.refs_1_
  18.9 0.0 copy-start.2
  18.9 0.7 copy-done.2
  19.6 0.6 shard_map.114.mine
  20.2 0.1 collective-permute-start.3
  20.3 0.0 all-gather.2.cloned.1.call-update
  20.4 0.0 reduce-scatter.2.cloned.1.call-start
  20.4 0.1 pad_add_fusion.meta
  20.5 1.7 %collective-permute-done.3.other = bf16[64,4096]{1,0:T(8,128)(2,1)S(1)} collective-permute-done((bf16[64,4096]{1,0:T(8,128)(2,1)S(1)}, bf16[64,4096]{1,0:T(8,128)(2,1)S(1)}, u32[]{:S(2)}, u32[]{:S(2)}) %collective-permute-start.3) | collective-permute-done | bytes 524320 | tf_op jit(solution)/shard_map/ppermute | solution.py:21
  22.2 0.7 copy-done.3
  22.9 3.0 %shard_map.117 = (bf16[16,128,128]{2,1,0:T(8,128)(2,1)S(1)}, bf16[16,128,128]{2,1,0:T(8,128)(2,1)S(1)}) custom-call(s32[578]{0:T(1024)S(1)} %copy-done.3, s32[2]{0:T(128)S(1)} %pad_add_fusion.meta, bf16[256,128,128]{2,1,0:T(8,128)(2,1)} %bitcast.12, bf16[64,4096]{1,0:T(8,128)(2,1)S(1)} %shard_map.114.mine, bf16[64,4096]{1,0:T(8,128)(2,1)S(1)} %collective-permute-done.3.other), custom_call_target="tpu_custom_call" | custom-call | bytes 16777216 | tf_op jit(solution)/shard_map/pallas_call | solution.py:169
  25.9 3.1 %collective-permute-start.8 = (bf16[16,128,128]{2,1,0:T(8,128)(2,1)S(1)}, bf16[16,128,128]{2,1,0:T(8,128)(2,1)S(1)}, u32[]{:S(2)}, u32[]{:S(2)}) collective-permute-start(bf16[16,128,128]{2,1,0:T(8,128)(2,1)S(1)} %get-tuple-element.17), channel_id=1, source_target_pairs={{0,192},{64,0},{128,64},{192,128},{1,193},{65,1},{129,65},{193,129... | collective-permute-start | bytes 1572872 | tf_op jit(solution)/shard_map/ppermute | solution.py:17
  29.0 0.0 collective-permute-start.4
  29.0 6.3 %shard_map.115 = (bf16[16,128,128]{2,1,0:T(8,128)(2,1)}, bf16[16,128,128]{2,1,0:T(8,128)(2,1)}, bf16[16,128,128]{2,1,0:T(8,128)(2,1)S(1)}, bf16[16,128,128]{2,1,0:T(8,128)(2,1)S(1)}, bf16[32,128,128]{2,1,0:T(8,128)(2,1)S(1)}) custom-call(s32[578]{0:T(1024)S(1)} %copy-done.4, s32[2]{0:T(128)S(1)} %pad_add_fusion.meta, bf16[256,128,128]{2,1,0:T(8,128)(2,1)} %bitcast.13, ...), custom_call_target="tpu_custom_call" | custom-call | bytes 16777216 | tf_op jit(solution)/shard_map/pallas_call | solution.py:169
  35.3 0.0 copy-start.5
  35.3 0.0 copy-start.6
  35.4 0.0 copy-start.7
  35.4 0.1 collective-permute-start.6
  35.5 3.2 %collective-permute-start.7 = (bf16[16,128,128]{2,1,0:T(8,128)(2,1)}, bf16[16,128,128]{2,1,0:T(8,128)(2,1)S(1)}, u32[]{:S(2)}, u32[]{:S(2)}) collective-permute-start(bf16[16,128,128]{2,1,0:T(8,128)(2,1)} %get-tuple-element.15), channel_id=1, source_target_pairs={{0,192},{64,0},{128,64},{192,128},{1,193},{65,1},{129,65},{193,129... | collective-permute-start | bytes 1572872 | tf_op jit(solution)/shard_map/ppermute | solution.py:17
  38.7 2.6 %collective-permute-done.8 = bf16[16,128,128]{2,1,0:T(8,128)(2,1)S(1)} collective-permute-done((bf16[16,128,128]{2,1,0:T(8,128)(2,1)S(1)}, bf16[16,128,128]{2,1,0:T(8,128)(2,1)S(1)}, u32[]{:S(2)}, u32[]{:S(2)}) %collective-permute-start.8) | collective-permute-done | bytes 524320 | tf_op jit(solution)/shard_map/ppermute | solution.py:17
  41.3 0.9 add_convert_fusion
  42.2 3.7 %collective-permute-start.9 = (bf16[16,128,128]{2,1,0:T(8,128)(2,1)}, bf16[16,128,128]{2,1,0:T(8,128)(2,1)S(1)}, u32[]{:S(2)}, u32[]{:S(2)}) collective-permute-start(bf16[16,128,128]{2,1,0:T(8,128)(2,1)} %add_convert_fusion), channel_id=1, source_target_pairs={{0,192},{64,0},{128,64},{192,128},{1,193},{65,1},{129,65},{193,129... | collective-permute-start | bytes 1572872 | tf_op jit(solution)/shard_map/ppermute | solution.py:17
  45.9 0.9 add_convert_fusion.1
  46.9 0.1 shard_map.116.c0
  47.0 13.7 %all-gather.2.cloned.1.call-done = bf16[4096,128]{1,0:T(8,128)(2,1)} async-done(((bf16[512,128]{1,0:T(8,128)(2,1)}), bf16[4096,128]{1,0:T(8,128)(2,1)}) %all-gather.2.cloned.1.call-update) | async-done | bytes 1048592 | tf_op jit(solution)/shard_map/all_gather | solution.py:234
  60.6 1.2 %copy-done = bf16[4096,128]{1,0:T(8,128)(2,1)S(1)} copy-done((bf16[4096,128]{1,0:T(8,128)(2,1)S(1)}, bf16[4096,128]{1,0:T(8,128)(2,1)}, u32[]{:S(2)}) %copy-start) | copy-done | bytes 1048600
  61.9 0.1 shard_map.118.feats
  62.0 0.0 collective-permute-done.6.upb
  62.0 0.0 collective-permute-done.7.downa
  62.0 1.1 collective-permute-done.9.downb
  63.1 3.1 %collective-permute-done.5.upa = bf16[16,128,128]{2,1,0:T(8,128)(2,1)S(1)} collective-permute-done((bf16[16,128,128]{2,1,0:T(8,128)(2,1)}, bf16[16,128,128]{2,1,0:T(8,128)(2,1)S(1)}, u32[]{:S(2)}, u32[]{:S(2)}) %collective-permute-start.5) | collective-permute-done | bytes 524320 | tf_op jit(solution)/shard_map/ppermute | solution.py:17
  66.1 1.4 %shard_map.119 = (bf16[32,128,128]{2,1,0:T(8,128)(2,1)}, f32[128,128]{1,0:T(8,128)S(1)}) custom-call(bf16[32,128,128]{2,1,0:T(8,128)(2,1)S(1)} %shard_map.116.c0, bf16[16,128,128]{2,1,0:T(8,128)(2,1)S(1)} %collective-permute-done.5.upa, bf16[16,128,128]{2,1,0:T(8,128)(2,1)S(1)} %collective-permute-done.6.upb, ...), custom_call_target="tpu_custom_call" | custom-call | flops 134217728 | bytes 5242880 | tf_op jit(solution)/shard_map/pallas_call | solution.py:198
  67.5 0.0 reduce-scatter.2.cloned.1.call-update
  67.5 0.1 collective-permute-start.10
  67.6 1.2 %collective-permute-done.10 = f32[128,128]{1,0:T(8,128)S(1)} collective-permute-done((f32[128,128]{1,0:T(8,128)S(1)}, f32[128,128]{1,0:T(8,128)S(1)}, u32[]{:S(2)}, u32[]{:S(2)}) %collective-permute-start.10) | collective-permute-done | bytes 65568 | tf_op jit(solution)/shard_map/ppermute | solution.py:21
  68.9 1.1 collective-permute-start.11
  69.9 2.5 %collective-permute-start.12 = (f32[128,128]{1,0:T(8,128)S(1)}, f32[128,128]{1,0:T(8,128)S(1)}, u32[]{:S(2)}, u32[]{:S(2)}) collective-permute-start(f32[128,128]{1,0:T(8,128)S(1)} %add.43), channel_id=1, source_target_pairs={{0,2},{2,4},{4,6},{6,0},{1,3},{3,5},{5,7},{7,1},{8,10},{10,12},{12... | collective-permute-start | bytes 196616 | tf_op jit(solution)/shard_map/ppermute | solution.py:17
  72.5 0.7 collective-permute-start.13
  73.2 2.1 %collective-permute-done.11 = f32[128,128]{1,0:T(8,128)S(1)} collective-permute-done((f32[128,128]{1,0:T(8,128)S(1)}, f32[128,128]{1,0:T(8,128)S(1)}, u32[]{:S(2)}, u32[]{:S(2)}) %collective-permute-start.11) | collective-permute-done | bytes 65568 | tf_op jit(solution)/shard_map/ppermute | solution.py:17
  75.3 0.8 collective-permute-done.12
  76.0 0.7 collective-permute-done.13
  76.8 0.1 collective-permute-start.14
  76.9 1.1 collective-permute-start.15
  78.0 2.2 %collective-permute-start.16 = (f32[128,128]{1,0:T(8,128)S(1)}, f32[128,128]{1,0:T(8,128)S(1)}, u32[]{:S(2)}, u32[]{:S(2)}) collective-permute-start(f32[128,128]{1,0:T(8,128)S(1)} %add_add_fusion.2), channel_id=1, source_target_pairs={{0,192},{64,0},{128,64},{192,128},{1,193},{65,1},{129,65},{193,129... | collective-permute-start | bytes 196616 | tf_op jit(solution)/shard_map/ppermute | solution.py:17
  80.2 2.5 %collective-permute-done.14 = f32[128,128]{1,0:T(8,128)S(1)} collective-permute-done((f32[128,128]{1,0:T(8,128)S(1)}, f32[128,128]{1,0:T(8,128)S(1)}, u32[]{:S(2)}, u32[]{:S(2)}) %collective-permute-start.14) | collective-permute-done | bytes 65568 | tf_op jit(solution)/shard_map/ppermute | solution.py:17
  82.7 0.4 collective-permute-done.15
  83.2 8.0 %collective-permute-start.17 = (f32[128,128]{1,0:T(8,128)S(1)}, f32[128,128]{1,0:T(8,128)S(1)}, u32[]{:S(2)}, u32[]{:S(2)}) collective-permute-start(f32[128,128]{1,0:T(8,128)S(1)} %add_add_fusion.1), channel_id=1, source_target_pairs={{0,32},{8,40},{16,48},{24,56},{32,0},{40,8},{48,16},{56,24},{2,34}... | collective-permute-start | bytes 196616 | tf_op jit(solution)/shard_map/ppermute | solution.py:30
  91.1 0.3 collective-permute-start.18
  91.5 1.6 %collective-permute-start.19 = (f32[128,128]{1,0:T(8,128)S(1)}, f32[128,128]{1,0:T(8,128)S(1)}, u32[]{:S(2)}, u32[]{:S(2)}) collective-permute-start(f32[128,128]{1,0:T(8,128)S(1)} %add_add_fusion.1), channel_id=1, source_target_pairs={{0,16},{8,24},{16,32},{24,40},{32,48},{40,56},{48,0},{56,8},{1,49}... | collective-permute-start | bytes 196616 | tf_op jit(solution)/shard_map/ppermute | solution.py:30
  93.1 2.1 %collective-permute-start.20 = (f32[128,128]{1,0:T(8,128)S(1)}, f32[128,128]{1,0:T(8,128)S(1)}, u32[]{:S(2)}, u32[]{:S(2)}) collective-permute-start(f32[128,128]{1,0:T(8,128)S(1)} %add_add_fusion.1), channel_id=1, source_target_pairs={{0,8},{8,16},{16,24},{24,32},{32,40},{40,48},{48,56},{56,0},{1,57}... | collective-permute-start | bytes 196616 | tf_op jit(solution)/shard_map/ppermute | solution.py:30
  95.2 0.9 collective-permute-done.17
  96.0 3.2 %collective-permute-done.18 = f32[128,128]{1,0:T(8,128)S(1)} collective-permute-done((f32[128,128]{1,0:T(8,128)S(1)}, f32[128,128]{1,0:T(8,128)S(1)}, u32[]{:S(2)}, u32[]{:S(2)}) %collective-permute-start.18) | collective-permute-done | bytes 65568 | tf_op jit(solution)/shard_map/ppermute | solution.py:30
  99.2 4.6 %collective-permute-done.19 = f32[128,128]{1,0:T(8,128)S(1)} collective-permute-done((f32[128,128]{1,0:T(8,128)S(1)}, f32[128,128]{1,0:T(8,128)S(1)}, u32[]{:S(2)}, u32[]{:S(2)}) %collective-permute-start.19) | collective-permute-done | bytes 65568 | tf_op jit(solution)/shard_map/ppermute | solution.py:30
  103.8 0.1 collective-permute-start.21
  103.9 1.2 %collective-permute-done.21.more = f32[128,128]{1,0:T(8,128)S(1)} collective-permute-done((f32[128,128]{1,0:T(8,128)S(1)}, f32[128,128]{1,0:T(8,128)S(1)}, u32[]{:S(2)}, u32[]{:S(2)}) %collective-permute-start.21) | collective-permute-done | bytes 65568 | tf_op jit(solution)/shard_map/ppermute | solution.py:21
  105.1 4.3 %reduce-scatter.2.cloned.1.call-done.aggregate = bf16[4,128,128]{2,1,0:T(8,128)(2,1)} async-done(((bf16[32,128,128]{2,1,0:T(8,128)(2,1)}), bf16[4,128,128]{2,1,0:T(8,128)(2,1)}) %reduce-scatter.2.cloned.1.call-update) | async-done | bytes 131088 | tf_op jit(solution)/shard_map/reduce_scatter | solution.py:250
  109.5 0.9 copy-done.1
  110.4 0.9 shard_map.120
  (18 shorter events, 0.1 us)
Async XLA Ops:
  7.2 53.5 %all-gather.2.cloned.1.call-start = ((), (), s32[]{:S(2)}) async-start(), calls=%async_computation.1 | async-start | bytes 1179648 | tf_op jit(solution)/shard_map/all_gather | solution.py:234
  8.2 10.7 %collective-permute-start = (bf16[16,4096]{1,0:T(8,128)(2,1)S(1)}, bf16[16,4096]{1,0:T(8,128)(2,1)S(1)}, u32[]{:S(2)}, u32[]{:S(2)}) collective-permute-start(bf16[16,4096]{1,0:T(8,128)(2,1)S(1)} %fusion.refs_0_), channel_id=1, source_target_pairs={{0,4},{2,6},{4,0},{6,2},{1,5},{3,7},{5,1},{7,3},{8,12},{10,14},{12... | collective-permute-start | bytes 393224 | tf_op jit(solution)/shard_map/ppermute | solution.py:17
  11.5 7.4 %collective-permute-start.1 = (bf16[16,4096]{1,0:T(8,128)(2,1)S(1)}, bf16[16,4096]{1,0:T(8,128)(2,1)S(1)}, u32[]{:S(2)}, u32[]{:S(2)}) collective-permute-start(bf16[16,4096]{1,0:T(8,128)(2,1)S(1)} %fusion.refs_0_), channel_id=1, source_target_pairs={{0,2},{2,4},{4,6},{6,0},{1,3},{3,5},{5,7},{7,1},{8,10},{10,12},{12... | collective-permute-start | bytes 393224 | tf_op jit(solution)/shard_map/ppermute | solution.py:17
  12.2 6.7 %collective-permute-start.2 = (bf16[16,4096]{1,0:T(8,128)(2,1)S(1)}, bf16[16,4096]{1,0:T(8,128)(2,1)S(1)}, u32[]{:S(2)}, u32[]{:S(2)}) collective-permute-start(bf16[16,4096]{1,0:T(8,128)(2,1)S(1)} %fusion.refs_0_), channel_id=1, source_target_pairs={{0,6},{2,0},{4,2},{6,4},{1,7},{3,1},{5,3},{7,5},{8,14},{10,8},{12,... | collective-permute-start | bytes 393224 | tf_op jit(solution)/shard_map/ppermute | solution.py:17
  18.9 0.7 copy-start.2
  19.6 9.4 %copy-start.4 = (s32[578]{0:T(1024)S(1)}, s32[578]{0:T(1024)}, u32[]{:S(2)}) copy-start(s32[578]{0:T(1024)} %shard_map.113.token.codes) | copy-start | bytes 6940
  20.2 2.0 %collective-permute-start.3 = (bf16[64,4096]{1,0:T(8,128)(2,1)S(1)}, bf16[64,4096]{1,0:T(8,128)(2,1)S(1)}, u32[]{:S(2)}, u32[]{:S(2)}) collective-permute-start(bf16[64,4096]{1,0:T(8,128)(2,1)S(1)} %shard_map.114.mine), channel_id=1, source_target_pairs={{0,1},{1,0},{2,3},{3,2},{4,5},{5,4},{6,7},{7,6},{8,9},{9,8},{10,11... | collective-permute-start | bytes 1572872 | tf_op jit(solution)/shard_map/ppermute | solution.py:21
  20.4 89.1 %reduce-scatter.2.cloned.1.call-start = ((), (), s32[]{:S(2)}) async-start(), calls=%async_computation.2 | async-start | bytes 1179648 | tf_op jit(solution)/shard_map/reduce_scatter | solution.py:250
  22.2 0.7 copy-start.3
  25.9 15.4 %collective-permute-start.8 = (bf16[16,128,128]{2,1,0:T(8,128)(2,1)S(1)}, bf16[16,128,128]{2,1,0:T(8,128)(2,1)S(1)}, u32[]{:S(2)}, u32[]{:S(2)}) collective-permute-start(bf16[16,128,128]{2,1,0:T(8,128)(2,1)S(1)} %get-tuple-element.17), channel_id=1, source_target_pairs={{0,192},{64,0},{128,64},{192,128},{1,193},{65,1},{129,65},{193,129... | collective-permute-start | bytes 1572872 | tf_op jit(solution)/shard_map/ppermute | solution.py:17
  29.0 16.9 %collective-permute-start.4 = (bf16[16,128,128]{2,1,0:T(8,128)(2,1)S(1)}, bf16[16,128,128]{2,1,0:T(8,128)(2,1)S(1)}, u32[]{:S(2)}, u32[]{:S(2)}) collective-permute-start(bf16[16,128,128]{2,1,0:T(8,128)(2,1)S(1)} %get-tuple-element.13), channel_id=1, source_target_pairs={{0,64},{64,128},{128,192},{192,0},{1,65},{65,129},{129,193},{193,1... | collective-permute-start | bytes 1572872 | tf_op jit(solution)/shard_map/ppermute | solution.py:17
  35.3 74.2 %copy-start.5 = (f32[128,128]{1,0:T(8,128)S(1)}, f32[128,128]{1,0:T(8,128)}, u32[]{:S(2)}) copy-start(f32[128,128]{1,0:T(8,128)} %importance.1) | copy-start | bytes 196612
  35.3 74.2 %copy-start.6 = (f32[128,128]{1,0:T(8,128)S(1)}, f32[128,128]{1,0:T(8,128)}, u32[]{:S(2)}) copy-start(f32[128,128]{1,0:T(8,128)} %delta.1) | copy-start | bytes 196612
  35.4 74.1 %copy-start.7 = (bf16[128,128]{1,0:T(8,128)(2,1)S(1)}, bf16[128,128]{1,0:T(8,128)(2,1)}, u32[]{:S(2)}) copy-start(bf16[128,128]{1,0:T(8,128)(2,1)} %weight.1) | copy-start | bytes 98308
  35.4 26.6 %collective-permute-start.6 = (bf16[16,128,128]{2,1,0:T(8,128)(2,1)}, bf16[16,128,128]{2,1,0:T(8,128)(2,1)S(1)}, u32[]{:S(2)}, u32[]{:S(2)}) collective-permute-start(bf16[16,128,128]{2,1,0:T(8,128)(2,1)} %get-tuple-element.14), channel_id=1, source_target_pairs={{0,64},{64,128},{128,192},{192,0},{1,65},{65,129},{129,193},{193,1... | collective-permute-start | bytes 1572872 | tf_op jit(solution)/shard_map/ppermute | solution.py:17
  35.5 26.5 %collective-permute-start.7 = (bf16[16,128,128]{2,1,0:T(8,128)(2,1)}, bf16[16,128,128]{2,1,0:T(8,128)(2,1)S(1)}, u32[]{:S(2)}, u32[]{:S(2)}) collective-permute-start(bf16[16,128,128]{2,1,0:T(8,128)(2,1)} %get-tuple-element.15), channel_id=1, source_target_pairs={{0,192},{64,0},{128,64},{192,128},{1,193},{65,1},{129,65},{193,129... | collective-permute-start | bytes 1572872 | tf_op jit(solution)/shard_map/ppermute | solution.py:17
  42.2 20.8 %collective-permute-start.9 = (bf16[16,128,128]{2,1,0:T(8,128)(2,1)}, bf16[16,128,128]{2,1,0:T(8,128)(2,1)S(1)}, u32[]{:S(2)}, u32[]{:S(2)}) collective-permute-start(bf16[16,128,128]{2,1,0:T(8,128)(2,1)} %add_convert_fusion), channel_id=1, source_target_pairs={{0,192},{64,0},{128,64},{192,128},{1,193},{65,1},{129,65},{193,129... | collective-permute-start | bytes 1572872 | tf_op jit(solution)/shard_map/ppermute | solution.py:17
  46.9 19.3 %collective-permute-start.5 = (bf16[16,128,128]{2,1,0:T(8,128)(2,1)}, bf16[16,128,128]{2,1,0:T(8,128)(2,1)S(1)}, u32[]{:S(2)}, u32[]{:S(2)}) collective-permute-start(bf16[16,128,128]{2,1,0:T(8,128)(2,1)} %add_convert_fusion.1), channel_id=1, source_target_pairs={{0,64},{64,128},{128,192},{192,0},{1,65},{65,129},{129,193},{193,1... | collective-permute-start | bytes 1572872 | tf_op jit(solution)/shard_map/ppermute | solution.py:17
  60.6 1.2 %copy-start = (bf16[4096,128]{1,0:T(8,128)(2,1)S(1)}, bf16[4096,128]{1,0:T(8,128)(2,1)}, u32[]{:S(2)}) copy-start(bf16[4096,128]{1,0:T(8,128)(2,1)} %all-gather.2.cloned.1.call-done) | copy-start | bytes 3145732
  67.5 1.3 %collective-permute-start.10 = (f32[128,128]{1,0:T(8,128)S(1)}, f32[128,128]{1,0:T(8,128)S(1)}, u32[]{:S(2)}, u32[]{:S(2)}) collective-permute-start(f32[128,128]{1,0:T(8,128)S(1)} %get-tuple-element.19), channel_id=1, source_target_pairs={{0,1},{1,0},{2,3},{3,2},{4,5},{5,4},{6,7},{7,6},{8,9},{9,8},{10,11... | collective-permute-start | bytes 196616 | tf_op jit(solution)/shard_map/ppermute | solution.py:21
  68.9 6.4 %collective-permute-start.11 = (f32[128,128]{1,0:T(8,128)S(1)}, f32[128,128]{1,0:T(8,128)S(1)}, u32[]{:S(2)}, u32[]{:S(2)}) collective-permute-start(f32[128,128]{1,0:T(8,128)S(1)} %add.43), channel_id=1, source_target_pairs={{0,4},{2,6},{4,0},{6,2},{1,5},{3,7},{5,1},{7,3},{8,12},{10,14},{12... | collective-permute-start | bytes 196616 | tf_op jit(solution)/shard_map/ppermute | solution.py:17
  69.9 6.1 %collective-permute-start.12 = (f32[128,128]{1,0:T(8,128)S(1)}, f32[128,128]{1,0:T(8,128)S(1)}, u32[]{:S(2)}, u32[]{:S(2)}) collective-permute-start(f32[128,128]{1,0:T(8,128)S(1)} %add.43), channel_id=1, source_target_pairs={{0,2},{2,4},{4,6},{6,0},{1,3},{3,5},{5,7},{7,1},{8,10},{10,12},{12... | collective-permute-start | bytes 196616 | tf_op jit(solution)/shard_map/ppermute | solution.py:17
  72.5 4.3 %collective-permute-start.13 = (f32[128,128]{1,0:T(8,128)S(1)}, f32[128,128]{1,0:T(8,128)S(1)}, u32[]{:S(2)}, u32[]{:S(2)}) collective-permute-start(f32[128,128]{1,0:T(8,128)S(1)} %add.43), channel_id=1, source_target_pairs={{0,6},{2,0},{4,2},{6,4},{1,7},{3,1},{5,3},{7,5},{8,14},{10,8},{12,... | collective-permute-start | bytes 196616 | tf_op jit(solution)/shard_map/ppermute | solution.py:17
  76.8 6.0 %collective-permute-start.14 = (f32[128,128]{1,0:T(8,128)S(1)}, f32[128,128]{1,0:T(8,128)S(1)}, u32[]{:S(2)}, u32[]{:S(2)}) collective-permute-start(f32[128,128]{1,0:T(8,128)S(1)} %add_add_fusion.2), channel_id=1, source_target_pairs={{0,128},{64,192},{128,0},{192,64},{1,129},{65,193},{129,1},{193,65... | collective-permute-start | bytes 196616 | tf_op jit(solution)/shard_map/ppermute | solution.py:17
  76.9 6.3 %collective-permute-start.15 = (f32[128,128]{1,0:T(8,128)S(1)}, f32[128,128]{1,0:T(8,128)S(1)}, u32[]{:S(2)}, u32[]{:S(2)}) collective-permute-start(f32[128,128]{1,0:T(8,128)S(1)} %add_add_fusion.2), channel_id=1, source_target_pairs={{0,64},{64,128},{128,192},{192,0},{1,65},{65,129},{129,193},{193,1... | collective-permute-start | bytes 196616 | tf_op jit(solution)/shard_map/ppermute | solution.py:17
  78.0 5.1 %collective-permute-start.16 = (f32[128,128]{1,0:T(8,128)S(1)}, f32[128,128]{1,0:T(8,128)S(1)}, u32[]{:S(2)}, u32[]{:S(2)}) collective-permute-start(f32[128,128]{1,0:T(8,128)S(1)} %add_add_fusion.2), channel_id=1, source_target_pairs={{0,192},{64,0},{128,64},{192,128},{1,193},{65,1},{129,65},{193,129... | collective-permute-start | bytes 196616 | tf_op jit(solution)/shard_map/ppermute | solution.py:17
  83.2 12.9 %collective-permute-start.17 = (f32[128,128]{1,0:T(8,128)S(1)}, f32[128,128]{1,0:T(8,128)S(1)}, u32[]{:S(2)}, u32[]{:S(2)}) collective-permute-start(f32[128,128]{1,0:T(8,128)S(1)} %add_add_fusion.1), channel_id=1, source_target_pairs={{0,32},{8,40},{16,48},{24,56},{32,0},{40,8},{48,16},{56,24},{2,34}... | collective-permute-start | bytes 196616 | tf_op jit(solution)/shard_map/ppermute | solution.py:30
  91.1 8.1 %collective-permute-start.18 = (f32[128,128]{1,0:T(8,128)S(1)}, f32[128,128]{1,0:T(8,128)S(1)}, u32[]{:S(2)}, u32[]{:S(2)}) collective-permute-start(f32[128,128]{1,0:T(8,128)S(1)} %add_add_fusion.1), channel_id=1, source_target_pairs={{0,24},{8,32},{16,40},{24,48},{32,56},{40,0},{48,8},{56,16},{1,41}... | collective-permute-start | bytes 196616 | tf_op jit(solution)/shard_map/ppermute | solution.py:30
  91.5 12.3 %collective-permute-start.19 = (f32[128,128]{1,0:T(8,128)S(1)}, f32[128,128]{1,0:T(8,128)S(1)}, u32[]{:S(2)}, u32[]{:S(2)}) collective-permute-start(f32[128,128]{1,0:T(8,128)S(1)} %add_add_fusion.1), channel_id=1, source_target_pairs={{0,16},{8,24},{16,32},{24,40},{32,48},{40,56},{48,0},{56,8},{1,49}... | collective-permute-start | bytes 196616 | tf_op jit(solution)/shard_map/ppermute | solution.py:30
  93.1 10.7 %collective-permute-start.20 = (f32[128,128]{1,0:T(8,128)S(1)}, f32[128,128]{1,0:T(8,128)S(1)}, u32[]{:S(2)}, u32[]{:S(2)}) collective-permute-start(f32[128,128]{1,0:T(8,128)S(1)} %add_add_fusion.1), channel_id=1, source_target_pairs={{0,8},{8,16},{16,24},{24,32},{32,40},{40,48},{48,56},{56,0},{1,57}... | collective-permute-start | bytes 196616 | tf_op jit(solution)/shard_map/ppermute | solution.py:30
  103.8 1.3 %collective-permute-start.21 = (f32[128,128]{1,0:T(8,128)S(1)}, f32[128,128]{1,0:T(8,128)S(1)}, u32[]{:S(2)}, u32[]{:S(2)}) collective-permute-start(f32[128,128]{1,0:T(8,128)S(1)} %add_add_fusion.grad), channel_id=1, source_target_pairs={{0,1},{1,0},{2,3},{3,2},{4,5},{5,4},{6,7},{7,6},{8,9},{9,8},{10,11... | collective-permute-start | bytes 196616 | tf_op jit(solution)/shard_map/ppermute | solution.py:21
  109.5 0.9 copy-start.1
Sparse Core Ops, SparseCore 0:
  20.5 40.1 all-gather.1
  67.7 41.7 reduce-scatter.1

commit v5 on v4

--- a/solution.py
+++ b/solution.py
@@ -53,9 +53,10 @@
 CHUNK2 = ((64, 16), (80, 16))
 OTHERS = ((48, 16), (96, 16), (32, 16), (112, 16), (0, 32))
 UNUSED = 128
-
-
-def sort_kernel(rows, cols, count, x, lists):
+LISTS = 1024
+
+
+def sort_kernel(rows, cols, count, x, out, lists, sem):
     slots = rows.shape[0]
     second = slots + GROUP
 
@@ -84,6 +85,9 @@
     lax.fori_loop(0, GROUP, fill, 0)
     lists[2 * second] = a
     lists[2 * second + 1] = b - second
+    copy = pltpu.make_async_copy(lists, out.at[pl.ds(0, LISTS)], sem)
+    copy.start()
+    copy.wait()
 
 
 def sort_tiles(*operands):
@@ -91,8 +95,9 @@
     return pl.pallas_call(
         sort_kernel,
         in_specs=[smem] * 4,
-        out_specs=smem,
-        out_shape=jax.ShapeDtypeStruct((2 * (operands[0].shape[0] + GROUP) + 2,), jnp.int32),
+        out_specs=pl.BlockSpec(memory_space=pl.ANY),
+        out_shape=jax.ShapeDtypeStruct((2**24,), jnp.int32),
+        scratch_shapes=[pltpu.SMEM((LISTS,), jnp.int32), pltpu.SemaphoreType.DMA],
         cost_estimate=pl.CostEstimate(flops=0, bytes_accessed=2**12, transcendentals=0),
     )(*operands)
 
@@ -106,7 +111,7 @@
     spec = pl.BlockSpec(memory_space=pltpu.VMEM)
     return pl.pallas_call(
         join_kernel,
-        in_specs=[pl.BlockSpec(memory_space=pltpu.SMEM)] + [spec] * len(parts),
+        in_specs=[pl.BlockSpec(memory_space=pl.ANY)] + [spec] * len(parts),
         out_specs=spec,
         out_shape=jax.ShapeDtypeStruct((16 * len(parts), parts[0].shape[1]), BF16),
         compiler_params=pltpu.CompilerParams(vmem_limit_bytes=4 * 2**20),
@@ -114,8 +119,16 @@
     )(token, *parts)
 
 
-def tile_kernel(which, placed, codes, meta, source, mine, other, *rest):
-    outs, (tiles, wide, acc, sems) = rest[: len(placed)], rest[len(placed) :]
+def tile_kernel(which, placed, lists, meta, source, mine, other, *rest):
+    outs, (codes, tiles, wide, acc, list_sem, sems) = rest[: len(placed)], rest[len(placed) :]
+    listed = pltpu.make_async_copy(lists.at[pl.ds(0, LISTS)], codes, list_sem)
+    listed.start()
+    for part, dist in enumerate((0,) + DISTS):
+        y_of = (meta[0] - dist) & (YS - 1)
+        for ref, core in ((mine, meta[1]), (other, 1 - meta[1])):
+            at = pl.multiple_of((y_of * CS + core) * 16, 16)
+            wide[pl.ds(at, 16), :] = ref[part * 16 : part * 16 + 16, :]
+    listed.wait()
     slots = source.shape[0]
     start = which * (slots + GROUP)
     groups = (codes[2 * (slots + GROUP) + which] + GROUP - 1) >> 5
@@ -127,11 +140,6 @@
         return 0
 
     lax.fori_loop(0, groups, bring, 0)
-    for part, dist in enumerate((0,) + DISTS):
-        y_of = (meta[0] - dist) & (YS - 1)
-        for ref, core in ((mine, meta[1]), (other, 1 - meta[1])):
-            at = pl.multiple_of((y_of * CS + core) * 16, 16)
-            wide[pl.ds(at, 16), :] = ref[part * 16 : part * 16 + 16, :]
     for first, size in placed:
 
         def clear(i, _):
@@ -168,12 +176,14 @@
     smem, vmem = pl.BlockSpec(memory_space=pltpu.SMEM), pl.BlockSpec(memory_space=pltpu.VMEM)
     return pl.pallas_call(
         functools.partial(tile_kernel, which, placed),
-        in_specs=[smem] * 2 + [pl.BlockSpec(memory_space=pl.ANY)] + [vmem] * 2,
+        in_specs=[pl.BlockSpec(memory_space=pl.ANY), smem, pl.BlockSpec(memory_space=pl.ANY)] + [vmem] * 2,
         out_specs=[vmem] * len(placed),
         scratch_shapes=[
+            pltpu.SMEM((LISTS,), jnp.int32),
             pltpu.VMEM(tiles.shape, BF16),
             pltpu.VMEM((T, mine.shape[1]), BF16),
             pltpu.VMEM((129, T, T), F32),
+            pltpu.SemaphoreType.DMA,
             pltpu.SemaphoreType.DMA((tiles.shape[0] // GROUP,)),
         ],
         out_shape=[jax.ShapeDtypeStruct((n, T, T), BF16) for _, n in placed],
@@ -206,10 +216,10 @@
 
 
 def last_kernel(aggregate, weight, grad, more, importance, delta, input_grad, importance_out):
+    importance_out[...] = importance[...] - (grad[...] + more[...]) * delta[...]
     for q in range(4):
         product = jnp.dot(weight[...], aggregate[q], preferred_element_type=F32)
         input_grad[q * T : q * T + T, :] = product.T.astype(BF16)
-    importance_out[...] = importance[...] - (grad[...] + more[...]) * delta[...]
 
 
 def last(*operands):
@@ -252,7 +262,7 @@
     grad = grad + swap(grad)
     grad = grad + shift(grad, "y", YS, 2) + shift(grad, "y", YS, 1) + shift(grad, "y", YS, 3)
     grad = grad + shift(grad, "x", XS, 2) + shift(grad, "x", XS, 1) + shift(grad, "x", XS, 3)
-    grad = spread(grad, "z", ZS, ((4, None), (3, 5), (2, 6), (1, 7)), core)
+    grad = spread(grad, "z", ZS, ((1, 7), (2, 6), (3, 5), (4, None)), core)
     return last(aggregate, weight, grad, swap(grad), importance, weight_delta)
 
 

time: 119 us -> 116 us (0.975)
  starting transfers between devices: 36.6 us -> 34.9 us
  Pallas kernels: 15.9 us -> 17.4 us
  local copies, waits for them, and re-layouts: 3.52 us -> 2.14 us
    pallas_call x4, Pallas kernels: 13.4 us -> 15 us  [the longest x2 11.4 us: tile_products(): pl.pallas_call(functools.partial(tile_kernel, which, placed), in_specs=[p...]
    unnamed x16 -> x10, local copies, waits for them, and re-layouts: 3.52 us -> 2.14 us
  transfers between devices with their start and end apart: 24 -> 24, of which waited for: 16 -> 15; matrix products, arithmetic and copies ran while one was open for 2% -> 2% of each run, Pallas kernels for 11% -> 13%
where the time goes in v5:
time: 116 us
  waiting for transfers between devices  43.3 us (37%)
  starting transfers between devices  34.9 us (30%)
  Pallas kernels  17.4 us (15%)
  between operations  14.9 us (13%)
  other arithmetic  3.03 us (3%)
  local copies, waits for them, and re-layouts  2.14 us (2%)
    ppermute x15, starting transfers between devices, shift(): lax.ppermute(value, axis, [(i, (i + by) % size) for i in range(size)])  23.4 us
    all_gather x1, waiting for transfers between devices, local(): lax.all_gather(features, 'z', axis=0, tiled=True).reshape(ZS * 4, T, T)  13.9 us
    ppermute x15, waiting for transfers between devices, shift(): lax.ppermute(value, axis, [(i, (i + by) % size) for i in range(size)])  12.9 us
    pallas_call x2, Pallas kernels, tile_products(): pl.pallas_call(functools.partial(tile_kernel, which, placed), in_specs=[p...  11.4 us
    ppermute x4, starting transfers between devices, spread(): total = total + lax.ppermute(value, (axis, 'core'), pairs)  11.1 us
    ppermute x4, waiting for transfers between devices, spread(): total = total + lax.ppermute(value, (axis, 'core'), pairs)  8.28 us
    ppermute x3, waiting for transfers between devices, swap(): return lax.ppermute(value, 'core', [(0, 1), (1, 0)])  4.23 us
    reduce_scatter x1, waiting for transfers between devices, local(): aggregate = lax.psum_scatter(reduced, 'z', scatter_dimension=0, tiled=True)  3.86 us
  transfers between devices with their start and end apart: 24, of which 15 were waited for; matrix products, arithmetic and copies ran while one was open for 2% of the time, Pallas kernels for 13%

profile of v5, /device:TPU:32, one launch (start us, length us, event | category | flops | bytes accessed | tf_op | source)
XLA Modules:
  0.0 115.6 jit_solution(291188002977692863)
XLA Ops:
  7.2 0.0 all-gather.2.cloned.1.call-start
  7.2 1.0 fusion.refs_0_
  8.2 3.3 %collective-permute-start = (bf16[16,4096]{1,0:T(8,128)(2,1)S(1)}, bf16[16,4096]{1,0:T(8,128)(2,1)S(1)}, u32[]{:S(2)}, u32[]{:S(2)}) collective-permute-start(bf16[16,4096]{1,0:T(8,128)(2,1)S(1)} %fusion.refs_0_), channel_id=1, source_target_pairs={{0,4},{2,6},{4,0},{6,2},{1,5},{3,7},{5,1},{7,3},{8,12},{10,14},{12... | collective-permute-start | bytes 393224 | tf_op jit(solution)/shard_map/ppermute | solution.py:17
  11.5 0.7 collective-permute-start.1
  12.2 2.6 %collective-permute-start.2 = (bf16[16,4096]{1,0:T(8,128)(2,1)S(1)}, bf16[16,4096]{1,0:T(8,128)(2,1)S(1)}, u32[]{:S(2)}, u32[]{:S(2)}) collective-permute-start(bf16[16,4096]{1,0:T(8,128)(2,1)S(1)} %fusion.refs_0_), channel_id=1, source_target_pairs={{0,6},{2,0},{4,2},{6,4},{1,7},{3,1},{5,3},{7,5},{8,14},{10,8},{12,... | collective-permute-start | bytes 393224 | tf_op jit(solution)/shard_map/ppermute | solution.py:17
  15.4 3.5 %shard_map.113.token.lists = s32[16777216]{0:T(1024)} custom-call(s32[256]{0:T(256)} %bitcast.14, s32[256]{0:T(256)} %bitcast.15, s32[1]{0:T(128)} %bitcast.10.count, s32[1]{0:T(128)} %bitcast.3.x), custom_call_target="tpu_custom_call" | custom-call | bytes 4096 | tf_op jit(solution)/shard_map/pallas_call | solution.py:95
  18.9 0.0 collective-permute-done.refs_1_
  18.9 0.0 collective-permute-done.1.refs_2_
  18.9 0.0 collective-permute-done.2.refs_3_
  19.0 0.1 collective-permute-start.3
  19.1 0.0 all-gather.2.cloned.1.call-update
  19.1 0.0 reduce-scatter.2.cloned.1.call-start
  19.2 0.1 pad_add_fusion.meta
  19.2 1.7 %collective-permute-done.3.other = bf16[64,4096]{1,0:T(8,128)(2,1)S(1)} collective-permute-done((bf16[64,4096]{1,0:T(8,128)(2,1)S(1)}, bf16[64,4096]{1,0:T(8,128)(2,1)S(1)}, u32[]{:S(2)}, u32[]{:S(2)}) %collective-permute-start.3) | collective-permute-done | bytes 524320 | tf_op jit(solution)/shard_map/ppermute | solution.py:21
  21.0 4.4 %shard_map.117 = (bf16[16,128,128]{2,1,0:T(8,128)(2,1)S(1)}, bf16[16,128,128]{2,1,0:T(8,128)(2,1)S(1)}) custom-call(s32[16777216]{0:T(1024)} %shard_map.113.token.lists, s32[2]{0:T(128)S(1)} %pad_add_fusion.meta, bf16[256,128,128]{2,1,0:T(8,128)(2,1)} %bitcast.12, bf16[64,4096]{1,0:T(8,128)(2,1)S(1)} %shard_map.114.mine, ...), custom_call_target="tpu_custom_call" | custom-call | bytes 16777216 | tf_op jit(solution)/shard_map/pallas_call | solution.py:177
  25.4 2.2 %collective-permute-start.8 = (bf16[16,128,128]{2,1,0:T(8,128)(2,1)S(1)}, bf16[16,128,128]{2,1,0:T(8,128)(2,1)S(1)}, u32[]{:S(2)}, u32[]{:S(2)}) collective-permute-start(bf16[16,128,128]{2,1,0:T(8,128)(2,1)S(1)} %get-tuple-element.17), channel_id=1, source_target_pairs={{0,192},{64,0},{128,64},{192,128},{1,193},{65,1},{129,65},{193,129... | collective-permute-start | bytes 1572872 | tf_op jit(solution)/shard_map/ppermute | solution.py:17
  27.5 0.0 collective-permute-start.4
  27.5 7.1 %shard_map.115 = (bf16[16,128,128]{2,1,0:T(8,128)(2,1)}, bf16[16,128,128]{2,1,0:T(8,128)(2,1)}, bf16[16,128,128]{2,1,0:T(8,128)(2,1)S(1)}, bf16[16,128,128]{2,1,0:T(8,128)(2,1)S(1)}, bf16[32,128,128]{2,1,0:T(8,128)(2,1)S(1)}) custom-call(s32[16777216]{0:T(1024)} %shard_map.113.token.lists, s32[2]{0:T(128)S(1)} %pad_add_fusion.meta, ...), custom_call_target="tpu_custom_call" | custom-call | bytes 16777216 | tf_op jit(solution)/shard_map/pallas_call | solution.py:177
  34.6 0.8 collective-permute-start.6
  35.4 2.6 %collective-permute-start.7 = (bf16[16,128,128]{2,1,0:T(8,128)(2,1)}, bf16[16,128,128]{2,1,0:T(8,128)(2,1)S(1)}, u32[]{:S(2)}, u32[]{:S(2)}) collective-permute-start(bf16[16,128,128]{2,1,0:T(8,128)(2,1)} %get-tuple-element.15), channel_id=1, source_target_pairs={{0,192},{64,0},{128,64},{192,128},{1,193},{65,1},{129,65},{193,129... | collective-permute-start | bytes 1572872 | tf_op jit(solution)/shard_map/ppermute | solution.py:17
  38.0 1.8 %collective-permute-done.8 = bf16[16,128,128]{2,1,0:T(8,128)(2,1)S(1)} collective-permute-done((bf16[16,128,128]{2,1,0:T(8,128)(2,1)S(1)}, bf16[16,128,128]{2,1,0:T(8,128)(2,1)S(1)}, u32[]{:S(2)}, u32[]{:S(2)}) %collective-permute-start.8) | collective-permute-done | bytes 524320 | tf_op jit(solution)/shard_map/ppermute | solution.py:17
  39.8 0.9 add_convert_fusion
  40.7 3.7 %collective-permute-start.9 = (bf16[16,128,128]{2,1,0:T(8,128)(2,1)}, bf16[16,128,128]{2,1,0:T(8,128)(2,1)S(1)}, u32[]{:S(2)}, u32[]{:S(2)}) collective-permute-start(bf16[16,128,128]{2,1,0:T(8,128)(2,1)} %add_convert_fusion), channel_id=1, source_target_pairs={{0,192},{64,0},{128,64},{192,128},{1,193},{65,1},{129,65},{193,129... | collective-permute-start | bytes 1572872 | tf_op jit(solution)/shard_map/ppermute | solution.py:17
  44.4 0.0 collective-permute-done.4
  44.4 0.9 add_convert_fusion.1
  45.3 0.0 collective-permute-start.5
  45.3 0.1 shard_map.116.c0
  45.4 13.9 %all-gather.2.cloned.1.call-done = bf16[4096,128]{1,0:T(8,128)(2,1)} async-done(((bf16[512,128]{1,0:T(8,128)(2,1)}), bf16[4096,128]{1,0:T(8,128)(2,1)}) %all-gather.2.cloned.1.call-update) | async-done | bytes 1048592 | tf_op jit(solution)/shard_map/all_gather | solution.py:244
  59.4 1.2 %copy-done = bf16[4096,128]{1,0:T(8,128)(2,1)S(1)} copy-done((bf16[4096,128]{1,0:T(8,128)(2,1)S(1)}, bf16[4096,128]{1,0:T(8,128)(2,1)}, u32[]{:S(2)}) %copy-start) | copy-done | bytes 1048600
  60.6 0.1 shard_map.118.feats
  60.7 0.0 collective-permute-done.6.upb
  60.7 0.0 collective-permute-done.7.downa
  60.7 1.3 %collective-permute-done.9.downb = bf16[16,128,128]{2,1,0:T(8,128)(2,1)S(1)} collective-permute-done((bf16[16,128,128]{2,1,0:T(8,128)(2,1)}, bf16[16,128,128]{2,1,0:T(8,128)(2,1)S(1)}, u32[]{:S(2)}, u32[]{:S(2)}) %collective-permute-start.9) | collective-permute-done | bytes 524320 | tf_op jit(solution)/shard_map/ppermute | solution.py:17
  62.0 3.3 %collective-permute-done.5.upa = bf16[16,128,128]{2,1,0:T(8,128)(2,1)S(1)} collective-permute-done((bf16[16,128,128]{2,1,0:T(8,128)(2,1)}, bf16[16,128,128]{2,1,0:T(8,128)(2,1)S(1)}, u32[]{:S(2)}, u32[]{:S(2)}) %collective-permute-start.5) | collective-permute-done | bytes 524320 | tf_op jit(solution)/shard_map/ppermute | solution.py:17
  65.3 1.4 %shard_map.119 = (bf16[32,128,128]{2,1,0:T(8,128)(2,1)}, f32[128,128]{1,0:T(8,128)S(1)}) custom-call(bf16[32,128,128]{2,1,0:T(8,128)(2,1)S(1)} %shard_map.116.c0, bf16[16,128,128]{2,1,0:T(8,128)(2,1)S(1)} %collective-permute-done.5.upa, bf16[16,128,128]{2,1,0:T(8,128)(2,1)S(1)} %collective-permute-done.6.upb, ...), custom_call_target="tpu_custom_call" | custom-call | flops 134217728 | bytes 5242880 | tf_op jit(solution)/shard_map/pallas_call | solution.py:208
  66.7 0.0 reduce-scatter.2.cloned.1.call-update
  66.7 0.1 collective-permute-start.10
  66.8 1.2 %collective-permute-done.10 = f32[128,128]{1,0:T(8,128)S(1)} collective-permute-done((f32[128,128]{1,0:T(8,128)S(1)}, f32[128,128]{1,0:T(8,128)S(1)}, u32[]{:S(2)}, u32[]{:S(2)}) %collective-permute-start.10) | collective-permute-done | bytes 65568 | tf_op jit(solution)/shard_map/ppermute | solution.py:21
  68.1 1.0 collective-permute-start.11
  69.1 2.6 %collective-permute-start.12 = (f32[128,128]{1,0:T(8,128)S(1)}, f32[128,128]{1,0:T(8,128)S(1)}, u32[]{:S(2)}, u32[]{:S(2)}) collective-permute-start(f32[128,128]{1,0:T(8,128)S(1)} %add.43), channel_id=1, source_target_pairs={{0,2},{2,4},{4,6},{6,0},{1,3},{3,5},{5,7},{7,1},{8,10},{10,12},{12... | collective-permute-start | bytes 196616 | tf_op jit(solution)/shard_map/ppermute | solution.py:17
  71.7 0.6 collective-permute-start.13
  72.3 2.3 %collective-permute-done.11 = f32[128,128]{1,0:T(8,128)S(1)} collective-permute-done((f32[128,128]{1,0:T(8,128)S(1)}, f32[128,128]{1,0:T(8,128)S(1)}, u32[]{:S(2)}, u32[]{:S(2)}) %collective-permute-start.11) | collective-permute-done | bytes 65568 | tf_op jit(solution)/shard_map/ppermute | solution.py:17
  74.6 0.6 collective-permute-done.12
  75.2 0.7 collective-permute-done.13
  76.0 0.1 collective-permute-start.14
  76.1 1.0 collective-permute-start.15
  77.0 2.4 %collective-permute-start.16 = (f32[128,128]{1,0:T(8,128)S(1)}, f32[128,128]{1,0:T(8,128)S(1)}, u32[]{:S(2)}, u32[]{:S(2)}) collective-permute-start(f32[128,128]{1,0:T(8,128)S(1)} %add_add_fusion.2), channel_id=1, source_target_pairs={{0,192},{64,0},{128,64},{192,128},{1,193},{65,1},{129,65},{193,129... | collective-permute-start | bytes 196616 | tf_op jit(solution)/shard_map/ppermute | solution.py:17
  79.4 2.5 %collective-permute-done.14 = f32[128,128]{1,0:T(8,128)S(1)} collective-permute-done((f32[128,128]{1,0:T(8,128)S(1)}, f32[128,128]{1,0:T(8,128)S(1)}, u32[]{:S(2)}, u32[]{:S(2)}) %collective-permute-start.14) | collective-permute-done | bytes 65568 | tf_op jit(solution)/shard_map/ppermute | solution.py:17
  81.9 0.4 collective-permute-done.15
  82.3 0.0 collective-permute-done.16
  82.3 1.0 collective-permute-start.17
  83.3 4.5 %collective-permute-start.18 = (f32[128,128]{1,0:T(8,128)S(1)}, f32[128,128]{1,0:T(8,128)S(1)}, u32[]{:S(2)}, u32[]{:S(2)}) collective-permute-start(f32[128,128]{1,0:T(8,128)S(1)} %add_add_fusion.1), channel_id=1, source_target_pairs={{0,16},{8,24},{16,32},{24,40},{32,48},{40,56},{48,0},{56,8},{1,49}... | collective-permute-start | bytes 196616 | tf_op jit(solution)/shard_map/ppermute | solution.py:30
  87.8 2.8 %collective-permute-start.19 = (f32[128,128]{1,0:T(8,128)S(1)}, f32[128,128]{1,0:T(8,128)S(1)}, u32[]{:S(2)}, u32[]{:S(2)}) collective-permute-start(f32[128,128]{1,0:T(8,128)S(1)} %add_add_fusion.1), channel_id=1, source_target_pairs={{0,24},{8,32},{16,40},{24,48},{32,56},{40,0},{48,8},{56,16},{1,41}... | collective-permute-start | bytes 196616 | tf_op jit(solution)/shard_map/ppermute | solution.py:30
  90.5 2.9 %collective-permute-start.20 = (f32[128,128]{1,0:T(8,128)S(1)}, f32[128,128]{1,0:T(8,128)S(1)}, u32[]{:S(2)}, u32[]{:S(2)}) collective-permute-start(f32[128,128]{1,0:T(8,128)S(1)} %add_add_fusion.1), channel_id=1, source_target_pairs={{0,32},{8,40},{16,48},{24,56},{32,0},{40,8},{48,16},{56,24},{2,34}... | collective-permute-start | bytes 196616 | tf_op jit(solution)/shard_map/ppermute | solution.py:30
  93.4 0.0 collective-permute-done.17
  93.4 0.0 collective-permute-done.18
  93.4 3.4 %collective-permute-done.19 = f32[128,128]{1,0:T(8,128)S(1)} collective-permute-done((f32[128,128]{1,0:T(8,128)S(1)}, f32[128,128]{1,0:T(8,128)S(1)}, u32[]{:S(2)}, u32[]{:S(2)}) %collective-permute-start.19) | collective-permute-done | bytes 65568 | tf_op jit(solution)/shard_map/ppermute | solution.py:30
  96.9 4.8 %collective-permute-done.20 = f32[128,128]{1,0:T(8,128)S(1)} collective-permute-done((f32[128,128]{1,0:T(8,128)S(1)}, f32[128,128]{1,0:T(8,128)S(1)}, u32[]{:S(2)}, u32[]{:S(2)}) %collective-permute-start.20) | collective-permute-done | bytes 65568 | tf_op jit(solution)/shard_map/ppermute | solution.py:30
  101.7 0.1 collective-permute-start.21
  101.8 1.2 %collective-permute-done.21.more = f32[128,128]{1,0:T(8,128)S(1)} collective-permute-done((f32[128,128]{1,0:T(8,128)S(1)}, f32[128,128]{1,0:T(8,128)S(1)}, u32[]{:S(2)}, u32[]{:S(2)}) %collective-permute-start.21) | collective-permute-done | bytes 65568 | tf_op jit(solution)/shard_map/ppermute | solution.py:21
  103.1 3.9 %reduce-scatter.2.cloned.1.call-done.aggregate = bf16[4,128,128]{2,1,0:T(8,128)(2,1)} async-done(((bf16[32,128,128]{2,1,0:T(8,128)(2,1)}), bf16[4,128,128]{2,1,0:T(8,128)(2,1)}) %reduce-scatter.2.cloned.1.call-update) | async-done | bytes 131088 | tf_op jit(solution)/shard_map/reduce_scatter | solution.py:260
  106.9 0.0 copy-done.2
  107.0 0.9 copy-done.1
  107.9 0.9 shard_map.120
  (12 shorter events, 0.1 us)
Async XLA Ops:
  7.2 52.2 %all-gather.2.cloned.1.call-start = ((), (), s32[]{:S(2)}) async-start(), calls=%async_computation.1 | async-start | bytes 1179648 | tf_op jit(solution)/shard_map/all_gather | solution.py:244
  8.2 10.7 %collective-permute-start = (bf16[16,4096]{1,0:T(8,128)(2,1)S(1)}, bf16[16,4096]{1,0:T(8,128)(2,1)S(1)}, u32[]{:S(2)}, u32[]{:S(2)}) collective-permute-start(bf16[16,4096]{1,0:T(8,128)(2,1)S(1)} %fusion.refs_0_), channel_id=1, source_target_pairs={{0,4},{2,6},{4,0},{6,2},{1,5},{3,7},{5,1},{7,3},{8,12},{10,14},{12... | collective-permute-start | bytes 393224 | tf_op jit(solution)/shard_map/ppermute | solution.py:17
  11.5 7.4 %collective-permute-start.1 = (bf16[16,4096]{1,0:T(8,128)(2,1)S(1)}, bf16[16,4096]{1,0:T(8,128)(2,1)S(1)}, u32[]{:S(2)}, u32[]{:S(2)}) collective-permute-start(bf16[16,4096]{1,0:T(8,128)(2,1)S(1)} %fusion.refs_0_), channel_id=1, source_target_pairs={{0,2},{2,4},{4,6},{6,0},{1,3},{3,5},{5,7},{7,1},{8,10},{10,12},{12... | collective-permute-start | bytes 393224 | tf_op jit(solution)/shard_map/ppermute | solution.py:17
  12.2 6.7 %collective-permute-start.2 = (bf16[16,4096]{1,0:T(8,128)(2,1)S(1)}, bf16[16,4096]{1,0:T(8,128)(2,1)S(1)}, u32[]{:S(2)}, u32[]{:S(2)}) collective-permute-start(bf16[16,4096]{1,0:T(8,128)(2,1)S(1)} %fusion.refs_0_), channel_id=1, source_target_pairs={{0,6},{2,0},{4,2},{6,4},{1,7},{3,1},{5,3},{7,5},{8,14},{10,8},{12,... | collective-permute-start | bytes 393224 | tf_op jit(solution)/shard_map/ppermute | solution.py:17
  19.0 2.0 %collective-permute-start.3 = (bf16[64,4096]{1,0:T(8,128)(2,1)S(1)}, bf16[64,4096]{1,0:T(8,128)(2,1)S(1)}, u32[]{:S(2)}, u32[]{:S(2)}) collective-permute-start(bf16[64,4096]{1,0:T(8,128)(2,1)S(1)} %shard_map.114.mine), channel_id=1, source_target_pairs={{0,1},{1,0},{2,3},{3,2},{4,5},{5,4},{6,7},{7,6},{8,9},{9,8},{10,11... | collective-permute-start | bytes 1572872 | tf_op jit(solution)/shard_map/ppermute | solution.py:21
  19.1 87.8 %reduce-scatter.2.cloned.1.call-start = ((), (), s32[]{:S(2)}) async-start(), calls=%async_computation.2 | async-start | bytes 1179648 | tf_op jit(solution)/shard_map/reduce_scatter | solution.py:260
  21.0 86.0 %copy-start.2 = (f32[128,128]{1,0:T(8,128)S(1)}, f32[128,128]{1,0:T(8,128)}, u32[]{:S(2)}) copy-start(f32[128,128]{1,0:T(8,128)} %importance.1) | copy-start | bytes 196612
  21.0 86.0 %copy-start.3 = (f32[128,128]{1,0:T(8,128)S(1)}, f32[128,128]{1,0:T(8,128)}, u32[]{:S(2)}) copy-start(f32[128,128]{1,0:T(8,128)} %delta.1) | copy-start | bytes 196612
  21.0 86.0 %copy-start.4 = (bf16[128,128]{1,0:T(8,128)(2,1)S(1)}, bf16[128,128]{1,0:T(8,128)(2,1)}, u32[]{:S(2)}) copy-start(bf16[128,128]{1,0:T(8,128)(2,1)} %weight.1) | copy-start | bytes 98308
  25.4 14.4 %collective-permute-start.8 = (bf16[16,128,128]{2,1,0:T(8,128)(2,1)S(1)}, bf16[16,128,128]{2,1,0:T(8,128)(2,1)S(1)}, u32[]{:S(2)}, u32[]{:S(2)}) collective-permute-start(bf16[16,128,128]{2,1,0:T(8,128)(2,1)S(1)} %get-tuple-element.17), channel_id=1, source_target_pairs={{0,192},{64,0},{128,64},{192,128},{1,193},{65,1},{129,65},{193,129... | collective-permute-start | bytes 1572872 | tf_op jit(solution)/shard_map/ppermute | solution.py:17
  27.5 16.9 %collective-permute-start.4 = (bf16[16,128,128]{2,1,0:T(8,128)(2,1)S(1)}, bf16[16,128,128]{2,1,0:T(8,128)(2,1)S(1)}, u32[]{:S(2)}, u32[]{:S(2)}) collective-permute-start(bf16[16,128,128]{2,1,0:T(8,128)(2,1)S(1)} %get-tuple-element.13), channel_id=1, source_target_pairs={{0,64},{64,128},{128,192},{192,0},{1,65},{65,129},{129,193},{193,1... | collective-permute-start | bytes 1572872 | tf_op jit(solution)/shard_map/ppermute | solution.py:17
  34.6 26.1 %collective-permute-start.6 = (bf16[16,128,128]{2,1,0:T(8,128)(2,1)}, bf16[16,128,128]{2,1,0:T(8,128)(2,1)S(1)}, u32[]{:S(2)}, u32[]{:S(2)}) collective-permute-start(bf16[16,128,128]{2,1,0:T(8,128)(2,1)} %get-tuple-element.14), channel_id=1, source_target_pairs={{0,64},{64,128},{128,192},{192,0},{1,65},{65,129},{129,193},{193,1... | collective-permute-start | bytes 1572872 | tf_op jit(solution)/shard_map/ppermute | solution.py:17
  35.4 25.3 %collective-permute-start.7 = (bf16[16,128,128]{2,1,0:T(8,128)(2,1)}, bf16[16,128,128]{2,1,0:T(8,128)(2,1)S(1)}, u32[]{:S(2)}, u32[]{:S(2)}) collective-permute-start(bf16[16,128,128]{2,1,0:T(8,128)(2,1)} %get-tuple-element.15), channel_id=1, source_target_pairs={{0,192},{64,0},{128,64},{192,128},{1,193},{65,1},{129,65},{193,129... | collective-permute-start | bytes 1572872 | tf_op jit(solution)/shard_map/ppermute | solution.py:17
  40.7 21.3 %collective-permute-start.9 = (bf16[16,128,128]{2,1,0:T(8,128)(2,1)}, bf16[16,128,128]{2,1,0:T(8,128)(2,1)S(1)}, u32[]{:S(2)}, u32[]{:S(2)}) collective-permute-start(bf16[16,128,128]{2,1,0:T(8,128)(2,1)} %add_convert_fusion), channel_id=1, source_target_pairs={{0,192},{64,0},{128,64},{192,128},{1,193},{65,1},{129,65},{193,129... | collective-permute-start | bytes 1572872 | tf_op jit(solution)/shard_map/ppermute | solution.py:17
  45.3 20.0 %collective-permute-start.5 = (bf16[16,128,128]{2,1,0:T(8,128)(2,1)}, bf16[16,128,128]{2,1,0:T(8,128)(2,1)S(1)}, u32[]{:S(2)}, u32[]{:S(2)}) collective-permute-start(bf16[16,128,128]{2,1,0:T(8,128)(2,1)} %add_convert_fusion.1), channel_id=1, source_target_pairs={{0,64},{64,128},{128,192},{192,0},{1,65},{65,129},{129,193},{193,1... | collective-permute-start | bytes 1572872 | tf_op jit(solution)/shard_map/ppermute | solution.py:17
  59.4 1.2 %copy-start = (bf16[4096,128]{1,0:T(8,128)(2,1)S(1)}, bf16[4096,128]{1,0:T(8,128)(2,1)}, u32[]{:S(2)}) copy-start(bf16[4096,128]{1,0:T(8,128)(2,1)} %all-gather.2.cloned.1.call-done) | copy-start | bytes 3145732
  66.7 1.3 %collective-permute-start.10 = (f32[128,128]{1,0:T(8,128)S(1)}, f32[128,128]{1,0:T(8,128)S(1)}, u32[]{:S(2)}, u32[]{:S(2)}) collective-permute-start(f32[128,128]{1,0:T(8,128)S(1)} %get-tuple-element.19), channel_id=1, source_target_pairs={{0,1},{1,0},{2,3},{3,2},{4,5},{5,4},{6,7},{7,6},{8,9},{9,8},{10,11... | collective-permute-start | bytes 196616 | tf_op jit(solution)/shard_map/ppermute | solution.py:21
  68.1 6.5 %collective-permute-start.11 = (f32[128,128]{1,0:T(8,128)S(1)}, f32[128,128]{1,0:T(8,128)S(1)}, u32[]{:S(2)}, u32[]{:S(2)}) collective-permute-start(f32[128,128]{1,0:T(8,128)S(1)} %add.43), channel_id=1, source_target_pairs={{0,4},{2,6},{4,0},{6,2},{1,5},{3,7},{5,1},{7,3},{8,12},{10,14},{12... | collective-permute-start | bytes 196616 | tf_op jit(solution)/shard_map/ppermute | solution.py:17
  69.1 6.1 %collective-permute-start.12 = (f32[128,128]{1,0:T(8,128)S(1)}, f32[128,128]{1,0:T(8,128)S(1)}, u32[]{:S(2)}, u32[]{:S(2)}) collective-permute-start(f32[128,128]{1,0:T(8,128)S(1)} %add.43), channel_id=1, source_target_pairs={{0,2},{2,4},{4,6},{6,0},{1,3},{3,5},{5,7},{7,1},{8,10},{10,12},{12... | collective-permute-start | bytes 196616 | tf_op jit(solution)/shard_map/ppermute | solution.py:17
  71.7 4.3 %collective-permute-start.13 = (f32[128,128]{1,0:T(8,128)S(1)}, f32[128,128]{1,0:T(8,128)S(1)}, u32[]{:S(2)}, u32[]{:S(2)}) collective-permute-start(f32[128,128]{1,0:T(8,128)S(1)} %add.43), channel_id=1, source_target_pairs={{0,6},{2,0},{4,2},{6,4},{1,7},{3,1},{5,3},{7,5},{8,14},{10,8},{12,... | collective-permute-start | bytes 196616 | tf_op jit(solution)/shard_map/ppermute | solution.py:17
  76.0 6.0 %collective-permute-start.14 = (f32[128,128]{1,0:T(8,128)S(1)}, f32[128,128]{1,0:T(8,128)S(1)}, u32[]{:S(2)}, u32[]{:S(2)}) collective-permute-start(f32[128,128]{1,0:T(8,128)S(1)} %add_add_fusion.2), channel_id=1, source_target_pairs={{0,128},{64,192},{128,0},{192,64},{1,129},{65,193},{129,1},{193,65... | collective-permute-start | bytes 196616 | tf_op jit(solution)/shard_map/ppermute | solution.py:17
  76.1 6.3 %collective-permute-start.15 = (f32[128,128]{1,0:T(8,128)S(1)}, f32[128,128]{1,0:T(8,128)S(1)}, u32[]{:S(2)}, u32[]{:S(2)}) collective-permute-start(f32[128,128]{1,0:T(8,128)S(1)} %add_add_fusion.2), channel_id=1, source_target_pairs={{0,64},{64,128},{128,192},{192,0},{1,65},{65,129},{129,193},{193,1... | collective-permute-start | bytes 196616 | tf_op jit(solution)/shard_map/ppermute | solution.py:17
  77.0 5.3 %collective-permute-start.16 = (f32[128,128]{1,0:T(8,128)S(1)}, f32[128,128]{1,0:T(8,128)S(1)}, u32[]{:S(2)}, u32[]{:S(2)}) collective-permute-start(f32[128,128]{1,0:T(8,128)S(1)} %add_add_fusion.2), channel_id=1, source_target_pairs={{0,192},{64,0},{128,64},{192,128},{1,193},{65,1},{129,65},{193,129... | collective-permute-start | bytes 196616 | tf_op jit(solution)/shard_map/ppermute | solution.py:17
  82.3 11.1 %collective-permute-start.17 = (f32[128,128]{1,0:T(8,128)S(1)}, f32[128,128]{1,0:T(8,128)S(1)}, u32[]{:S(2)}, u32[]{:S(2)}) collective-permute-start(f32[128,128]{1,0:T(8,128)S(1)} %add_add_fusion.1), channel_id=1, source_target_pairs={{0,8},{8,16},{16,24},{24,32},{32,40},{40,48},{48,56},{56,0},{1,57}... | collective-permute-start | bytes 196616 | tf_op jit(solution)/shard_map/ppermute | solution.py:30
  83.3 10.1 %collective-permute-start.18 = (f32[128,128]{1,0:T(8,128)S(1)}, f32[128,128]{1,0:T(8,128)S(1)}, u32[]{:S(2)}, u32[]{:S(2)}) collective-permute-start(f32[128,128]{1,0:T(8,128)S(1)} %add_add_fusion.1), channel_id=1, source_target_pairs={{0,16},{8,24},{16,32},{24,40},{32,48},{40,56},{48,0},{56,8},{1,49}... | collective-permute-start | bytes 196616 | tf_op jit(solution)/shard_map/ppermute | solution.py:30
  87.8 9.1 %collective-permute-start.19 = (f32[128,128]{1,0:T(8,128)S(1)}, f32[128,128]{1,0:T(8,128)S(1)}, u32[]{:S(2)}, u32[]{:S(2)}) collective-permute-start(f32[128,128]{1,0:T(8,128)S(1)} %add_add_fusion.1), channel_id=1, source_target_pairs={{0,24},{8,32},{16,40},{24,48},{32,56},{40,0},{48,8},{56,16},{1,41}... | collective-permute-start | bytes 196616 | tf_op jit(solution)/shard_map/ppermute | solution.py:30
  90.5 11.2 %collective-permute-start.20 = (f32[128,128]{1,0:T(8,128)S(1)}, f32[128,128]{1,0:T(8,128)S(1)}, u32[]{:S(2)}, u32[]{:S(2)}) collective-permute-start(f32[128,128]{1,0:T(8,128)S(1)} %add_add_fusion.1), channel_id=1, source_target_pairs={{0,32},{8,40},{16,48},{24,56},{32,0},{40,8},{48,16},{56,24},{2,34}... | collective-permute-start | bytes 196616 | tf_op jit(solution)/shard_map/ppermute | solution.py:30
  101.7 1.3 %collective-permute-start.21 = (f32[128,128]{1,0:T(8,128)S(1)}, f32[128,128]{1,0:T(8,128)S(1)}, u32[]{:S(2)}, u32[]{:S(2)}) collective-permute-start(f32[128,128]{1,0:T(8,128)S(1)} %add_add_fusion.grad), channel_id=1, source_target_pairs={{0,1},{1,0},{2,3},{3,2},{4,5},{5,4},{6,7},{7,6},{8,9},{9,8},{10,11... | collective-permute-start | bytes 196616 | tf_op jit(solution)/shard_map/ppermute | solution.py:21
  107.0 0.9 copy-start.1
Sparse Core Ops, SparseCore 0:
  19.2 40.0 all-gather.1
  66.8 40.0 reduce-scatter.1

commit v6 on v5

--- a/solution.py
+++ b/solution.py
@@ -128,6 +128,14 @@
         for ref, core in ((mine, meta[1]), (other, 1 - meta[1])):
             at = pl.multiple_of((y_of * CS + core) * 16, 16)
             wide[pl.ds(at, 16), :] = ref[part * 16 : part * 16 + 16, :]
+    for first, size in placed:
+
+        def clear(i, _):
+            acc[pl.ds(first + i * 4, 4)] = jnp.zeros((4, T, T), F32)
+            return 0
+
+        lax.fori_loop(0, size // 4, clear, 0)
+
     listed.wait()
     slots = source.shape[0]
     start = which * (slots + GROUP)
@@ -140,14 +148,6 @@
         return 0
 
     lax.fori_loop(0, groups, bring, 0)
-    for first, size in placed:
-
-        def clear(i, _):
-            acc[pl.ds(first + i * 4, 4)] = jnp.zeros((4, T, T), F32)
-            return 0
-
-        lax.fori_loop(0, size // 4, clear, 0)
-
     def several(g, _):
         base = pl.multiple_of(g * GROUP, GROUP)
         here = tiles.at[pl.ds(base, GROUP)]
@@ -192,15 +192,22 @@
     )(codes, meta, tiles, mine, other)
 
 
-def middle_kernel(c0, upa, upb, downa, downb, feats, out, grad):
+def middle_kernel(c0, upa, upb, downa, downb, feats, out, grad, sums, sems):
+    copies = []
+    for part in range(4):
+        for k in range(part * 8, part * 8 + 8):
+            up, down = (upa, downa) if k < 16 else (upb, downb)
+            n = k % 16
+            sums[k] = (c0[k].astype(F32) + up[n].astype(F32) + down[n].astype(F32)).astype(BF16)
+        here = pl.ds(part * 8, 8)
+        copies.append(pltpu.make_async_copy(sums.at[here], out.at[here], sems.at[part]))
+        copies[-1].start()
     total = jnp.zeros((T, T), F32)
     for k in range(32):
-        up, down = (upa, downa) if k < 16 else (upb, downb)
-        n = k % 16
-        value = (c0[k].astype(F32) + up[n].astype(F32) + down[n].astype(F32)).astype(BF16)
-        out[k] = value
-        total += jnp.dot(value, feats[k], preferred_element_type=F32)
+        total += jnp.dot(sums[k], feats[k], preferred_element_type=F32)
     grad[...] = total.T
+    for copy in copies:
+        copy.wait()
 
 
 def middle(*operands):
@@ -208,8 +215,9 @@
     return pl.pallas_call(
         middle_kernel,
         in_specs=[spec] * 6,
-        out_specs=[spec] * 2,
+        out_specs=[pl.BlockSpec(memory_space=pl.ANY), spec],
         out_shape=[jax.ShapeDtypeStruct((32, T, T), BF16), jax.ShapeDtypeStruct((T, T), F32)],
+        scratch_shapes=[pltpu.VMEM((32, T, T), BF16), pltpu.SemaphoreType.DMA((4,))],
         compiler_params=pltpu.CompilerParams(vmem_limit_bytes=12 * 2**20),
         cost_estimate=pl.CostEstimate(flops=2**27, bytes_accessed=5 * 2**20, transcendentals=0),
     )(*operands)

time: 116 us -> 116 us (level)
    ppermute x4, starting transfers between devices: 11.1 us -> 12.5 us  [spread(): total = total + lax.ppermute(value, (axis, 'core'), pairs)]
where the time goes in v6:
time: 116 us; the launch traced here: 115 us
  waiting for transfers between devices  42.5 us (37%)
  starting transfers between devices  35.8 us (31%)
  Pallas kernels  17 us (15%)
  between operations  14.9 us (13%)
  other arithmetic  3.03 us (3%)
  local copies, waits for them, and re-layouts  2.14 us (2%)
    ppermute x15, starting transfers between devices, shift(): lax.ppermute(value, axis, [(i, (i + by) % size) for i in range(size)])  23 us
    all_gather x1, waiting for transfers between devices, local(): lax.all_gather(features, 'z', axis=0, tiled=True).reshape(ZS * 4, T, T)  14.2 us
    ppermute x4, starting transfers between devices, spread(): total = total + lax.ppermute(value, (axis, 'core'), pairs)  12.5 us
    ppermute x15, waiting for transfers between devices, shift(): lax.ppermute(value, axis, [(i, (i + by) % size) for i in range(size)])  12.2 us
    pallas_call x2, Pallas kernels, tile_products(): pl.pallas_call(functools.partial(tile_kernel, which, placed), in_specs=[p...  11.2 us
    ppermute x4, waiting for transfers between devices, spread(): total = total + lax.ppermute(value, (axis, 'core'), pairs)  7.14 us
    reduce_scatter x1, waiting for transfers between devices, local(): aggregate = lax.psum_scatter(reduced, 'z', scatter_dimension=0, tiled=True)  4.67 us
    ppermute x3, waiting for transfers between devices, swap(): return lax.ppermute(value, 'core', [(0, 1), (1, 0)])  4.23 us
  transfers between devices with their start and end apart: 24, of which 15 were waited for; matrix products, arithmetic and copies ran while one was open for 2% of the time, Pallas kernels for 13%

profile of v6, /device:TPU:32, one launch (start us, length us, event | category | flops | bytes accessed | tf_op | source)
XLA Modules:
  0.0 115.5 jit_solution(17166204413792551886)
XLA Ops:
  7.2 0.0 all-gather.2.cloned.1.call-start
  7.2 1.0 fusion.refs_0_
  8.2 3.3 %collective-permute-start = (bf16[16,4096]{1,0:T(8,128)(2,1)S(1)}, bf16[16,4096]{1,0:T(8,128)(2,1)S(1)}, u32[]{:S(2)}, u32[]{:S(2)}) collective-permute-start(bf16[16,4096]{1,0:T(8,128)(2,1)S(1)} %fusion.refs_0_), channel_id=1, source_target_pairs={{0,4},{2,6},{4,0},{6,2},{1,5},{3,7},{5,1},{7,3},{8,12},{10,14},{12... | collective-permute-start | bytes 393224 | tf_op jit(solution)/shard_map/ppermute | solution.py:17
  11.5 0.7 collective-permute-start.1
  12.2 2.6 %collective-permute-start.2 = (bf16[16,4096]{1,0:T(8,128)(2,1)S(1)}, bf16[16,4096]{1,0:T(8,128)(2,1)S(1)}, u32[]{:S(2)}, u32[]{:S(2)}) collective-permute-start(bf16[16,4096]{1,0:T(8,128)(2,1)S(1)} %fusion.refs_0_), channel_id=1, source_target_pairs={{0,6},{2,0},{4,2},{6,4},{1,7},{3,1},{5,3},{7,5},{8,14},{10,8},{12,... | collective-permute-start | bytes 393224 | tf_op jit(solution)/shard_map/ppermute | solution.py:17
  15.4 3.5 %shard_map.113.token.lists = s32[16777216]{0:T(1024)} custom-call(s32[256]{0:T(256)} %bitcast.14, s32[256]{0:T(256)} %bitcast.15, s32[1]{0:T(128)} %bitcast.10.count, s32[1]{0:T(128)} %bitcast.3.x), custom_call_target="tpu_custom_call" | custom-call | bytes 4096 | tf_op jit(solution)/shard_map/pallas_call | solution.py:95
  18.9 0.0 collective-permute-done.refs_1_
  18.9 0.0 collective-permute-done.1.refs_2_
  18.9 0.0 collective-permute-done.2.refs_3_
  19.0 0.1 collective-permute-start.3
  19.1 0.0 all-gather.2.cloned.1.call-update
  19.1 0.0 reduce-scatter.2.cloned.1.call-start
  19.2 0.1 pad_add_fusion.meta
  19.2 1.7 %collective-permute-done.3.other = bf16[64,4096]{1,0:T(8,128)(2,1)S(1)} collective-permute-done((bf16[64,4096]{1,0:T(8,128)(2,1)S(1)}, bf16[64,4096]{1,0:T(8,128)(2,1)S(1)}, u32[]{:S(2)}, u32[]{:S(2)}) %collective-permute-start.3) | collective-permute-done | bytes 524320 | tf_op jit(solution)/shard_map/ppermute | solution.py:21
  21.0 4.2 %shard_map.117 = (bf16[16,128,128]{2,1,0:T(8,128)(2,1)S(1)}, bf16[16,128,128]{2,1,0:T(8,128)(2,1)S(1)}) custom-call(s32[16777216]{0:T(1024)} %shard_map.113.token.lists, s32[2]{0:T(128)S(1)} %pad_add_fusion.meta, bf16[256,128,128]{2,1,0:T(8,128)(2,1)} %bitcast.12, bf16[64,4096]{1,0:T(8,128)(2,1)S(1)} %shard_map.114.mine, ...), custom_call_target="tpu_custom_call" | custom-call | bytes 16777216 | tf_op jit(solution)/shard_map/pallas_call | solution.py:177
  25.2 2.0 %collective-permute-start.8 = (bf16[16,128,128]{2,1,0:T(8,128)(2,1)S(1)}, bf16[16,128,128]{2,1,0:T(8,128)(2,1)S(1)}, u32[]{:S(2)}, u32[]{:S(2)}) collective-permute-start(bf16[16,128,128]{2,1,0:T(8,128)(2,1)S(1)} %get-tuple-element.17), channel_id=1, source_target_pairs={{0,192},{64,0},{128,64},{192,128},{1,193},{65,1},{129,65},{193,129... | collective-permute-start | bytes 1572872 | tf_op jit(solution)/shard_map/ppermute | solution.py:17
  27.2 0.1 collective-permute-start.4
  27.3 7.0 %shard_map.115 = (bf16[16,128,128]{2,1,0:T(8,128)(2,1)}, bf16[16,128,128]{2,1,0:T(8,128)(2,1)}, bf16[16,128,128]{2,1,0:T(8,128)(2,1)S(1)}, bf16[16,128,128]{2,1,0:T(8,128)(2,1)S(1)}, bf16[32,128,128]{2,1,0:T(8,128)(2,1)S(1)}) custom-call(s32[16777216]{0:T(1024)} %shard_map.113.token.lists, s32[2]{0:T(128)S(1)} %pad_add_fusion.meta, ...), custom_call_target="tpu_custom_call" | custom-call | bytes 16777216 | tf_op jit(solution)/shard_map/pallas_call | solution.py:177
  34.4 0.1 collective-permute-start.6
  34.4 3.2 %collective-permute-start.7 = (bf16[16,128,128]{2,1,0:T(8,128)(2,1)}, bf16[16,128,128]{2,1,0:T(8,128)(2,1)S(1)}, u32[]{:S(2)}, u32[]{:S(2)}) collective-permute-start(bf16[16,128,128]{2,1,0:T(8,128)(2,1)} %get-tuple-element.15), channel_id=1, source_target_pairs={{0,192},{64,0},{128,64},{192,128},{1,193},{65,1},{129,65},{193,129... | collective-permute-start | bytes 1572872 | tf_op jit(solution)/shard_map/ppermute | solution.py:17
  37.7 2.5 %collective-permute-done.8 = bf16[16,128,128]{2,1,0:T(8,128)(2,1)S(1)} collective-permute-done((bf16[16,128,128]{2,1,0:T(8,128)(2,1)S(1)}, bf16[16,128,128]{2,1,0:T(8,128)(2,1)S(1)}, u32[]{:S(2)}, u32[]{:S(2)}) %collective-permute-start.8) | collective-permute-done | bytes 524320 | tf_op jit(solution)/shard_map/ppermute | solution.py:17
  40.1 0.9 add_convert_fusion
  41.1 3.0 %collective-permute-start.9 = (bf16[16,128,128]{2,1,0:T(8,128)(2,1)}, bf16[16,128,128]{2,1,0:T(8,128)(2,1)S(1)}, u32[]{:S(2)}, u32[]{:S(2)}) collective-permute-start(bf16[16,128,128]{2,1,0:T(8,128)(2,1)} %add_convert_fusion), channel_id=1, source_target_pairs={{0,192},{64,0},{128,64},{192,128},{1,193},{65,1},{129,65},{193,129... | collective-permute-start | bytes 1572872 | tf_op jit(solution)/shard_map/ppermute | solution.py:17
  44.1 0.0 collective-permute-done.4
  44.1 0.9 add_convert_fusion.1
  45.1 0.0 collective-permute-start.5
  45.1 0.1 shard_map.116.c0
  45.1 14.2 %all-gather.2.cloned.1.call-done = bf16[4096,128]{1,0:T(8,128)(2,1)} async-done(((bf16[512,128]{1,0:T(8,128)(2,1)}), bf16[4096,128]{1,0:T(8,128)(2,1)}) %all-gather.2.cloned.1.call-update) | async-done | bytes 1048592 | tf_op jit(solution)/shard_map/all_gather | solution.py:252
  59.4 1.2 %copy-done = bf16[4096,128]{1,0:T(8,128)(2,1)S(1)} copy-done((bf16[4096,128]{1,0:T(8,128)(2,1)S(1)}, bf16[4096,128]{1,0:T(8,128)(2,1)}, u32[]{:S(2)}) %copy-start) | copy-done | bytes 1048600
  60.6 0.1 shard_map.118.feats
  60.7 0.0 collective-permute-done.6.upb
  60.7 0.0 collective-permute-done.7.downa
  60.7 0.9 collective-permute-done.9.downb
  61.6 3.3 %collective-permute-done.5.upa = bf16[16,128,128]{2,1,0:T(8,128)(2,1)S(1)} collective-permute-done((bf16[16,128,128]{2,1,0:T(8,128)(2,1)}, bf16[16,128,128]{2,1,0:T(8,128)(2,1)S(1)}, u32[]{:S(2)}, u32[]{:S(2)}) %collective-permute-start.5) | collective-permute-done | bytes 524320 | tf_op jit(solution)/shard_map/ppermute | solution.py:17
  64.9 1.2 %shard_map.119 = (bf16[32,128,128]{2,1,0:T(8,128)(2,1)}, f32[128,128]{1,0:T(8,128)S(1)}) custom-call(bf16[32,128,128]{2,1,0:T(8,128)(2,1)S(1)} %shard_map.116.c0, bf16[16,128,128]{2,1,0:T(8,128)(2,1)S(1)} %collective-permute-done.5.upa, bf16[16,128,128]{2,1,0:T(8,128)(2,1)S(1)} %collective-permute-done.6.upb, ...), custom_call_target="tpu_custom_call" | custom-call | flops 134217728 | bytes 5242880 | tf_op jit(solution)/shard_map/pallas_call | solution.py:215
  66.1 0.0 reduce-scatter.2.cloned.1.call-update
  66.1 0.1 collective-permute-start.10
  66.2 1.2 %collective-permute-done.10 = f32[128,128]{1,0:T(8,128)S(1)} collective-permute-done((f32[128,128]{1,0:T(8,128)S(1)}, f32[128,128]{1,0:T(8,128)S(1)}, u32[]{:S(2)}, u32[]{:S(2)}) %collective-permute-start.10) | collective-permute-done | bytes 65568 | tf_op jit(solution)/shard_map/ppermute | solution.py:21
  67.4 1.4 %collective-permute-start.11 = (f32[128,128]{1,0:T(8,128)S(1)}, f32[128,128]{1,0:T(8,128)S(1)}, u32[]{:S(2)}, u32[]{:S(2)}) collective-permute-start(f32[128,128]{1,0:T(8,128)S(1)} %add.43), channel_id=1, source_target_pairs={{0,4},{2,6},{4,0},{6,2},{1,5},{3,7},{5,1},{7,3},{8,12},{10,14},{12... | collective-permute-start | bytes 196616 | tf_op jit(solution)/shard_map/ppermute | solution.py:17
  68.9 1.6 %collective-permute-start.12 = (f32[128,128]{1,0:T(8,128)S(1)}, f32[128,128]{1,0:T(8,128)S(1)}, u32[]{:S(2)}, u32[]{:S(2)}) collective-permute-start(f32[128,128]{1,0:T(8,128)S(1)} %add.43), channel_id=1, source_target_pairs={{0,2},{2,4},{4,6},{6,0},{1,3},{3,5},{5,7},{7,1},{8,10},{10,12},{12... | collective-permute-start | bytes 196616 | tf_op jit(solution)/shard_map/ppermute | solution.py:17
  70.5 1.6 %collective-permute-start.13 = (f32[128,128]{1,0:T(8,128)S(1)}, f32[128,128]{1,0:T(8,128)S(1)}, u32[]{:S(2)}, u32[]{:S(2)}) collective-permute-start(f32[128,128]{1,0:T(8,128)S(1)} %add.43), channel_id=1, source_target_pairs={{0,6},{2,0},{4,2},{6,4},{1,7},{3,1},{5,3},{7,5},{8,14},{10,8},{12,... | collective-permute-start | bytes 196616 | tf_op jit(solution)/shard_map/ppermute | solution.py:17
  72.1 1.7 %collective-permute-done.11 = f32[128,128]{1,0:T(8,128)S(1)} collective-permute-done((f32[128,128]{1,0:T(8,128)S(1)}, f32[128,128]{1,0:T(8,128)S(1)}, u32[]{:S(2)}, u32[]{:S(2)}) %collective-permute-start.11) | collective-permute-done | bytes 65568 | tf_op jit(solution)/shard_map/ppermute | solution.py:17
  73.8 0.8 collective-permute-done.12
  74.6 0.1 collective-permute-done.13
  74.7 0.1 collective-permute-start.14
  74.9 1.1 collective-permute-start.15
  76.0 2.2 %collective-permute-start.16 = (f32[128,128]{1,0:T(8,128)S(1)}, f32[128,128]{1,0:T(8,128)S(1)}, u32[]{:S(2)}, u32[]{:S(2)}) collective-permute-start(f32[128,128]{1,0:T(8,128)S(1)} %add_add_fusion.2), channel_id=1, source_target_pairs={{0,192},{64,0},{128,64},{192,128},{1,193},{65,1},{129,65},{193,129... | collective-permute-start | bytes 196616 | tf_op jit(solution)/shard_map/ppermute | solution.py:17
  78.2 2.5 %collective-permute-done.14 = f32[128,128]{1,0:T(8,128)S(1)} collective-permute-done((f32[128,128]{1,0:T(8,128)S(1)}, f32[128,128]{1,0:T(8,128)S(1)}, u32[]{:S(2)}, u32[]{:S(2)}) %collective-permute-start.14) | collective-permute-done | bytes 65568 | tf_op jit(solution)/shard_map/ppermute | solution.py:17
  80.7 0.4 collective-permute-done.15
  81.1 0.0 collective-permute-done.16
  81.1 2.6 %collective-permute-start.17 = (f32[128,128]{1,0:T(8,128)S(1)}, f32[128,128]{1,0:T(8,128)S(1)}, u32[]{:S(2)}, u32[]{:S(2)}) collective-permute-start(f32[128,128]{1,0:T(8,128)S(1)} %add_add_fusion.1), channel_id=1, source_target_pairs={{0,8},{8,16},{16,24},{24,32},{32,40},{40,48},{48,56},{56,0},{1,57}... | collective-permute-start | bytes 196616 | tf_op jit(solution)/shard_map/ppermute | solution.py:30
  83.7 4.7 %collective-permute-start.18 = (f32[128,128]{1,0:T(8,128)S(1)}, f32[128,128]{1,0:T(8,128)S(1)}, u32[]{:S(2)}, u32[]{:S(2)}) collective-permute-start(f32[128,128]{1,0:T(8,128)S(1)} %add_add_fusion.1), channel_id=1, source_target_pairs={{0,16},{8,24},{16,32},{24,40},{32,48},{40,56},{48,0},{56,8},{1,49}... | collective-permute-start | bytes 196616 | tf_op jit(solution)/shard_map/ppermute | solution.py:30
  88.4 1.6 %collective-permute-start.19 = (f32[128,128]{1,0:T(8,128)S(1)}, f32[128,128]{1,0:T(8,128)S(1)}, u32[]{:S(2)}, u32[]{:S(2)}) collective-permute-start(f32[128,128]{1,0:T(8,128)S(1)} %add_add_fusion.1), channel_id=1, source_target_pairs={{0,24},{8,32},{16,40},{24,48},{32,56},{40,0},{48,8},{56,16},{1,41}... | collective-permute-start | bytes 196616 | tf_op jit(solution)/shard_map/ppermute | solution.py:30
  90.0 3.5 %collective-permute-start.20 = (f32[128,128]{1,0:T(8,128)S(1)}, f32[128,128]{1,0:T(8,128)S(1)}, u32[]{:S(2)}, u32[]{:S(2)}) collective-permute-start(f32[128,128]{1,0:T(8,128)S(1)} %add_add_fusion.1), channel_id=1, source_target_pairs={{0,32},{8,40},{16,48},{24,56},{32,0},{40,8},{48,16},{56,24},{2,34}... | collective-permute-start | bytes 196616 | tf_op jit(solution)/shard_map/ppermute | solution.py:30
  93.6 0.0 collective-permute-done.17
  93.6 0.0 collective-permute-done.18
  93.6 2.8 %collective-permute-done.19 = f32[128,128]{1,0:T(8,128)S(1)} collective-permute-done((f32[128,128]{1,0:T(8,128)S(1)}, f32[128,128]{1,0:T(8,128)S(1)}, u32[]{:S(2)}, u32[]{:S(2)}) %collective-permute-start.19) | collective-permute-done | bytes 65568 | tf_op jit(solution)/shard_map/ppermute | solution.py:30
  96.4 4.4 %collective-permute-done.20 = f32[128,128]{1,0:T(8,128)S(1)} collective-permute-done((f32[128,128]{1,0:T(8,128)S(1)}, f32[128,128]{1,0:T(8,128)S(1)}, u32[]{:S(2)}, u32[]{:S(2)}) %collective-permute-start.20) | collective-permute-done | bytes 65568 | tf_op jit(solution)/shard_map/ppermute | solution.py:30
  100.8 0.1 collective-permute-start.21
  100.9 1.2 %collective-permute-done.21.more = f32[128,128]{1,0:T(8,128)S(1)} collective-permute-done((f32[128,128]{1,0:T(8,128)S(1)}, f32[128,128]{1,0:T(8,128)S(1)}, u32[]{:S(2)}, u32[]{:S(2)}) %collective-permute-start.21) | collective-permute-done | bytes 65568 | tf_op jit(solution)/shard_map/ppermute | solution.py:21
  102.1 4.7 %reduce-scatter.2.cloned.1.call-done.aggregate = bf16[4,128,128]{2,1,0:T(8,128)(2,1)} async-done(((bf16[32,128,128]{2,1,0:T(8,128)(2,1)}), bf16[4,128,128]{2,1,0:T(8,128)(2,1)}) %reduce-scatter.2.cloned.1.call-update) | async-done | bytes 131088 | tf_op jit(solution)/shard_map/reduce_scatter | solution.py:268
  106.8 0.0 copy-done.4
  106.8 0.9 copy-done.1
  107.7 0.9 shard_map.120
  (12 shorter events, 0.1 us)
Async XLA Ops:
  7.2 52.2 %all-gather.2.cloned.1.call-start = ((), (), s32[]{:S(2)}) async-start(), calls=%async_computation.1 | async-start | bytes 1179648 | tf_op jit(solution)/shard_map/all_gather | solution.py:252
  8.2 10.7 %collective-permute-start = (bf16[16,4096]{1,0:T(8,128)(2,1)S(1)}, bf16[16,4096]{1,0:T(8,128)(2,1)S(1)}, u32[]{:S(2)}, u32[]{:S(2)}) collective-permute-start(bf16[16,4096]{1,0:T(8,128)(2,1)S(1)} %fusion.refs_0_), channel_id=1, source_target_pairs={{0,4},{2,6},{4,0},{6,2},{1,5},{3,7},{5,1},{7,3},{8,12},{10,14},{12... | collective-permute-start | bytes 393224 | tf_op jit(solution)/shard_map/ppermute | solution.py:17
  11.5 7.4 %collective-permute-start.1 = (bf16[16,4096]{1,0:T(8,128)(2,1)S(1)}, bf16[16,4096]{1,0:T(8,128)(2,1)S(1)}, u32[]{:S(2)}, u32[]{:S(2)}) collective-permute-start(bf16[16,4096]{1,0:T(8,128)(2,1)S(1)} %fusion.refs_0_), channel_id=1, source_target_pairs={{0,2},{2,4},{4,6},{6,0},{1,3},{3,5},{5,7},{7,1},{8,10},{10,12},{12... | collective-permute-start | bytes 393224 | tf_op jit(solution)/shard_map/ppermute | solution.py:17
  12.2 6.7 %collective-permute-start.2 = (bf16[16,4096]{1,0:T(8,128)(2,1)S(1)}, bf16[16,4096]{1,0:T(8,128)(2,1)S(1)}, u32[]{:S(2)}, u32[]{:S(2)}) collective-permute-start(bf16[16,4096]{1,0:T(8,128)(2,1)S(1)} %fusion.refs_0_), channel_id=1, source_target_pairs={{0,6},{2,0},{4,2},{6,4},{1,7},{3,1},{5,3},{7,5},{8,14},{10,8},{12,... | collective-permute-start | bytes 393224 | tf_op jit(solution)/shard_map/ppermute | solution.py:17
  19.0 2.0 %collective-permute-start.3 = (bf16[64,4096]{1,0:T(8,128)(2,1)S(1)}, bf16[64,4096]{1,0:T(8,128)(2,1)S(1)}, u32[]{:S(2)}, u32[]{:S(2)}) collective-permute-start(bf16[64,4096]{1,0:T(8,128)(2,1)S(1)} %shard_map.114.mine), channel_id=1, source_target_pairs={{0,1},{1,0},{2,3},{3,2},{4,5},{5,4},{6,7},{7,6},{8,9},{9,8},{10,11... | collective-permute-start | bytes 1572872 | tf_op jit(solution)/shard_map/ppermute | solution.py:21
  19.1 87.7 %reduce-scatter.2.cloned.1.call-start = ((), (), s32[]{:S(2)}) async-start(), calls=%async_computation.2 | async-start | bytes 1179648 | tf_op jit(solution)/shard_map/reduce_scatter | solution.py:268
  21.0 85.8 %copy-start.2 = (f32[128,128]{1,0:T(8,128)S(1)}, f32[128,128]{1,0:T(8,128)}, u32[]{:S(2)}) copy-start(f32[128,128]{1,0:T(8,128)} %importance.1) | copy-start | bytes 196612
  21.0 85.8 %copy-start.3 = (f32[128,128]{1,0:T(8,128)S(1)}, f32[128,128]{1,0:T(8,128)}, u32[]{:S(2)}) copy-start(f32[128,128]{1,0:T(8,128)} %delta.1) | copy-start | bytes 196612
  21.0 85.8 %copy-start.4 = (bf16[128,128]{1,0:T(8,128)(2,1)S(1)}, bf16[128,128]{1,0:T(8,128)(2,1)}, u32[]{:S(2)}) copy-start(bf16[128,128]{1,0:T(8,128)(2,1)} %weight.1) | copy-start | bytes 98308
  25.2 14.9 %collective-permute-start.8 = (bf16[16,128,128]{2,1,0:T(8,128)(2,1)S(1)}, bf16[16,128,128]{2,1,0:T(8,128)(2,1)S(1)}, u32[]{:S(2)}, u32[]{:S(2)}) collective-permute-start(bf16[16,128,128]{2,1,0:T(8,128)(2,1)S(1)} %get-tuple-element.17), channel_id=1, source_target_pairs={{0,192},{64,0},{128,64},{192,128},{1,193},{65,1},{129,65},{193,129... | collective-permute-start | bytes 1572872 | tf_op jit(solution)/shard_map/ppermute | solution.py:17
  27.2 16.9 %collective-permute-start.4 = (bf16[16,128,128]{2,1,0:T(8,128)(2,1)S(1)}, bf16[16,128,128]{2,1,0:T(8,128)(2,1)S(1)}, u32[]{:S(2)}, u32[]{:S(2)}) collective-permute-start(bf16[16,128,128]{2,1,0:T(8,128)(2,1)S(1)} %get-tuple-element.13), channel_id=1, source_target_pairs={{0,64},{64,128},{128,192},{192,0},{1,65},{65,129},{129,193},{193,1... | collective-permute-start | bytes 1572872 | tf_op jit(solution)/shard_map/ppermute | solution.py:17
  34.4 26.3 %collective-permute-start.6 = (bf16[16,128,128]{2,1,0:T(8,128)(2,1)}, bf16[16,128,128]{2,1,0:T(8,128)(2,1)S(1)}, u32[]{:S(2)}, u32[]{:S(2)}) collective-permute-start(bf16[16,128,128]{2,1,0:T(8,128)(2,1)} %get-tuple-element.14), channel_id=1, source_target_pairs={{0,64},{64,128},{128,192},{192,0},{1,65},{65,129},{129,193},{193,1... | collective-permute-start | bytes 1572872 | tf_op jit(solution)/shard_map/ppermute | solution.py:17
  34.4 26.3 %collective-permute-start.7 = (bf16[16,128,128]{2,1,0:T(8,128)(2,1)}, bf16[16,128,128]{2,1,0:T(8,128)(2,1)S(1)}, u32[]{:S(2)}, u32[]{:S(2)}) collective-permute-start(bf16[16,128,128]{2,1,0:T(8,128)(2,1)} %get-tuple-element.15), channel_id=1, source_target_pairs={{0,192},{64,0},{128,64},{192,128},{1,193},{65,1},{129,65},{193,129... | collective-permute-start | bytes 1572872 | tf_op jit(solution)/shard_map/ppermute | solution.py:17
  41.1 20.5 %collective-permute-start.9 = (bf16[16,128,128]{2,1,0:T(8,128)(2,1)}, bf16[16,128,128]{2,1,0:T(8,128)(2,1)S(1)}, u32[]{:S(2)}, u32[]{:S(2)}) collective-permute-start(bf16[16,128,128]{2,1,0:T(8,128)(2,1)} %add_convert_fusion), channel_id=1, source_target_pairs={{0,192},{64,0},{128,64},{192,128},{1,193},{65,1},{129,65},{193,129... | collective-permute-start | bytes 1572872 | tf_op jit(solution)/shard_map/ppermute | solution.py:17
  45.1 19.8 %collective-permute-start.5 = (bf16[16,128,128]{2,1,0:T(8,128)(2,1)}, bf16[16,128,128]{2,1,0:T(8,128)(2,1)S(1)}, u32[]{:S(2)}, u32[]{:S(2)}) collective-permute-start(bf16[16,128,128]{2,1,0:T(8,128)(2,1)} %add_convert_fusion.1), channel_id=1, source_target_pairs={{0,64},{64,128},{128,192},{192,0},{1,65},{65,129},{129,193},{193,1... | collective-permute-start | bytes 1572872 | tf_op jit(solution)/shard_map/ppermute | solution.py:17
  59.4 1.2 %copy-start = (bf16[4096,128]{1,0:T(8,128)(2,1)S(1)}, bf16[4096,128]{1,0:T(8,128)(2,1)}, u32[]{:S(2)}) copy-start(bf16[4096,128]{1,0:T(8,128)(2,1)} %all-gather.2.cloned.1.call-done) | copy-start | bytes 3145732
  66.1 1.3 %collective-permute-start.10 = (f32[128,128]{1,0:T(8,128)S(1)}, f32[128,128]{1,0:T(8,128)S(1)}, u32[]{:S(2)}, u32[]{:S(2)}) collective-permute-start(f32[128,128]{1,0:T(8,128)S(1)} %get-tuple-element.19), channel_id=1, source_target_pairs={{0,1},{1,0},{2,3},{3,2},{4,5},{5,4},{6,7},{7,6},{8,9},{9,8},{10,11... | collective-permute-start | bytes 196616 | tf_op jit(solution)/shard_map/ppermute | solution.py:21
  67.4 6.4 %collective-permute-start.11 = (f32[128,128]{1,0:T(8,128)S(1)}, f32[128,128]{1,0:T(8,128)S(1)}, u32[]{:S(2)}, u32[]{:S(2)}) collective-permute-start(f32[128,128]{1,0:T(8,128)S(1)} %add.43), channel_id=1, source_target_pairs={{0,4},{2,6},{4,0},{6,2},{1,5},{3,7},{5,1},{7,3},{8,12},{10,14},{12... | collective-permute-start | bytes 196616 | tf_op jit(solution)/shard_map/ppermute | solution.py:17
  68.9 5.8 %collective-permute-start.12 = (f32[128,128]{1,0:T(8,128)S(1)}, f32[128,128]{1,0:T(8,128)S(1)}, u32[]{:S(2)}, u32[]{:S(2)}) collective-permute-start(f32[128,128]{1,0:T(8,128)S(1)} %add.43), channel_id=1, source_target_pairs={{0,2},{2,4},{4,6},{6,0},{1,3},{3,5},{5,7},{7,1},{8,10},{10,12},{12... | collective-permute-start | bytes 196616 | tf_op jit(solution)/shard_map/ppermute | solution.py:17
  70.5 4.3 %collective-permute-start.13 = (f32[128,128]{1,0:T(8,128)S(1)}, f32[128,128]{1,0:T(8,128)S(1)}, u32[]{:S(2)}, u32[]{:S(2)}) collective-permute-start(f32[128,128]{1,0:T(8,128)S(1)} %add.43), channel_id=1, source_target_pairs={{0,6},{2,0},{4,2},{6,4},{1,7},{3,1},{5,3},{7,5},{8,14},{10,8},{12,... | collective-permute-start | bytes 196616 | tf_op jit(solution)/shard_map/ppermute | solution.py:17
  74.7 5.9 %collective-permute-start.14 = (f32[128,128]{1,0:T(8,128)S(1)}, f32[128,128]{1,0:T(8,128)S(1)}, u32[]{:S(2)}, u32[]{:S(2)}) collective-permute-start(f32[128,128]{1,0:T(8,128)S(1)} %add_add_fusion.2), channel_id=1, source_target_pairs={{0,128},{64,192},{128,0},{192,64},{1,129},{65,193},{129,1},{193,65... | collective-permute-start | bytes 196616 | tf_op jit(solution)/shard_map/ppermute | solution.py:17
  74.9 6.2 %collective-permute-start.15 = (f32[128,128]{1,0:T(8,128)S(1)}, f32[128,128]{1,0:T(8,128)S(1)}, u32[]{:S(2)}, u32[]{:S(2)}) collective-permute-start(f32[128,128]{1,0:T(8,128)S(1)} %add_add_fusion.2), channel_id=1, source_target_pairs={{0,64},{64,128},{128,192},{192,0},{1,65},{65,129},{129,193},{193,1... | collective-permute-start | bytes 196616 | tf_op jit(solution)/shard_map/ppermute | solution.py:17
  76.0 5.1 %collective-permute-start.16 = (f32[128,128]{1,0:T(8,128)S(1)}, f32[128,128]{1,0:T(8,128)S(1)}, u32[]{:S(2)}, u32[]{:S(2)}) collective-permute-start(f32[128,128]{1,0:T(8,128)S(1)} %add_add_fusion.2), channel_id=1, source_target_pairs={{0,192},{64,0},{128,64},{192,128},{1,193},{65,1},{129,65},{193,129... | collective-permute-start | bytes 196616 | tf_op jit(solution)/shard_map/ppermute | solution.py:17
  81.1 12.5 %collective-permute-start.17 = (f32[128,128]{1,0:T(8,128)S(1)}, f32[128,128]{1,0:T(8,128)S(1)}, u32[]{:S(2)}, u32[]{:S(2)}) collective-permute-start(f32[128,128]{1,0:T(8,128)S(1)} %add_add_fusion.1), channel_id=1, source_target_pairs={{0,8},{8,16},{16,24},{24,32},{32,40},{40,48},{48,56},{56,0},{1,57}... | collective-permute-start | bytes 196616 | tf_op jit(solution)/shard_map/ppermute | solution.py:30
  83.7 9.9 %collective-permute-start.18 = (f32[128,128]{1,0:T(8,128)S(1)}, f32[128,128]{1,0:T(8,128)S(1)}, u32[]{:S(2)}, u32[]{:S(2)}) collective-permute-start(f32[128,128]{1,0:T(8,128)S(1)} %add_add_fusion.1), channel_id=1, source_target_pairs={{0,16},{8,24},{16,32},{24,40},{32,48},{40,56},{48,0},{56,8},{1,49}... | collective-permute-start | bytes 196616 | tf_op jit(solution)/shard_map/ppermute | solution.py:30
  88.4 8.0 %collective-permute-start.19 = (f32[128,128]{1,0:T(8,128)S(1)}, f32[128,128]{1,0:T(8,128)S(1)}, u32[]{:S(2)}, u32[]{:S(2)}) collective-permute-start(f32[128,128]{1,0:T(8,128)S(1)} %add_add_fusion.1), channel_id=1, source_target_pairs={{0,24},{8,32},{16,40},{24,48},{32,56},{40,0},{48,8},{56,16},{1,41}... | collective-permute-start | bytes 196616 | tf_op jit(solution)/shard_map/ppermute | solution.py:30
  90.0 10.7 %collective-permute-start.20 = (f32[128,128]{1,0:T(8,128)S(1)}, f32[128,128]{1,0:T(8,128)S(1)}, u32[]{:S(2)}, u32[]{:S(2)}) collective-permute-start(f32[128,128]{1,0:T(8,128)S(1)} %add_add_fusion.1), channel_id=1, source_target_pairs={{0,32},{8,40},{16,48},{24,56},{32,0},{40,8},{48,16},{56,24},{2,34}... | collective-permute-start | bytes 196616 | tf_op jit(solution)/shard_map/ppermute | solution.py:30
  100.8 1.3 %collective-permute-start.21 = (f32[128,128]{1,0:T(8,128)S(1)}, f32[128,128]{1,0:T(8,128)S(1)}, u32[]{:S(2)}, u32[]{:S(2)}) collective-permute-start(f32[128,128]{1,0:T(8,128)S(1)} %add_add_fusion.grad), channel_id=1, source_target_pairs={{0,1},{1,0},{2,3},{3,2},{4,5},{5,4},{6,7},{7,6},{8,9},{9,8},{10,11... | collective-permute-start | bytes 196616 | tf_op jit(solution)/shard_map/ppermute | solution.py:21
  106.8 0.9 copy-start.1
Sparse Core Ops, SparseCore 0:
  19.2 40.0 all-gather.1
  66.2 40.5 reduce-scatter.1
